TPU v7x, 512 devices: a whole 4x4x16 slice. The times are simulated.
512 devices in a mesh: shot: 8 (over y_lo, x), slab: 64 (over y_hi, z, core).
Axes of the slice: x: 4, y: 4 (y_hi: 2, y_lo: 2; y = y_hi * 2 + y_lo), z: 16, core: 2. Of those that a mesh axis runs over, the one named last changes fastest.
Arguments:
- src_prev: float32 [8, 64, 512, 128], P('shot', None, 'slab'), may hold values from -6 to 6
- src_cur: float32 [8, 64, 512, 128], P('shot', None, 'slab'), may hold values from -6 to 6
- rec_cur: float32 [8, 64, 512, 128], P('shot', None, 'slab'), may hold values from -6 to 6
- rec_next: float32 [8, 64, 512, 128], P('shot', None, 'slab'), may hold values from -6 to 6
- velocity: float32 [512, 512, 128], P('shot', 'slab'), may hold values from 0.15 to 0.42
- aperture_tiles: int32 [8, 8], replicated, may hold values from 0 to 63, as said below
- wavelet: float32 [8, 4], replicated, may hold values from -8 to 8
- src_x: int32 [8], replicated, may hold values from 0 to 63
- src_z: int32 [8], replicated, may hold values from 0 to 511
- src_y: int32 [8], replicated, may hold values from 0 to 127
- rec_depth: int32 [8], replicated, may hold values from 0 to 511
- rec_data: bfloat16 [8, 4, 64, 128], P('shot'), may hold values from -6 to 6
Outputs:
- image_model: float32 [512, 512, 128], P('shot', 'slab')
- src_last: float32 [8, 64, 512, 128], P('shot', None, 'slab')
- rec_first: float32 [8, 64, 512, 128], P('shot', None, 'slab')
Inputs may be any that keep to these rules, and one draw needn't show every extreme that they name: `aperture_tiles`: each row lists 8 distinct model tiles in increasing order; tile t is held by index t // 8 of shot; a row takes at most 2 tiles held by one index, and exactly 2 from some index in every row.
All inputs are finite; a program needn't handle non-finite values.
Results may differ from a plain program's by a relative error of at most 0.0003.
Values sent between devices are 32-bit elements; how exact they have to be, the bound alone decides.
No kernel may reach another device: no remote copies, remote signals or barrier semaphores. Data moves between devices by JAX's collectives and lax.ppermute only.
A program may use at most 64 MiB of HBM per device.

v0:
```python
import jax
import jax.numpy as jnp
from jax import lax
from jax.sharding import PartitionSpec as P

BX = 8
KT = 8
STEPS = 4


COEFFS = (-205.0 / 72.0, 8.0 / 5.0, -1.0 / 5.0, 8.0 / 315.0, -1.0 / 560.0)


def with_halo(array, sides, width):
    for axis, dim in sides:
        count, length = (lax.axis_size(axis), array.shape[dim])
        up = [(i, (i + 1) % count) for i in range(count - 1)]
        down = [(j, i) for i, j in up]
        last = lax.slice_in_dim(array, length - width, length, axis=dim)
        initial = lax.slice_in_dim(array, 0, width, axis=dim)
        before = lax.ppermute(last, axis, up)
        after = lax.ppermute(initial, axis, down)
        array = jnp.concatenate([before, array, after], axis=dim)
    return array


def laplace(extended):
    size_x, size_e, size_y = extended.shape
    size_z = size_e - 8
    padded = jnp.pad(extended, ((4, 4), (0, 0), (4, 4)))
    centre = padded[4 : 4 + size_x, 4 : 4 + size_z, 4 : 4 + size_y]
    result = 3.0 * COEFFS[0] * centre
    for reach in range(1, 5):
        along_z = (
            padded[4 : 4 + size_x, 4 + reach : 4 + reach + size_z, 4 : 4 + size_y]
            + padded[4 : 4 + size_x, 4 - reach : 4 - reach + size_z, 4 : 4 + size_y]
        )
        along_x = (
            padded[4 + reach : 4 + reach + size_x, 4 : 4 + size_z, 4 : 4 + size_y]
            + padded[4 - reach : 4 - reach + size_x, 4 : 4 + size_z, 4 : 4 + size_y]
        )
        along_y = (
            padded[4 : 4 + size_x, 4 : 4 + size_z, 4 + reach : 4 + reach + size_y]
            + padded[4 : 4 + size_x, 4 : 4 + size_z, 4 - reach : 4 - reach + size_y]
        )
        result = result + COEFFS[reach] * (along_z + along_x + along_y)
    return result


def local(
    src_prev,
    src_cur,
    rec_cur,
    rec_next,
    velocity,
    aperture_tiles,
    wavelet,
    src_x,
    src_z,
    src_y,
    rec_depth,
    rec_data,
):
    shot_index = lax.axis_index("shot")
    slab_index = lax.axis_index("slab")
    depth_cells = src_cur.shape[2]
    width_x = src_cur.shape[1]
    width_y = src_cur.shape[3]
    my_tiles = lax.dynamic_index_in_dim(aperture_tiles, shot_index, 0, keepdims=False)
    model_row = (my_tiles[:, None] * BX + jnp.arange(BX)[None, :]).reshape(-1)
    block_rows = lax.all_gather(velocity, "shot", axis=0, tiled=True)
    row_count = block_rows.shape[0]
    inside = (model_row >= 0) & (model_row < row_count)
    picked = jnp.take(block_rows, jnp.clip(model_row, 0, row_count - 1), axis=0)
    aperture_vel = jnp.where(inside[:, None, None], picked, 0.0)
    rate_field = aperture_vel * aperture_vel
    wave_row = lax.dynamic_index_in_dim(wavelet, shot_index, 0, keepdims=False)
    spot_x = lax.dynamic_index_in_dim(src_x, shot_index, 0, keepdims=False)
    spot_z = lax.dynamic_index_in_dim(src_z, shot_index, 0, keepdims=False)
    spot_y = lax.dynamic_index_in_dim(src_y, shot_index, 0, keepdims=False)
    plane_z = lax.dynamic_index_in_dim(rec_depth, shot_index, 0, keepdims=False)
    traces_all = rec_data[0]
    cells_x = jnp.arange(width_x)
    cells_y = jnp.arange(width_y)
    src_old = src_prev[0]
    src_now = src_cur[0]
    rec_later = rec_next[0]
    rec_now = rec_cur[0]
    src_snaps = [src_now]
    rec_snaps = [rec_now]
    for step_index in range(STEPS):
        later_step = STEPS - 1 - step_index
        ext_src, ext_rec = (
            with_halo(src_now, (("slab", 1),), 4),
            with_halo(rec_now, (("slab", 1),), 4),
        )
        source_global_z = slab_index * depth_cells + jnp.arange(depth_cells)
        spot = (
            (cells_x == spot_x)[:, None, None]
            & (source_global_z == spot_z)[None, :, None]
            & (cells_y == spot_y)[None, None, :]
        ).astype(jnp.float32)
        src_new = (
            2.0 * src_now - src_old + rate_field * laplace(ext_src) + wave_row[step_index] * spot
        )
        global_z = slab_index * depth_cells + jnp.arange(depth_cells)
        plane = (global_z == plane_z).astype(jnp.float32)[None, :, None]
        rec_new = (
            2.0 * rec_now
            - rec_later
            + rate_field * laplace(ext_rec)
            + plane * traces_all[later_step].astype(jnp.float32)[:, None, :]
        )
        src_old, src_now = (src_now, src_new)
        rec_later, rec_now = (rec_now, rec_new)
        src_snaps.append(src_now)
        rec_snaps.append(rec_now)
    image_sum = src_snaps[STEPS] * rec_snaps[0]
    for back in range(1, STEPS + 1):
        image_sum = image_sum + src_snaps[STEPS - back] * rec_snaps[back]
    rows_here = jnp.arange(velocity.shape[0] * lax.axis_size("shot"))
    matched = (rows_here // BX)[:, None] == my_tiles[None, :]
    found = jnp.any(matched, axis=1)
    which_tile = jnp.sum(matched.astype(jnp.int32) * jnp.arange(KT)[None, :], axis=1)
    source_row = which_tile * BX + rows_here % BX
    picked = jnp.take(image_sum, source_row, axis=0)
    image_model = lax.psum_scatter(
        jnp.where(found[:, None, None], picked, 0.0), "shot", scatter_dimension=0, tiled=True
    )
    return (image_model, src_now[None], rec_now[None])


def solution(mesh):
    return jax.shard_map(
        local,
        mesh=mesh,
        in_specs=(
            P("shot", None, "slab", None),
            P("shot", None, "slab", None),
            P("shot", None, "slab", None),
            P("shot", None, "slab", None),
            P("shot", "slab", None),
            P(),
            P(),
            P(),
            P(),
            P(),
            P(),
            P("shot", None, None, None),
        ),
        out_specs=(
            P("shot", "slab", None),
            P("shot", None, "slab", None),
            P("shot", None, "slab", None),
        ),
        check_vma=False,
    )
```

profile of v0, /device:TPU:32, one launch (start us, length us, event | category | flops | bytes accessed | tf_op | source)
XLA Modules:
  0.0 199.6 jit_solution(11211441935331872507)
XLA Ops:
  7.3 1.1 fusion.260
  8.4 1.9 collective-permute-start.1
  10.3 3.6 %collective-permute-start = (f32[64,4,128]{2,1,0:T(4,128)S(1)}, f32[64,4,128]{2,1,0:T(4,128)S(1)}, u32[]{:S(2)}, u32[]{:S(2)}) collective-permute-start(f32[64,4,128]{2,1,0:T(4,128)S(1)} %get-tuple-element.22), channel_id=1, source_target_pairs={{1,0},{2,1},{3,2},{4,3},{5,4},{6,5},{7,6},{8,7},{9,8},{10,9},{11,1... | collective-permute-start | bytes 393224 | tf_op jit(solution)/shard_map/ppermute | solution.py:22
  14.1 1.1 fusion.259
  15.2 2.2 %collective-permute-start.9 = (f32[64,4,128]{2,1,0:T(4,128)S(1)}, f32[64,4,128]{2,1,0:T(4,128)S(1)}, u32[]{:S(2)}, u32[]{:S(2)}) collective-permute-start(f32[64,4,128]{2,1,0:T(4,128)S(1)} %get-tuple-element.21), channel_id=1, source_target_pairs={{0,1},{1,2},{2,3},{3,4},{4,5},{5,6},{6,7},{7,8},{8,9},{9,10},{10,1... | collective-permute-start | bytes 393224 | tf_op jit(solution)/shard_map/ppermute | solution.py:21
  17.4 4.9 %collective-permute-start.8 = (f32[64,4,128]{2,1,0:T(4,128)S(1)}, f32[64,4,128]{2,1,0:T(4,128)S(1)}, u32[]{:S(2)}, u32[]{:S(2)}) collective-permute-start(f32[64,4,128]{2,1,0:T(4,128)S(1)} %get-tuple-element.20), channel_id=1, source_target_pairs={{1,0},{2,1},{3,2},{4,3},{5,4},{6,5},{7,6},{8,7},{9,8},{10,9},{11,1... | collective-permute-start | bytes 393224 | tf_op jit(solution)/shard_map/ppermute | solution.py:22
  25.6 1.2 iota_compare_fusion.4
  35.0 33.4 %all-gather.2.cloned.1.call-done = f32[512,8,128]{2,1,0:T(8,128)} async-done(((f32[64,8,128]{2,1,0:T(8,128)}), f32[512,8,128]{2,1,0:T(8,128)}) %all-gather.2.cloned.1.call-update) | async-done | bytes 2097168 | tf_op jit(solution)/shard_map/all_gather | solution.py:71
  68.5 2.3 %gather_fusion = f32[64,8,128]{2,1,0:T(8,128)S(1)} fusion(f32[512,8,128]{2,1,0:T(8,128)} %all-gather.2.cloned.1.call-done, s32[1024]{0:T(1024)} %pad_clamp_fusion.1), kind=kCustom, calls=%fused_computation | custom fusion | bytes 524544 | tf_op jit(solution)/shard_map/jit(_take)/gather | solution.py:74
  70.8 3.1 %fusion.3 = f32[64,8,128]{2,1,0:T(8,128)S(1)} fusion(f32[64,8,128]{2,1,0:T(8,128)S(1)} %bitcast.45, f32[64,4,128]{2,1,0:T(4,128)S(1)} %collective-permute-done.1, f32[64,4,128]{2,1,0:T(4,128)S(1)} %collective-permute-done, f32[72,16,136]{2,1,0:T(8,128)S(1)} %select_maximum_fusion.14, f32[1,64,8,128]{3,2,1,0:T(8,128)} %param.12, f32[]{:T(128)} %bitcast.7, ...), kind=kLoop, calls=%fused_computation.126 | loop fusion | flops 3080192 | bytes 5505796 | tf_op jit(solution)/shard_map/add | solution.py:104
  74.0 1.9 collective-permute-start.3
  75.9 3.6 %collective-permute-start.2 = (f32[64,4,128]{2,1,0:T(4,128)S(1)}, f32[64,4,128]{2,1,0:T(4,128)S(1)}, u32[]{:S(2)}, u32[]{:S(2)}) collective-permute-start(f32[64,4,128]{2,1,0:T(4,128)S(1)} %get-tuple-element.14), channel_id=1, source_target_pairs={{1,0},{2,1},{3,2},{4,3},{5,4},{6,5},{7,6},{8,7},{9,8},{10,9},{11,1... | collective-permute-start | bytes 393224 | tf_op jit(solution)/shard_map/ppermute | solution.py:22
  79.6 1.4 fusion.91
  81.1 1.9 collective-permute-start.11
  83.0 3.6 %collective-permute-start.10 = (f32[64,4,128]{2,1,0:T(4,128)S(1)}, f32[64,4,128]{2,1,0:T(4,128)S(1)}, u32[]{:S(2)}, u32[]{:S(2)}) collective-permute-start(f32[64,4,128]{2,1,0:T(4,128)S(1)} %get-tuple-element.18), channel_id=1, source_target_pairs={{1,0},{2,1},{3,2},{4,3},{5,4},{6,5},{7,6},{8,7},{9,8},{10,9},{11,1... | collective-permute-start | bytes 393224 | tf_op jit(solution)/shard_map/ppermute | solution.py:22
  87.3 2.1 %fusion.4 = f32[64,8,128]{2,1,0:T(8,128)S(1)} fusion(f32[64,8,128]{2,1,0:T(8,128)S(1)} %fusion.3, f32[64,4,128]{2,1,0:T(4,128)S(1)} %collective-permute-done.3, f32[64,4,128]{2,1,0:T(4,128)S(1)} %collective-permute-done.2, f32[72,16,136]{2,1,0:T(8,128)S(1)} %select_maximum_fusion.12, f32[]{:T(128)} %bitcast.8, pred[128]{0:T(512)(128)(4,1)S(1)} %copy-done.13, ...), kind=kLoop, calls=%fused_computation.127 | loop fusion | flops 3080192 | bytes 5505796 | tf_op jit(solution)/shard_map/add | solution.py:104
  89.5 1.9 collective-permute-start.5
  91.4 3.6 %collective-permute-start.4 = (f32[64,4,128]{2,1,0:T(4,128)S(1)}, f32[64,4,128]{2,1,0:T(4,128)S(1)}, u32[]{:S(2)}, u32[]{:S(2)}) collective-permute-start(f32[64,4,128]{2,1,0:T(4,128)S(1)} %get-tuple-element.12), channel_id=1, source_target_pairs={{1,0},{2,1},{3,2},{4,3},{5,4},{6,5},{7,6},{8,7},{9,8},{10,9},{11,1... | collective-permute-start | bytes 393224 | tf_op jit(solution)/shard_map/ppermute | solution.py:22
  95.7 1.4 fusion.66
  97.2 1.9 collective-permute-start.13
  99.1 3.6 %collective-permute-start.12 = (f32[64,4,128]{2,1,0:T(4,128)S(1)}, f32[64,4,128]{2,1,0:T(4,128)S(1)}, u32[]{:S(2)}, u32[]{:S(2)}) collective-permute-start(f32[64,4,128]{2,1,0:T(4,128)S(1)} %get-tuple-element.16), channel_id=1, source_target_pairs={{1,0},{2,1},{3,2},{4,3},{5,4},{6,5},{7,6},{8,7},{9,8},{10,9},{11,1... | collective-permute-start | bytes 393224 | tf_op jit(solution)/shard_map/ppermute | solution.py:22
  103.4 2.1 %fusion.5 = f32[64,8,128]{2,1,0:T(8,128)S(1)} fusion(f32[64,8,128]{2,1,0:T(8,128)S(1)} %fusion.4, f32[64,4,128]{2,1,0:T(4,128)S(1)} %collective-permute-done.5, f32[64,4,128]{2,1,0:T(4,128)S(1)} %collective-permute-done.4, f32[72,16,136]{2,1,0:T(8,128)S(1)} %select_maximum_fusion.10, f32[64,8,128]{2,1,0:T(8,128)S(1)} %fusion.3, f32[]{:T(128)} %bitcast.9, ...), kind=kLoop, calls=%fused_computation.128 | loop fusion | flops 3080192 | bytes 5505796 | tf_op jit(solution)/shard_map/add | solution.py:104
  105.5 1.9 collective-permute-start.6
  107.5 2.4 %collective-permute-start.7 = (f32[64,4,128]{2,1,0:T(4,128)S(1)}, f32[64,4,128]{2,1,0:T(4,128)S(1)}, u32[]{:S(2)}, u32[]{:S(2)}) collective-permute-start(f32[64,4,128]{2,1,0:T(4,128)S(1)} %get-tuple-element.10), channel_id=1, source_target_pairs={{0,1},{1,2},{2,3},{3,4},{4,5},{5,6},{6,7},{7,8},{8,9},{9,10},{10,1... | collective-permute-start | bytes 393224 | tf_op jit(solution)/shard_map/ppermute | solution.py:21
  110.5 1.4 fusion.41
  112.0 3.2 %collective-permute-start.14 = (f32[64,4,128]{2,1,0:T(4,128)S(1)}, f32[64,4,128]{2,1,0:T(4,128)S(1)}, u32[]{:S(2)}, u32[]{:S(2)}) collective-permute-start(f32[64,4,128]{2,1,0:T(4,128)S(1)} %get-tuple-element.9), channel_id=1, source_target_pairs={{1,0},{2,1},{3,2},{4,3},{5,4},{6,5},{7,6},{8,7},{9,8},{10,9},{11,1... | collective-permute-start | bytes 393224 | tf_op jit(solution)/shard_map/ppermute | solution.py:22
  115.1 2.1 %collective-permute-start.15 = (f32[64,4,128]{2,1,0:T(4,128)S(1)}, f32[64,4,128]{2,1,0:T(4,128)S(1)}, u32[]{:S(2)}, u32[]{:S(2)}) collective-permute-start(f32[64,4,128]{2,1,0:T(4,128)S(1)} %get-tuple-element.8), channel_id=1, source_target_pairs={{0,1},{1,2},{2,3},{3,4},{4,5},{5,6},{6,7},{7,8},{8,9},{9,10},{10,1... | collective-permute-start | bytes 393224 | tf_op jit(solution)/shard_map/ppermute | solution.py:21
  117.9 3.5 %collective-permute-done.15 = f32[64,4,128]{2,1,0:T(4,128)S(1)} collective-permute-done((f32[64,4,128]{2,1,0:T(4,128)S(1)}, f32[64,4,128]{2,1,0:T(4,128)S(1)}, u32[]{:S(2)}, u32[]{:S(2)}) %collective-permute-start.15) | collective-permute-done | bytes 131104 | tf_op jit(solution)/shard_map/ppermute | solution.py:21
  122.1 4.1 %multiply_add_fusion = (f32[64,8,128]{2,1,0:T(8,128)S(1)}, f32[64,8,128]{2,1,0:T(8,128)}, f32[64,8,128]{2,1,0:T(8,128)}) fusion(f32[64,8,128]{2,1,0:T(8,128)S(1)} %fusion.3, f32[64,8,128]{2,1,0:T(8,128)S(1)} %fusion.41, f32[64,8,128]{2,1,0:T(8,128)S(1)} %fusion.4, f32[64,8,128]{2,1,0:T(8,128)S(1)} %fusion.66, f32[64,8,128]{2,1,0:T(8,128)S(1)} %fusion.5, ...), kind=kLoop, calls=%fused_computation.440 | loop fusion | flops 6488064 | bytes 12092196 | tf_op jit(solution)/shard_map/add | solution.py:120
  126.2 1.9 gather_fusion.1
  128.1 3.4 %select_select_fusion = f32[512,8,128]{2,1,0:T(8,128)} fusion(f32[512,8,128]{2,1,0:T(8,128)S(1)} %gather_fusion.1, pred[512]{0:T(512)(128)(4,1)S(1)} %copy-done.15, pred[512]{0:T(512)(128)(4,1)S(1)} %copy-done.16), kind=kLoop, calls=%fused_computation.2 | loop fusion | flops 1048576 | bytes 4195328 | tf_op jit(solution)/shard_map/jit(_where)/select_n | solution.py:128
  131.5 61.3 %reduce-scatter.2.cloned.1.call-done = f32[64,8,128]{2,1,0:T(8,128)} async-done(((f32[512,8,128]{2,1,0:T(8,128)}), f32[64,8,128]{2,1,0:T(8,128)}) %reduce-scatter.2.cloned.1.call-update) | async-done | bytes 262160 | tf_op jit(solution)/shard_map/reduce_scatter | solution.py:127
  (102 shorter events, 15.6 us)
Async XLA Ops:
  7.2 20.9 %copy-start = (f32[8,4]{0,1:T(4,128)S(1)}, f32[8,4]{0,1:T(4,128)}, u32[]{:S(2)}) copy-start(f32[8,4]{0,1:T(4,128)} %param.18) | copy-start | bytes 388
  7.2 26.5 %copy-start.1 = (f32[1,64,8,128]{3,2,1,0:T(8,128)S(1)}, f32[1,64,8,128]{3,2,1,0:T(8,128)}, u32[]{:S(2)}) copy-start(f32[1,64,8,128]{3,2,1,0:T(8,128)} %param.13) | copy-start | bytes 786436
  7.2 16.0 %copy-start.17 = (s32[8]{0:T(128)S(1)}, s32[8]{0:T(128)}, u32[]{:S(2)}) copy-start(s32[8]{0:T(128)} %param.21) | copy-start | bytes 100
  7.2 16.6 %copy-start.18 = (s32[8]{0:T(128)S(1)}, s32[8]{0:T(128)}, u32[]{:S(2)}) copy-start(s32[8]{0:T(128)} %param.20) | copy-start | bytes 100
  7.2 17.2 %copy-start.19 = (s32[8]{0:T(128)S(1)}, s32[8]{0:T(128)}, u32[]{:S(2)}) copy-start(s32[8]{0:T(128)} %param.19) | copy-start | bytes 100
  7.2 17.8 %copy-start.20 = (s32[8]{0:T(128)S(1)}, s32[8]{0:T(128)}, u32[]{:S(2)}) copy-start(s32[8]{0:T(128)} %param.22) | copy-start | bytes 100
  7.2 23.5 %copy-start.10 = (bf16[1,4,64,128]{3,2,1,0:T(8,128)(2,1)S(1)}, bf16[1,4,64,128]{3,2,1,0:T(8,128)(2,1)}, u32[]{:S(2)}) copy-start(bf16[1,4,64,128]{3,2,1,0:T(8,128)(2,1)} %param.23) | copy-start | bytes 196612
  7.2 61.2 %all-gather.2.cloned.1.call-start = ((), (), s32[]{:S(2)}) async-start(), calls=%async_computation.1 | async-start | bytes 2359296 | tf_op jit(solution)/shard_map/all_gather | solution.py:71
  8.4 25.3 %collective-permute-start.1 = (f32[64,4,128]{2,1,0:T(4,128)S(1)}, f32[64,4,128]{2,1,0:T(4,128)S(1)}, u32[]{:S(2)}, u32[]{:S(2)}) collective-permute-start(f32[64,4,128]{2,1,0:T(4,128)S(1)} %get-tuple-element.23), channel_id=1, source_target_pairs={{0,1},{1,2},{2,3},{3,4},{4,5},{5,6},{6,7},{7,8},{8,9},{9,10},{10,1... | collective-permute-start | bytes 393224 | tf_op jit(solution)/shard_map/ppermute | solution.py:21
  10.3 23.4 %collective-permute-start = (f32[64,4,128]{2,1,0:T(4,128)S(1)}, f32[64,4,128]{2,1,0:T(4,128)S(1)}, u32[]{:S(2)}, u32[]{:S(2)}) collective-permute-start(f32[64,4,128]{2,1,0:T(4,128)S(1)} %get-tuple-element.22), channel_id=1, source_target_pairs={{1,0},{2,1},{3,2},{4,3},{5,4},{6,5},{7,6},{8,7},{9,8},{10,9},{11,1... | collective-permute-start | bytes 393224 | tf_op jit(solution)/shard_map/ppermute | solution.py:22
  14.0 178.8 %reduce-scatter.2.cloned.1.call-start = ((), (), s32[]{:S(2)}) async-start(), calls=%async_computation.2 | async-start | bytes 2359296 | tf_op jit(solution)/shard_map/reduce_scatter | solution.py:127
  14.1 20.3 %copy-start.2 = (f32[1,64,8,128]{3,2,1,0:T(8,128)S(1)}, f32[1,64,8,128]{3,2,1,0:T(8,128)}, u32[]{:S(2)}) copy-start(f32[1,64,8,128]{3,2,1,0:T(8,128)} %param.14) | copy-start | bytes 786436
  15.2 19.1 %collective-permute-start.9 = (f32[64,4,128]{2,1,0:T(4,128)S(1)}, f32[64,4,128]{2,1,0:T(4,128)S(1)}, u32[]{:S(2)}, u32[]{:S(2)}) collective-permute-start(f32[64,4,128]{2,1,0:T(4,128)S(1)} %get-tuple-element.21), channel_id=1, source_target_pairs={{0,1},{1,2},{2,3},{3,4},{4,5},{5,6},{6,7},{7,8},{8,9},{9,10},{10,1... | collective-permute-start | bytes 393224 | tf_op jit(solution)/shard_map/ppermute | solution.py:21
  17.4 16.9 %collective-permute-start.8 = (f32[64,4,128]{2,1,0:T(4,128)S(1)}, f32[64,4,128]{2,1,0:T(4,128)S(1)}, u32[]{:S(2)}, u32[]{:S(2)}) collective-permute-start(f32[64,4,128]{2,1,0:T(4,128)S(1)} %get-tuple-element.20), channel_id=1, source_target_pairs={{1,0},{2,1},{3,2},{4,3},{5,4},{6,5},{7,6},{8,7},{9,8},{10,9},{11,1... | collective-permute-start | bytes 393224 | tf_op jit(solution)/shard_map/ppermute | solution.py:22
  70.8 8.8 %copy-start.4 = (f32[64,4,128]{2,1,0:T(4,128)S(1)}, f32[64,4,128]{2,1,0:T(4,128)}, u32[]{:S(2)}) copy-start(f32[64,4,128]{2,1,0:T(4,128)} %copy-done.3) | copy-start | bytes 393220
  70.8 8.8 %copy-start.5 = (f32[1,64,8,128]{3,2,1,0:T(8,128)S(1)}, f32[1,64,8,128]{3,2,1,0:T(8,128)}, u32[]{:S(2)}) copy-start(f32[1,64,8,128]{3,2,1,0:T(8,128)} %param.15) | copy-start | bytes 786436
  70.8 8.8 %copy-start.9 = (f32[64,128]{1,0:T(8,128)S(1)}, f32[64,128]{1,0:T(8,128)}, u32[]{:S(2)}) copy-start(f32[64,128]{1,0:T(8,128)} %get-tuple-element.26) | copy-start | bytes 98308
  70.8 8.8 %copy-start.11 = (pred[64]{0:T(512)(128)(4,1)S(1)}, pred[64]{0:T(512)(128)(4,1)}, u32[]{:S(2)}) copy-start(pred[64]{0:T(512)(128)(4,1)} %and.139) | copy-start | bytes 196
  70.8 8.8 %copy-start.14 = (f32[8]{0:T(128)S(1)}, f32[8]{0:T(128)}, u32[]{:S(2)}) copy-start(f32[8]{0:T(128)} %compare_convert_fusion) | copy-start | bytes 100
  74.0 12.7 %collective-permute-start.3 = (f32[64,4,128]{2,1,0:T(4,128)S(1)}, f32[64,4,128]{2,1,0:T(4,128)S(1)}, u32[]{:S(2)}, u32[]{:S(2)}) collective-permute-start(f32[64,4,128]{2,1,0:T(4,128)S(1)} %get-tuple-element.15), channel_id=1, source_target_pairs={{0,1},{1,2},{2,3},{3,4},{4,5},{5,6},{6,7},{7,8},{8,9},{9,10},{10,1... | collective-permute-start | bytes 393224 | tf_op jit(solution)/shard_map/ppermute | solution.py:21
  75.9 10.8 %collective-permute-start.2 = (f32[64,4,128]{2,1,0:T(4,128)S(1)}, f32[64,4,128]{2,1,0:T(4,128)S(1)}, u32[]{:S(2)}, u32[]{:S(2)}) collective-permute-start(f32[64,4,128]{2,1,0:T(4,128)S(1)} %get-tuple-element.14), channel_id=1, source_target_pairs={{1,0},{2,1},{3,2},{4,3},{5,4},{6,5},{7,6},{8,7},{9,8},{10,9},{11,1... | collective-permute-start | bytes 393224 | tf_op jit(solution)/shard_map/ppermute | solution.py:22
  81.1 13.9 %collective-permute-start.11 = (f32[64,4,128]{2,1,0:T(4,128)S(1)}, f32[64,4,128]{2,1,0:T(4,128)S(1)}, u32[]{:S(2)}, u32[]{:S(2)}) collective-permute-start(f32[64,4,128]{2,1,0:T(4,128)S(1)} %get-tuple-element.19), channel_id=1, source_target_pairs={{0,1},{1,2},{2,3},{3,4},{4,5},{5,6},{6,7},{7,8},{8,9},{9,10},{10,1... | collective-permute-start | bytes 393224 | tf_op jit(solution)/shard_map/ppermute | solution.py:21
  83.0 12.0 %collective-permute-start.10 = (f32[64,4,128]{2,1,0:T(4,128)S(1)}, f32[64,4,128]{2,1,0:T(4,128)S(1)}, u32[]{:S(2)}, u32[]{:S(2)}) collective-permute-start(f32[64,4,128]{2,1,0:T(4,128)S(1)} %get-tuple-element.18), channel_id=1, source_target_pairs={{1,0},{2,1},{3,2},{4,3},{5,4},{6,5},{7,6},{8,7},{9,8},{10,9},{11,1... | collective-permute-start | bytes 393224 | tf_op jit(solution)/shard_map/ppermute | solution.py:22
  89.4 6.3 %copy-start.8 = (f32[64,128]{1,0:T(8,128)S(1)}, f32[64,128]{1,0:T(8,128)}, u32[]{:S(2)}) copy-start(f32[64,128]{1,0:T(8,128)} %get-tuple-element.25) | copy-start | bytes 98308
  89.5 13.3 %collective-permute-start.5 = (f32[64,4,128]{2,1,0:T(4,128)S(1)}, f32[64,4,128]{2,1,0:T(4,128)S(1)}, u32[]{:S(2)}, u32[]{:S(2)}) collective-permute-start(f32[64,4,128]{2,1,0:T(4,128)S(1)} %get-tuple-element.13), channel_id=1, source_target_pairs={{0,1},{1,2},{2,3},{3,4},{4,5},{5,6},{6,7},{7,8},{8,9},{9,10},{10,1... | collective-permute-start | bytes 393224 | tf_op jit(solution)/shard_map/ppermute | solution.py:21
  91.4 11.4 %collective-permute-start.4 = (f32[64,4,128]{2,1,0:T(4,128)S(1)}, f32[64,4,128]{2,1,0:T(4,128)S(1)}, u32[]{:S(2)}, u32[]{:S(2)}) collective-permute-start(f32[64,4,128]{2,1,0:T(4,128)S(1)} %get-tuple-element.12), channel_id=1, source_target_pairs={{1,0},{2,1},{3,2},{4,3},{5,4},{6,5},{7,6},{8,7},{9,8},{10,9},{11,1... | collective-permute-start | bytes 393224 | tf_op jit(solution)/shard_map/ppermute | solution.py:22
  97.2 12.7 %collective-permute-start.13 = (f32[64,4,128]{2,1,0:T(4,128)S(1)}, f32[64,4,128]{2,1,0:T(4,128)S(1)}, u32[]{:S(2)}, u32[]{:S(2)}) collective-permute-start(f32[64,4,128]{2,1,0:T(4,128)S(1)} %get-tuple-element.17), channel_id=1, source_target_pairs={{0,1},{1,2},{2,3},{3,4},{4,5},{5,6},{6,7},{7,8},{8,9},{9,10},{10,1... | collective-permute-start | bytes 393224 | tf_op jit(solution)/shard_map/ppermute | solution.py:21
  99.1 10.8 %collective-permute-start.12 = (f32[64,4,128]{2,1,0:T(4,128)S(1)}, f32[64,4,128]{2,1,0:T(4,128)S(1)}, u32[]{:S(2)}, u32[]{:S(2)}) collective-permute-start(f32[64,4,128]{2,1,0:T(4,128)S(1)} %get-tuple-element.16), channel_id=1, source_target_pairs={{1,0},{2,1},{3,2},{4,3},{5,4},{6,5},{7,6},{8,7},{9,8},{10,9},{11,1... | collective-permute-start | bytes 393224 | tf_op jit(solution)/shard_map/ppermute | solution.py:22
  105.5 11.7 %collective-permute-start.6 = (f32[64,4,128]{2,1,0:T(4,128)S(1)}, f32[64,4,128]{2,1,0:T(4,128)S(1)}, u32[]{:S(2)}, u32[]{:S(2)}) collective-permute-start(f32[64,4,128]{2,1,0:T(4,128)S(1)} %get-tuple-element.11), channel_id=1, source_target_pairs={{1,0},{2,1},{3,2},{4,3},{5,4},{6,5},{7,6},{8,7},{9,8},{10,9},{11,1... | collective-permute-start | bytes 393224 | tf_op jit(solution)/shard_map/ppermute | solution.py:22
  107.5 9.8 %collective-permute-start.7 = (f32[64,4,128]{2,1,0:T(4,128)S(1)}, f32[64,4,128]{2,1,0:T(4,128)S(1)}, u32[]{:S(2)}, u32[]{:S(2)}) collective-permute-start(f32[64,4,128]{2,1,0:T(4,128)S(1)} %get-tuple-element.10), channel_id=1, source_target_pairs={{0,1},{1,2},{2,3},{3,4},{4,5},{5,6},{6,7},{7,8},{8,9},{9,10},{10,1... | collective-permute-start | bytes 393224 | tf_op jit(solution)/shard_map/ppermute | solution.py:21
  112.0 5.9 %collective-permute-start.14 = (f32[64,4,128]{2,1,0:T(4,128)S(1)}, f32[64,4,128]{2,1,0:T(4,128)S(1)}, u32[]{:S(2)}, u32[]{:S(2)}) collective-permute-start(f32[64,4,128]{2,1,0:T(4,128)S(1)} %get-tuple-element.9), channel_id=1, source_target_pairs={{1,0},{2,1},{3,2},{4,3},{5,4},{6,5},{7,6},{8,7},{9,8},{10,9},{11,1... | collective-permute-start | bytes 393224 | tf_op jit(solution)/shard_map/ppermute | solution.py:22
  115.1 6.3 %collective-permute-start.15 = (f32[64,4,128]{2,1,0:T(4,128)S(1)}, f32[64,4,128]{2,1,0:T(4,128)S(1)}, u32[]{:S(2)}, u32[]{:S(2)}) collective-permute-start(f32[64,4,128]{2,1,0:T(4,128)S(1)} %get-tuple-element.8), channel_id=1, source_target_pairs={{0,1},{1,2},{2,3},{3,4},{4,5},{5,6},{6,7},{7,8},{8,9},{9,10},{10,1... | collective-permute-start | bytes 393224 | tf_op jit(solution)/shard_map/ppermute | solution.py:21
  (7 other events, 24.0 us)
Sparse Core Ops, SparseCore 0:
  14.1 54.2 all-gather.1
  131.6 61.1 reduce-scatter.1
where the time goes:
time: 201 us; the launch traced here: 200 us
  waiting for transfers between devices  98.3 us (49%)
  starting transfers between devices  44.5 us (22%)
  other arithmetic  31.3 us (16%)
  between operations  14.8 us (7%)
  local copies, waits for them, and re-layouts  10.7 us (5%)
    reduce_scatter x1, waiting for transfers between devices, local(): lax.psum_scatter(jnp.where(found[:, None, None], picked, 0.0), 'shot', sc...  61.3 us
    all_gather x1, waiting for transfers between devices, local(): block_rows = lax.all_gather(velocity, 'shot', axis=0, tiled=True)  33.4 us
    ppermute x8, starting transfers between devices, with_halo(): after = lax.ppermute(initial, axis, down)  28.1 us
    ppermute x8, starting transfers between devices, with_halo(): before = lax.ppermute(last, axis, up)  16.3 us
    add x3, other arithmetic, local(): 2.0 * src_now - src_old + rate_field * laplace(ext_src)  7.25 us
    concatenate x8, other arithmetic, with_halo(): array = jnp.concatenate([before, array, after], axis=dim)  4.91 us
    add x3, other arithmetic, local(): 2.0 * rec_now - rec_later + rate_field * laplace(ext_rec)  4.2 us
    add x1, other arithmetic, local(): image_sum = image_sum + src_snaps[STEPS - back] * rec_snaps[back]  4.07 us
  transfers between devices with their start and end apart: 18, of which 3 were waited for; matrix products, arithmetic and copies ran while one was open for 13% of the time, Pallas kernels for 0%

commit v1 on v0

v1 whole, which is shorter than its diff:
```python
import functools

import jax
import jax.numpy as jnp
from jax import lax
from jax.experimental import pallas as pl
from jax.experimental.pallas import tpu as pltpu
from jax.sharding import PartitionSpec as P

BX = 8
KT = 8
STEPS = 4
CAP = 2
REACH = 4
CHUNK = 8
VMEM = pltpu.VMEM
SMEM = pltpu.SMEM

COEFFS = (-205.0 / 72.0, 8.0 / 5.0, -1.0 / 5.0, 8.0 / 315.0, -1.0 / 560.0)


def call(body, outs, in_spaces, *args, scratch=(), flops=0, bytes_accessed=0):
    return pl.pallas_call(
        body,
        out_shape=[jax.ShapeDtypeStruct(s, jnp.float32) for s in outs],
        in_specs=[pl.BlockSpec(memory_space=s) for s in in_spaces],
        out_specs=[pl.BlockSpec(memory_space=VMEM) for _ in outs],
        scratch_shapes=list(scratch),
        compiler_params=pltpu.CompilerParams(vmem_limit_bytes=24 * 1024 * 1024),
        cost_estimate=pl.CostEstimate(
            flops=flops, bytes_accessed=bytes_accessed, transcendentals=0
        ),
    )(*args)


def rows_of(shape):
    return lax.broadcasted_iota(jnp.int32, shape, len(shape) - 2)


def pack_pairs(field, low_ref, high_ref, at, odd):
    pairs = field.reshape(field.shape[0] // 2, 2, 8, field.shape[2])
    first, second = pairs[:, 0], pairs[:, 1]
    top = rows_of(first.shape) < REACH
    low = jnp.where(top, first, pltpu.roll(second, REACH, 1))
    high = jnp.where(top, pltpu.roll(first, REACH, 1), second)
    low_ref[at] = jnp.where(odd, high, low)
    high_ref[at] = jnp.where(odd, low, high)


def pack_kernel(tiles, vel, src, rec, send, to_far, to_near):
    shot = lax.axis_index("shot")
    odd = lax.rem(lax.axis_index("slab"), 2) == 1
    n_shot = send.shape[0]

    def one_shot(g, _):
        before = jnp.int32(0)
        for k in range(KT):
            before += (tiles[g, k] < shot * BX).astype(jnp.int32)
        for j in range(CAP):
            k = jnp.minimum(before + j, KT - 1)
            own = jnp.clip(tiles[g, k] - shot * BX, 0, vel.shape[0] // BX - 1)
            send[g, pl.ds(j * BX, BX)] = vel[pl.ds(own * BX, BX)]
        return 0

    lax.fori_loop(0, n_shot, one_shot, 0)
    half = src.shape[0] // 2
    for f, field in enumerate((src, rec)):

        def one_chunk(c, _):
            at = pl.ds(f * half + c * (CHUNK // 2), CHUNK // 2)
            pack_pairs(field[pl.ds(c * CHUNK, CHUNK)], to_far, to_near, at, odd)
            return 0

        lax.fori_loop(0, field.shape[0] // CHUNK, one_chunk, 0)


def interior_kernel(src, rec, src_lap, rec_lap, padded):
    size_x, size_z, size_y = src.shape
    zeros = jnp.zeros((REACH, size_z, size_y), jnp.float32)
    shape = (1, size_z, size_y)
    row = rows_of(shape)
    lane = lax.broadcasted_iota(jnp.int32, shape, 2)
    padded[pl.ds(0, REACH)] = zeros
    padded[pl.ds(REACH + size_x, REACH)] = zeros
    for field, out in ((src, src_lap), (rec, rec_lap)):
        padded[pl.ds(REACH, size_x)] = field[...]

        def one_chunk(c, _):
            base = c * CHUNK
            wide = padded[pl.ds(base, CHUNK + 2 * REACH)]
            centre = wide[REACH : REACH + CHUNK]
            total = (3.0 * COEFFS[0]) * centre
            for r in range(1, REACH + 1):
                terms = wide[REACH + r : REACH + r + CHUNK] + wide[REACH - r : REACH - r + CHUNK]
                terms += jnp.where(row < size_z - r, pltpu.roll(centre, size_z - r, 1), 0.0)
                terms += jnp.where(row >= r, pltpu.roll(centre, r, 1), 0.0)
                terms += jnp.where(lane < size_y - r, pltpu.roll(centre, size_y - r, 2), 0.0)
                terms += jnp.where(lane >= r, pltpu.roll(centre, r, 2), 0.0)
                total += COEFFS[r] * terms
            out[pl.ds(base, CHUNK)] = total
            return 0

        lax.fori_loop(0, size_x // CHUNK, one_chunk, 0)


def finish_kernel(
    step,
    tiles,
    wavelet,
    spot_x,
    spot_z,
    spot_y,
    depth,
    traces,
    far,
    near,
    src,
    src_old,
    src_lap,
    rec,
    rec_old,
    rec_lap,
    *rest,
):
    shot = lax.axis_index("shot")
    slab = lax.axis_index("slab")
    last_slab = lax.axis_size("slab") - 1
    odd = lax.rem(slab, 2) == 1
    first, last = step == 0, step == STEPS - 1
    rest = list(rest)
    if first:
        vel_got = rest.pop(0)
    else:
        rate = rest.pop(0)
    if last:
        partial, src_first, rec_first = rest[:3]
        rest = rest[3:]
    src_new, rec_new = rest[:2]
    rest = rest[2:]
    if first:
        rate = rest.pop(0)
    if last:
        send = rest.pop(0)
    else:
        to_far, to_near = rest[:2]
        rest = rest[2:]
    (plane_rows,) = rest
    size_x, size_z, size_y = src.shape

    def place_of(k):
        owner = lax.shift_right_logical(tiles[shot, k], 3)
        before = lax.shift_right_logical(tiles[shot, max(k - 1, 0)], 3)
        slot = (before == owner).astype(jnp.int32) if k else jnp.int32(0)
        return owner, pl.ds(slot * BX, BX)

    if first:
        for k in range(KT):
            owner, at = place_of(k)
            block = vel_got[owner, at]
            rate[pl.ds(k * BX, BX)] = block * block

    row = rows_of((1, size_z, size_y))
    top = row < REACH
    mine = jnp.where(odd, 0, 1)
    has_left, has_right = slab > 0, slab < last_slab
    keep = (top & has_right) | (jnp.logical_not(top) & has_left)
    weights = []
    for shift in range(1, size_z):
        weight = jnp.zeros((1, size_z, size_y), jnp.float32)
        if shift <= REACH:
            weight = jnp.where(row < shift, COEFFS[shift], weight)
        if size_z - shift <= REACH:
            weight = jnp.where(row >= shift, COEFFS[size_z - shift], weight)
        weights.append(weight)
    half = size_x // 2
    for f, (now, old, lap, new) in enumerate(
        ((src, src_old, src_lap, src_new), (rec, rec_old, rec_lap, rec_new))
    ):

        def one_chunk(c, _):
            at = pl.ds(c * CHUNK, CHUNK)
            packed = pl.ds(f * half + c * (CHUNK // 2), CHUNK // 2)
            from_far, from_near = far[packed], near[mine, packed]
            left = jnp.where(odd, from_near, from_far)
            right = jnp.where(odd, from_far, from_near)
            even_x = jnp.where(top, right, pltpu.roll(left, REACH, 1))
            odd_x = jnp.where(top, pltpu.roll(right, REACH, 1), left)
            halo = jnp.stack([even_x, odd_x], axis=1).reshape(CHUNK, size_z, size_y)
            halo = jnp.where(keep, halo, 0.0)
            total = lap[at]
            for shift in range(1, size_z):
                total += weights[shift - 1] * pltpu.roll(halo, shift, 1)
            value = now[at]
            new[at] = 2.0 * value - old[at] + rate[at] * total
            return 0

        lax.fori_loop(0, size_x // CHUNK, one_chunk, 0)

    local_spot = spot_z[shot] - slab * size_z
    row2 = lax.broadcasted_iota(jnp.int32, (size_z, size_y), 0)
    lane2 = lax.broadcasted_iota(jnp.int32, (size_z, size_y), 1)

    @pl.when((local_spot >= 0) & (local_spot < size_z))
    def _():
        x = spot_x[shot]
        here = (row2 == local_spot) & (lane2 == spot_y[shot])
        src_new[x] += jnp.where(here, wavelet[shot, step], 0.0)

    local_plane = depth[shot] - slab * size_z

    @pl.when((local_plane >= 0) & (local_plane < size_z))
    def _():
        plane_rows[...] = traces[STEPS - 1 - step].astype(jnp.float32)

        def one_x(x, _):
            line = plane_rows[pl.ds(x, 1)]
            rec_new[x] += jnp.where(row2 == local_plane, line, 0.0)
            return 0

        lax.fori_loop(0, size_x, one_x, 0)

    if last:
        send[...] = jnp.zeros(send.shape, jnp.float32)
        for k in range(KT):
            owner, slot = place_of(k)
            at = pl.ds(k * BX, BX)
            image = partial[at] + src_new[at] * rec_first[at] + src_first[at] * rec_new[at]
            send[owner, slot] = image
    else:
        for f, field in enumerate((src_new, rec_new)):

            def one_pack(c, _):
                packed = pl.ds(f * half + c * (CHUNK // 2), CHUNK // 2)
                pack_pairs(field[pl.ds(c * CHUNK, CHUNK)], to_far, to_near, packed, odd)
                return 0

            lax.fori_loop(0, size_x // CHUNK, one_pack, 0)


def gather_kernel(tiles, got, out):
    shot = lax.axis_index("shot")
    out[...] = jnp.zeros(out.shape, jnp.float32)

    def one_shot(g, _):
        before = jnp.int32(0)
        for k in range(KT):
            before += (tiles[g, k] < shot * BX).astype(jnp.int32)
        for j in range(CAP):
            k = jnp.minimum(before + j, KT - 1)
            own = tiles[g, k] - shot * BX

            @pl.when((before + j < KT) & (own >= 0) & (own < out.shape[0] // BX))
            def _():
                out[pl.ds(own * BX, BX)] += got[g, pl.ds(j * BX, BX)]

        return 0

    lax.fori_loop(0, got.shape[0], one_shot, 0)


def image_part(s1, s2, s3, r1, r2, r3):
    return s3 * r1 + s2 * r2 + s1 * r3


def local(
    src_prev,
    src_cur,
    rec_cur,
    rec_next,
    velocity,
    aperture_tiles,
    wavelet,
    src_x,
    src_z,
    src_y,
    rec_depth,
    rec_data,
):
    slabs = lax.axis_size("slab")
    shots = lax.axis_size("shot")
    far_pairs = []
    for i in range(1, slabs - 1, 2):
        far_pairs += [(i, i + 1), (i + 1, i)]
    near_groups = [[i, i + 1] for i in range(0, slabs, 2)]

    def exchange(to_far, to_near):
        far = lax.ppermute(to_far, "slab", far_pairs)
        near = lax.all_gather(to_near, "slab", axis_index_groups=near_groups)
        return far, near

    src_old, src = src_prev[0], src_cur[0]
    rec_old, rec = rec_next[0], rec_cur[0]
    block = src.shape
    buffer = (shots, CAP * BX) + block[1:]
    send, to_far, to_near = call(
        pack_kernel, [buffer, block, block], [SMEM] + [VMEM] * 3,
        aperture_tiles, velocity, src, rec,
    )
    vel_got = lax.all_to_all(send, "shot", 0, 0)
    snaps = [(src, rec)]
    rate = None
    for step in range(STEPS):
        first, last = step == 0, step == STEPS - 1
        far, near = exchange(to_far, to_near)
        src_lap, rec_lap = call(
            interior_kernel, [block, block], [VMEM] * 2, src, rec,
            scratch=[VMEM((block[0] + 2 * REACH,) + block[1:], jnp.float32)],
            flops=2 * 45 * src.size, bytes_accessed=4 * 4 * src.size,
        )
        args = [aperture_tiles, wavelet, src_x, src_z, src_y, rec_depth]
        args += [rec_data[0], far, near, src, src_old, src_lap, rec, rec_old, rec_lap]
        args += [vel_got] if first else [rate]
        outs = [block, block]
        if last:
            (s0, r0), (s1, r1), (s2, r2), (s3, r3) = snaps
            args += [image_part(s1, s2, s3, r1, r2, r3), s0, r0]
            outs += [buffer]
        else:
            outs += [block] * (3 if first else 2)
        spaces = [SMEM] * 6 + [VMEM] * (len(args) - 6)
        got = call(
            functools.partial(finish_kernel, step), outs, spaces, *args,
            scratch=[VMEM((block[0], block[2]), jnp.float32)],
            flops=2 * 30 * src.size, bytes_accessed=10 * 4 * src.size,
        )
        src_old, rec_old = src, rec
        src, rec = got[:2]
        snaps.append((src, rec))
        if last:
            send = got[2]
        elif first:
            rate, to_far, to_near = got[2:]
        else:
            to_far, to_near = got[2:]
    image_got = lax.all_to_all(send, "shot", 0, 0)
    (image,) = call(gather_kernel, [velocity.shape], [SMEM, VMEM], aperture_tiles, image_got)
    return image, src[None], rec[None]


def solution(mesh):
    wave = P("shot", None, "slab", None)
    model = P("shot", "slab", None)
    return jax.shard_map(
        local,
        mesh=mesh,
        in_specs=(wave,) * 4 + (model,) + (P(),) * 6 + (P("shot", None, None, None),),
        out_specs=(model, wave, wave),
        check_vma=False,
    )
```

time: 201 us -> 86.8 us (0.43)
  the two profiles are of different devices: /device:TPU:32 before, /device:TPU:16 now
where the time goes in v1:
time: 86.8 us; the launch traced here: 86.3 us
  starting transfers between devices  38.3 us (44%)
  blocking collectives  21.6 us (25%)
  Pallas kernels  19.2 us (22%)
  local copies, waits for them, and re-layouts  4.29 us (5%)
  waiting for transfers between devices  1.99 us (2%)
    ppermute x4, starting transfers between devices, exchange(): far = lax.ppermute(to_far, 'slab', far_pairs)  33.2 us
    pallas_call x10, Pallas kernels, call(): pl.pallas_call(body, out_shape=[jax.ShapeDtypeStruct(s, jnp.float32) for...  19.2 us
    all_to_all x1, blocking collectives, local(): image_got = lax.all_to_all(send, 'shot', 0, 0)  12.7 us
    all_gather x4, blocking collectives, exchange(): near = lax.all_gather(to_near, 'slab', axis_index_groups=near_groups)  8.86 us
    all_to_all x1, starting transfers between devices, local(): vel_got = lax.all_to_all(send, 'shot', 0, 0)  5.15 us
    unnamed x31, local copies, waits for them, and re-layouts  4.29 us
    ppermute x4, waiting for transfers between devices, exchange(): far = lax.ppermute(to_far, 'slab', far_pairs)  1.99 us
  transfers between devices with their start and end apart: 5, of which 1 were waited for; matrix products, arithmetic and copies ran while one was open for 0% of the time, Pallas kernels for 10%

profile of v1, /device:TPU:16, one launch (start us, length us, event | category | flops | bytes accessed | tf_op | source)
XLA Modules:
  0.0 86.3 jit_solution(11401241408757185663)
XLA Ops:
  0.6 0.0 copy-start
  0.6 0.9 %copy-done = f32[1,64,8,128]{3,2,1,0:T(8,128)S(1)} copy-done((f32[1,64,8,128]{3,2,1,0:T(8,128)S(1)}, f32[1,64,8,128]{3,2,1,0:T(8,128)}, u32[]{:S(2)}) %copy-start) | copy-done | bytes 262168
  1.6 0.9 %copy-done.2 = f32[1,64,8,128]{3,2,1,0:T(8,128)S(1)} copy-done((f32[1,64,8,128]{3,2,1,0:T(8,128)S(1)}, f32[1,64,8,128]{3,2,1,0:T(8,128)}, u32[]{:S(2)}) %copy-start.2) | copy-done | bytes 262168
  2.5 0.9 %copy-done.5 = f32[64,8,128]{2,1,0:T(8,128)S(1)} copy-done((f32[64,8,128]{2,1,0:T(8,128)S(1)}, f32[64,8,128]{2,1,0:T(8,128)}, u32[]{:S(2)}) %copy-start.5) | copy-done | bytes 262168
  3.5 0.7 copy-done.8
  4.2 1.8 %shard_map.139 = (f32[8,16,8,128]{3,2,1,0:T(8,128)}, f32[64,8,128]{2,1,0:T(8,128)S(1)}, f32[64,8,128]{2,1,0:T(8,128)S(1)}) custom-call(s32[8,8]{1,0:T(8,128)S(1)} %copy-done.8, f32[64,8,128]{2,1,0:T(8,128)S(1)} %copy-done.5, f32[64,8,128]{2,1,0:T(8,128)S(1)} %bitcast.11, f32[64,8,128]{2,1,0:T(8,128)S(1)} %bitcast.16), custom_call_target="tpu_custom_call" | custom-call | tf_op jit(solution)/shard_map/pallas_call | solution.py:23
  6.0 5.2 %all-to-all-start = ((f32[8,16,8,128]{3,2,1,0:T(8,128)}), f32[8,16,8,128]{3,2,1,0:T(8,128)S(1)}, u32[]{:S(2)}, u32[]{:S(2)}) async-start(f32[8,16,8,128]{3,2,1,0:T(8,128)} %get-tuple-element.34), calls=%async_computation | async-start | bytes 1048576 | tf_op jit(solution)/shard_map/all_to_all | solution.py:299
  11.1 10.6 %collective-permute-start = (f32[64,8,128]{2,1,0:T(8,128)S(1)}, f32[64,8,128]{2,1,0:T(8,128)S(1)}, u32[]{:S(2)}, u32[]{:S(2)}) collective-permute-start(f32[64,8,128]{2,1,0:T(8,128)S(1)} %get-tuple-element.30), channel_id=1, source_target_pairs={{1,2},{2,1},{3,4},{4,3},{5,6},{6,5},{7,8},{8,7},{9,10},{10,9},{11,... | collective-permute-start | bytes 786440 | tf_op jit(solution)/shard_map/ppermute | solution.py:287
  21.8 0.1 copy.22.wavelet
  21.8 2.2 %shard_map.140 = (f32[64,8,128]{2,1,0:T(8,128)S(1)}, f32[64,8,128]{2,1,0:T(8,128)S(1)}) custom-call(f32[64,8,128]{2,1,0:T(8,128)S(1)} %bitcast.12, f32[64,8,128]{2,1,0:T(8,128)S(1)} %bitcast.17), custom_call_target="tpu_custom_call" | custom-call | flops 5898240 | bytes 1048576 | tf_op jit(solution)/shard_map/pallas_call | solution.py:23
  24.1 0.0 copy-start.7
  24.1 0.0 copy-start.13
  24.1 2.3 %all-gather = f32[128,8,128]{2,1,0:T(8,128)S(1)} all-gather(f32[64,8,128]{2,1,0:T(8,128)S(1)} %get-tuple-element.31), channel_id=2, replica_groups={{0,1},{2,3},{4,5},{6,7},{8,9},{10,11},{12,13},{14,15},{16,17},{18,19},{..., dimensions={0}, use_global_device_ids=true | all-gather | bytes 786432 | tf_op jit(solution)/shard_map/all_gather | solution.py:288
  26.5 0.6 copy-done.9
  27.1 0.0 copy-done.12
  27.2 1.5 %shard_map.141 = (f32[64,8,128]{2,1,0:T(8,128)S(1)}, f32[64,8,128]{2,1,0:T(8,128)S(1)}, f32[64,8,128]{2,1,0:T(8,128)S(1)}, f32[64,8,128]{2,1,0:T(8,128)S(1)}, f32[64,8,128]{2,1,0:T(8,128)S(1)}) custom-call(s32[8,8]{1,0:T(8,128)S(1)} %copy-done.9, f32[8,4]{1,0:T(8,128)S(1)} %copy.22.wavelet, s32[8]{0:T(128)S(1)} %copy-done.10, s32[8]{0:T(128)S(1)} %copy-done.11, ...), custom_call_target="tpu_custom_call" | custom-call | flops 3932160 | bytes 2621440 | tf_op jit(solution)/shard_map/pallas_call | solution.py:23
  28.7 8.8 %collective-permute-start.1 = (f32[64,8,128]{2,1,0:T(8,128)S(1)}, f32[64,8,128]{2,1,0:T(8,128)S(1)}, u32[]{:S(2)}, u32[]{:S(2)}) collective-permute-start(f32[64,8,128]{2,1,0:T(8,128)S(1)} %get-tuple-element.35), channel_id=1, source_target_pairs={{1,2},{2,1},{3,4},{4,3},{5,6},{6,5},{7,8},{8,7},{9,10},{10,9},{11,... | collective-permute-start | bytes 786440 | tf_op jit(solution)/shard_map/ppermute | solution.py:287
  37.6 2.2 %shard_map.142 = (f32[64,8,128]{2,1,0:T(8,128)S(1)}, f32[64,8,128]{2,1,0:T(8,128)S(1)}) custom-call(f32[64,8,128]{2,1,0:T(8,128)S(1)} %get-tuple-element.37.src.src_old, f32[64,8,128]{2,1,0:T(8,128)S(1)} %get-tuple-element.38.rec.rec_old), custom_call_target="tpu_custom_call" | custom-call | flops 5898240 | bytes 1048576 | tf_op jit(solution)/shard_map/pallas_call | solution.py:23
  39.8 2.2 %all-gather.1 = f32[128,8,128]{2,1,0:T(8,128)S(1)} all-gather(f32[64,8,128]{2,1,0:T(8,128)S(1)} %get-tuple-element.36), channel_id=3, replica_groups={{0,1},{2,3},{4,5},{6,7},{8,9},{10,11},{12,13},{14,15},{16,17},{18,19},{..., dimensions={0}, use_global_device_ids=true | all-gather | bytes 786432 | tf_op jit(solution)/shard_map/all_gather | solution.py:288
  42.0 1.5 %shard_map.143 = (f32[64,8,128]{2,1,0:T(8,128)S(1)}, f32[64,8,128]{2,1,0:T(8,128)S(1)}, f32[64,8,128]{2,1,0:T(8,128)S(1)}, f32[64,8,128]{2,1,0:T(8,128)S(1)}) custom-call(s32[8,8]{1,0:T(8,128)S(1)} %copy-done.9, f32[8,4]{1,0:T(8,128)S(1)} %copy.22.wavelet, s32[8]{0:T(128)S(1)} %copy-done.10, s32[8]{0:T(128)S(1)} %copy-done.11, s32[8]{0:T(128)S(1)} %copy-done.12, ...), custom_call_target="tpu_custom_call" | custom-call | flops 3932160 | bytes 2621440 | tf_op jit(solution)/shard_map/pallas_call | solution.py:23
  43.5 6.9 %collective-permute-start.2 = (f32[64,8,128]{2,1,0:T(8,128)S(1)}, f32[64,8,128]{2,1,0:T(8,128)S(1)}, u32[]{:S(2)}, u32[]{:S(2)}) collective-permute-start(f32[64,8,128]{2,1,0:T(8,128)S(1)} %get-tuple-element.42), channel_id=1, source_target_pairs={{1,2},{2,1},{3,4},{4,3},{5,6},{6,5},{7,8},{8,7},{9,10},{10,9},{11,... | collective-permute-start | bytes 786440 | tf_op jit(solution)/shard_map/ppermute | solution.py:287
  50.3 2.2 %shard_map.144 = (f32[64,8,128]{2,1,0:T(8,128)S(1)}, f32[64,8,128]{2,1,0:T(8,128)S(1)}) custom-call(f32[64,8,128]{2,1,0:T(8,128)S(1)} %get-tuple-element.44.src.src_old, f32[64,8,128]{2,1,0:T(8,128)S(1)} %get-tuple-element.45.rec.rec_old), custom_call_target="tpu_custom_call" | custom-call | flops 5898240 | bytes 1048576 | tf_op jit(solution)/shard_map/pallas_call | solution.py:23
  52.6 2.2 %all-gather.2 = f32[128,8,128]{2,1,0:T(8,128)S(1)} all-gather(f32[64,8,128]{2,1,0:T(8,128)S(1)} %get-tuple-element.43), channel_id=4, replica_groups={{0,1},{2,3},{4,5},{6,7},{8,9},{10,11},{12,13},{14,15},{16,17},{18,19},{..., dimensions={0}, use_global_device_ids=true | all-gather | bytes 786432 | tf_op jit(solution)/shard_map/all_gather | solution.py:288
  54.8 1.5 %shard_map.145 = (f32[64,8,128]{2,1,0:T(8,128)S(1)}, f32[64,8,128]{2,1,0:T(8,128)S(1)}, f32[64,8,128]{2,1,0:T(8,128)S(1)}, f32[64,8,128]{2,1,0:T(8,128)S(1)}) custom-call(s32[8,8]{1,0:T(8,128)S(1)} %copy-done.9, f32[8,4]{1,0:T(8,128)S(1)} %copy.22.wavelet, s32[8]{0:T(128)S(1)} %copy-done.10, s32[8]{0:T(128)S(1)} %copy-done.11, s32[8]{0:T(128)S(1)} %copy-done.12, ...), custom_call_target="tpu_custom_call" | custom-call | flops 3932160 | bytes 2621440 | tf_op jit(solution)/shard_map/pallas_call | solution.py:23
  56.2 6.9 %collective-permute-start.3 = (f32[64,8,128]{2,1,0:T(8,128)S(1)}, f32[64,8,128]{2,1,0:T(8,128)S(1)}, u32[]{:S(2)}, u32[]{:S(2)}) collective-permute-start(f32[64,8,128]{2,1,0:T(8,128)S(1)} %get-tuple-element.48), channel_id=1, source_target_pairs={{1,2},{2,1},{3,4},{4,3},{5,6},{6,5},{7,8},{8,7},{9,10},{10,9},{11,... | collective-permute-start | bytes 786440 | tf_op jit(solution)/shard_map/ppermute | solution.py:287
  63.1 2.2 %all-gather.3 = f32[128,8,128]{2,1,0:T(8,128)S(1)} all-gather(f32[64,8,128]{2,1,0:T(8,128)S(1)} %get-tuple-element.49), channel_id=5, replica_groups={{0,1},{2,3},{4,5},{6,7},{8,9},{10,11},{12,13},{14,15},{16,17},{18,19},{..., dimensions={0}, use_global_device_ids=true | all-gather | bytes 786432 | tf_op jit(solution)/shard_map/all_gather | solution.py:288
  65.3 2.2 %shard_map.146 = (f32[64,8,128]{2,1,0:T(8,128)S(1)}, f32[64,8,128]{2,1,0:T(8,128)S(1)}) custom-call(f32[64,8,128]{2,1,0:T(8,128)S(1)} %get-tuple-element.50.src, f32[64,8,128]{2,1,0:T(8,128)S(1)} %get-tuple-element.51.rec), custom_call_target="tpu_custom_call" | custom-call | flops 5898240 | bytes 1048576 | tf_op jit(solution)/shard_map/pallas_call | solution.py:23
  67.5 0.1 multiply_add_fusion.rest_1_
  67.6 2.0 %collective-permute-done.3.far = f32[64,8,128]{2,1,0:T(8,128)S(1)} collective-permute-done((f32[64,8,128]{2,1,0:T(8,128)S(1)}, f32[64,8,128]{2,1,0:T(8,128)S(1)}, u32[]{:S(2)}, u32[]{:S(2)}) %collective-permute-start.3) | collective-permute-done | bytes 262176 | tf_op jit(solution)/shard_map/ppermute | solution.py:287
  69.6 2.2 %shard_map.147 = (f32[64,8,128]{2,1,0:T(8,128)}, f32[64,8,128]{2,1,0:T(8,128)}, f32[8,16,8,128]{3,2,1,0:T(8,128)S(1)}) custom-call(s32[8,8]{1,0:T(8,128)S(1)} %copy-done.9, f32[8,4]{1,0:T(8,128)S(1)} %copy.22.wavelet, s32[8]{0:T(128)S(1)} %copy-done.10, s32[8]{0:T(128)S(1)} %copy-done.11, s32[8]{0:T(128)S(1)} %copy-done.12, s32[8]{0:T(128)S(1)} %copy-done.13, ...), custom_call_target="tpu_custom_call" | custom-call | flops 3932160 | bytes 2621440 | tf_op jit(solution)/shard_map/pallas_call | solution.py:23
  71.9 12.7 %all_to_all.10.got = f32[8,16,8,128]{3,2,1,0:T(8,128)S(1)} all-to-all(f32[8,16,8,128]{3,2,1,0:T(8,128)S(1)} %get-tuple-element.54), channel_id=1, replica_groups=mesh['shot'=8,'slab'=64] {'shot'}, dimensions={0} | all-to-all | bytes 1048576 | tf_op jit(solution)/shard_map/all_to_all | solution.py:335
  84.6 1.7 %shard_map.148 = f32[64,8,128]{2,1,0:T(8,128)} custom-call(s32[8,8]{1,0:T(8,128)S(1)} %copy-done.9, f32[8,16,8,128]{3,2,1,0:T(8,128)S(1)} %all_to_all.10.got), custom_call_target="tpu_custom_call" | custom-call | tf_op jit(solution)/shard_map/pallas_call | solution.py:23
  (25 shorter events, 0.1 us)
Async XLA Ops:
  0.6 1.0 %copy-start = (f32[1,64,8,128]{3,2,1,0:T(8,128)S(1)}, f32[1,64,8,128]{3,2,1,0:T(8,128)}, u32[]{:S(2)}) copy-start(f32[1,64,8,128]{3,2,1,0:T(8,128)} %param.13) | copy-start | bytes 786436
  1.6 0.9 %copy-start.2 = (f32[1,64,8,128]{3,2,1,0:T(8,128)S(1)}, f32[1,64,8,128]{3,2,1,0:T(8,128)}, u32[]{:S(2)}) copy-start(f32[1,64,8,128]{3,2,1,0:T(8,128)} %param.14) | copy-start | bytes 786436
  2.5 0.9 %copy-start.5 = (f32[64,8,128]{2,1,0:T(8,128)S(1)}, f32[64,8,128]{2,1,0:T(8,128)}, u32[]{:S(2)}) copy-start(f32[64,8,128]{2,1,0:T(8,128)} %vel.1) | copy-start | bytes 786436
  3.5 0.7 copy-start.8
  6.0 15.8 %copy-start.14 = (f32[8,4]{0,1:T(4,128)S(1)}, f32[8,4]{0,1:T(4,128)}, u32[]{:S(2)}) copy-start(f32[8,4]{0,1:T(4,128)} %param.18) | copy-start | bytes 388
  6.0 15.9 %copy-start.1 = (f32[1,64,8,128]{3,2,1,0:T(8,128)S(1)}, f32[1,64,8,128]{3,2,1,0:T(8,128)}, u32[]{:S(2)}) copy-start(f32[1,64,8,128]{3,2,1,0:T(8,128)} %param.13) | copy-start | bytes 786436
  6.0 15.9 %copy-start.3 = (f32[1,64,8,128]{3,2,1,0:T(8,128)S(1)}, f32[1,64,8,128]{3,2,1,0:T(8,128)}, u32[]{:S(2)}) copy-start(f32[1,64,8,128]{3,2,1,0:T(8,128)} %param.14) | copy-start | bytes 786436
  6.0 20.5 %all-to-all-start = ((f32[8,16,8,128]{3,2,1,0:T(8,128)}), f32[8,16,8,128]{3,2,1,0:T(8,128)S(1)}, u32[]{:S(2)}, u32[]{:S(2)}) async-start(f32[8,16,8,128]{3,2,1,0:T(8,128)} %get-tuple-element.34), calls=%async_computation | async-start | bytes 1048576 | tf_op jit(solution)/shard_map/all_to_all | solution.py:299
  11.1 15.3 %collective-permute-start = (f32[64,8,128]{2,1,0:T(8,128)S(1)}, f32[64,8,128]{2,1,0:T(8,128)S(1)}, u32[]{:S(2)}, u32[]{:S(2)}) collective-permute-start(f32[64,8,128]{2,1,0:T(8,128)S(1)} %get-tuple-element.30), channel_id=1, source_target_pairs={{1,2},{2,1},{3,4},{4,3},{5,6},{6,5},{7,8},{8,7},{9,10},{10,9},{11,... | collective-permute-start | bytes 786440 | tf_op jit(solution)/shard_map/ppermute | solution.py:287
  24.1 2.4 %copy-start.4 = (bf16[1,4,64,128]{3,2,1,0:T(8,128)(2,1)S(1)}, bf16[1,4,64,128]{3,2,1,0:T(8,128)(2,1)}, u32[]{:S(2)}) copy-start(bf16[1,4,64,128]{3,2,1,0:T(8,128)(2,1)} %param.23) | copy-start | bytes 196612
  24.1 2.4 %copy-start.6 = (f32[1,64,8,128]{3,2,1,0:T(8,128)S(1)}, f32[1,64,8,128]{3,2,1,0:T(8,128)}, u32[]{:S(2)}) copy-start(f32[1,64,8,128]{3,2,1,0:T(8,128)} %param.12) | copy-start | bytes 786436
  24.1 2.4 %copy-start.7 = (f32[1,64,8,128]{3,2,1,0:T(8,128)S(1)}, f32[1,64,8,128]{3,2,1,0:T(8,128)}, u32[]{:S(2)}) copy-start(f32[1,64,8,128]{3,2,1,0:T(8,128)} %param.15) | copy-start | bytes 786436
  24.1 2.4 %copy-start.13 = (s32[8]{0:T(128)S(1)}, s32[8]{0:T(128)}, u32[]{:S(2)}) copy-start(s32[8]{0:T(128)} %depth.7) | copy-start | bytes 100
  26.5 0.7 copy-start.9
  26.5 0.7 copy-start.10
  26.5 0.7 copy-start.11
  26.5 0.7 copy-start.12
  28.7 13.3 %collective-permute-start.1 = (f32[64,8,128]{2,1,0:T(8,128)S(1)}, f32[64,8,128]{2,1,0:T(8,128)S(1)}, u32[]{:S(2)}, u32[]{:S(2)}) collective-permute-start(f32[64,8,128]{2,1,0:T(8,128)S(1)} %get-tuple-element.35), channel_id=1, source_target_pairs={{1,2},{2,1},{3,4},{4,3},{5,6},{6,5},{7,8},{8,7},{9,10},{10,9},{11,... | collective-permute-start | bytes 786440 | tf_op jit(solution)/shard_map/ppermute | solution.py:287
  43.5 11.3 %collective-permute-start.2 = (f32[64,8,128]{2,1,0:T(8,128)S(1)}, f32[64,8,128]{2,1,0:T(8,128)S(1)}, u32[]{:S(2)}, u32[]{:S(2)}) collective-permute-start(f32[64,8,128]{2,1,0:T(8,128)S(1)} %get-tuple-element.42), channel_id=1, source_target_pairs={{1,2},{2,1},{3,4},{4,3},{5,6},{6,5},{7,8},{8,7},{9,10},{10,9},{11,... | collective-permute-start | bytes 786440 | tf_op jit(solution)/shard_map/ppermute | solution.py:287
  56.2 13.4 %collective-permute-start.3 = (f32[64,8,128]{2,1,0:T(8,128)S(1)}, f32[64,8,128]{2,1,0:T(8,128)S(1)}, u32[]{:S(2)}, u32[]{:S(2)}) collective-permute-start(f32[64,8,128]{2,1,0:T(8,128)S(1)} %get-tuple-element.48), channel_id=1, source_target_pairs={{1,2},{2,1},{3,4},{4,3},{5,6},{6,5},{7,8},{8,7},{9,10},{10,9},{11,... | collective-permute-start | bytes 786440 | tf_op jit(solution)/shard_map/ppermute | solution.py:287

commit v2 on v0

v2 whole, which is shorter than its diff:
```python
import jax
import jax.numpy as jnp
from jax import lax
from jax.experimental import pallas as pl
from jax.experimental.pallas import tpu as pltpu
from jax.sharding import PartitionSpec as P

BX = 8
KT = 8
STEPS = 4
CAP = 2
REACH = 4
CHUNK = 8
VMEM = pltpu.VMEM
SMEM = pltpu.SMEM


SCALE = 5040.0
TAPS = (-43050.0, 8064.0, -1008.0, 128.0, -9.0)
WHOLE = 16


def call(body, outs, in_spaces, *args, scratch=(), flops=0, bytes_accessed=0):
    outs = [o if isinstance(o, tuple) and isinstance(o[0], tuple) else (o, VMEM) for o in outs]
    outs = [o if len(o) == 3 else o + (jnp.float32,) for o in outs]
    return pl.pallas_call(
        body,
        out_shape=[jax.ShapeDtypeStruct(s, t) for s, _, t in outs],
        in_specs=[pl.BlockSpec(memory_space=s) for s in in_spaces],
        out_specs=[pl.BlockSpec(memory_space=m) for _, m, _ in outs],
        scratch_shapes=list(scratch),
        compiler_params=pltpu.CompilerParams(vmem_limit_bytes=24 * 1024 * 1024),
        cost_estimate=pl.CostEstimate(
            flops=flops, bytes_accessed=bytes_accessed, transcendentals=0
        ),
    )(*args)


def rows_of(shape):
    return lax.broadcasted_iota(jnp.int32, shape, len(shape) - 2)


def pack_pairs(field, low_ref, high_ref, at, odd):
    pairs = field.reshape(field.shape[0] // 2, 2, 8, field.shape[2])
    first, second = pairs[:, 0], pairs[:, 1]
    top = rows_of(first.shape) < REACH
    low = jnp.where(top, first, pltpu.roll(second, REACH, 1))
    high = jnp.where(top, pltpu.roll(first, REACH, 1), second)
    low_ref[at] = jnp.where(odd, high, low)
    high_ref[at] = jnp.where(odd, low, high)


def pack_kernel(
    tiles_in, vel_in, src_in, rec_in, send, to_far, to_near, src, rec, tiles_out, vel, tiles, sems
):
    shot = lax.axis_index("shot")
    odd = lax.rem(lax.axis_index("slab"), 2) == 1
    moves = ((src_in, src), (rec_in, rec), (tiles_in, tiles), (tiles_in, tiles_out), (vel_in, vel))
    copies = [pltpu.make_async_copy(a, b, sems.at[i]) for i, (a, b) in enumerate(moves)]
    for copy in copies:
        copy.start()
    half = src.shape[0] // 2
    for f, field in enumerate((src, rec)):
        copies[f].wait()

        def one_chunk(c, _):
            at = pl.ds(f * half + c * (CHUNK // 2), CHUNK // 2)
            pack_pairs(field[pl.ds(c * CHUNK, CHUNK)], to_far, to_near, at, odd)
            return 0

        lax.fori_loop(0, field.shape[0] // CHUNK, one_chunk, 0)
    for copy in copies[2:]:
        copy.wait()
    n_shot = send.shape[0]

    def one_shot(g, _):
        before = jnp.int32(0)
        for k in range(KT):
            before += (tiles[g, k] < shot * BX).astype(jnp.int32)
        for j in range(CAP):
            k = jnp.minimum(before + j, KT - 1)
            own = jnp.clip(tiles[g, k] - shot * BX, 0, vel.shape[0] // BX - 1)
            send[g, pl.ds(j * BX, BX)] = vel[pl.ds(own * BX, BX)]
        return 0

    lax.fori_loop(0, n_shot, one_shot, 0)


def tap_of(reach):
    weight = jnp.zeros(reach.shape, jnp.float32)
    for r in range(1, REACH + 1):
        weight = jnp.where(reach == r, TAPS[r], weight)
    return weight


def split(values, axis):
    high = values.astype(jnp.bfloat16)
    low = (values - high.astype(jnp.float32)).astype(jnp.bfloat16)
    return jnp.concatenate([high, low], axis=axis)


def along_y_matrix(size_y):
    shape = (2 * size_y, size_y)
    row = lax.rem(lax.broadcasted_iota(jnp.int32, shape, 0), size_y)
    return tap_of(jnp.abs(row - lax.broadcasted_iota(jnp.int32, shape, 1))).astype(jnp.bfloat16)


def halo_matrix(size_z, odd):
    rows, packed = WHOLE * size_z, WHOLE * REACH
    shape = (rows, 2 * packed)
    out = lax.broadcasted_iota(jnp.int32, shape, 0)
    at = lax.broadcasted_iota(jnp.int32, shape, 1)
    x, z = out // size_z, lax.rem(out, size_z)
    inner = lax.rem(at, packed)
    x_at, plane = inner // REACH, lax.rem(inner, REACH)
    left = (at < packed) != odd
    reach = jnp.where(left, z + REACH - plane, size_z + plane - z)
    weight = jnp.where(x == x_at, tap_of(reach), 0.0).astype(jnp.bfloat16)
    return jnp.concatenate([weight, weight], axis=1)


def around(field, base):
    size_x = field.shape[0]
    low, high = max(base - REACH, 0), min(base + WHOLE + REACH, size_x)
    wide = field[pl.ds(low, high - low)]
    zeros = jnp.zeros((REACH,) + field.shape[1:], jnp.float32)
    if base - REACH < 0:
        wide = jnp.concatenate([zeros, wide], axis=0)
    if base + WHOLE + REACH > size_x:
        wide = jnp.concatenate([wide, zeros], axis=0)
    return wide


def flat_sums(wide, to_y):
    centre = wide[REACH : REACH + WHOLE]
    lines = split(centre.reshape(-1, centre.shape[2]), 1)
    total = jnp.dot(lines, to_y, preferred_element_type=jnp.float32)
    total = total.reshape(centre.shape) + TAPS[0] * centre
    for r in range(1, REACH + 1):
        terms = wide[REACH + r : REACH + r + WHOLE] + wide[REACH - r : REACH - r + WHOLE]
        total += TAPS[r] * terms
    return total, centre


def up_down(up, down, r):
    size_z = up.shape[1]
    return pltpu.roll(up, size_z - r, 1) + pltpu.roll(down, r, 1)


def own_depth_sums(own, halo):
    size_z = own.shape[1]
    row = rows_of((1,) + own.shape[1:])
    total = 0.0
    for r in range(1, REACH + 1):
        up = jnp.where(row < r, halo, own)
        down = jnp.where(row >= size_z - r, halo, own)
        total += TAPS[r] * up_down(up, down, r)
    return total


def halo_depth_sums(own, halo, outer):
    size_z = own.shape[1]
    row = rows_of((1,) + own.shape[1:])
    top = row < REACH
    above, below = jnp.where(top, own, outer), jnp.where(top, outer, own)
    total = 0.0
    for r in range(1, REACH + 1):
        up_same = (lax.rem(row + size_z - r, size_z) < REACH) == top
        down_same = (lax.rem(row + r, size_z) < REACH) == top
        up, down = jnp.where(up_same, halo, above), jnp.where(down_same, halo, below)
        total += TAPS[r] * up_down(up, down, r)
    return total


def inner_sums(field, base, to_y):
    total, centre = flat_sums(around(field, base), to_y)
    return total + own_depth_sums(centre, jnp.zeros((1,) + centre.shape[1:], jnp.float32)), centre


def unpack_pairs(left, right):
    top = rows_of((1,) + left.shape[1:]) < REACH
    even_x = jnp.where(top, right, pltpu.roll(left, REACH, 1))
    odd_x = jnp.where(top, pltpu.roll(right, REACH, 1), left)
    pairs = jnp.stack([even_x, odd_x], axis=1)
    return pairs.reshape((2 * left.shape[0],) + left.shape[1:])


def add_sources(step, new, spots, plane_rows, slab, shot, halo=None):
    wavelet, spot_x, spot_z, spot_y, depth, traces = spots
    src_new, rec_new = new
    size_x, size_z, size_y = src_new.shape
    row = lax.broadcasted_iota(jnp.int32, (size_z, size_y), 0)
    lane = lax.broadcasted_iota(jnp.int32, (size_z, size_y), 1)
    reach = 0 if halo is None else REACH
    local_spot = spot_z[shot] - slab * size_z
    local_plane = depth[shot] - slab * size_z
    at_spot = lax.rem(local_spot + size_z, size_z)
    at_plane = lax.rem(local_plane + size_z, size_z)

    def add_spot(field):
        x = spot_x[shot]
        here = (row == at_spot) & (lane == spot_y[shot])
        field[x] += jnp.where(here, wavelet[shot, step], 0.0)

    def add_plane(field):
        plane_rows[...] = traces[STEPS - 1 - step].astype(jnp.float32)

        def one_x(x, _):
            line = plane_rows[pl.ds(x, 1)]
            field[x] += jnp.where(row == at_plane, line, 0.0)
            return 0

        lax.fori_loop(0, size_x, one_x, 0, unroll=8)

    def inside(at, edge):
        return (at >= -edge) & (at < size_z + edge)

    pl.when(inside(local_spot, 0))(lambda: add_spot(src_new))
    pl.when(inside(local_plane, 0))(lambda: add_plane(rec_new))
    if halo is not None:
        here = inside(local_spot, reach) & jnp.logical_not(inside(local_spot, 0))
        pl.when(here)(lambda: add_spot(halo[0]))
        here = inside(local_plane, reach) & jnp.logical_not(inside(local_plane, 0))
        pl.when(here)(lambda: add_plane(halo[1]))


def first_interior_kernel(src, src_old, rec, rec_old, src_lap, src_base, rec_lap, rec_base, halo_mat):
    odd = lax.rem(lax.axis_index("slab"), 2) == 1
    to_y = along_y_matrix(src.shape[2])
    halo_mat[...] = halo_matrix(src.shape[1], odd)
    for now, old, lap, out in (
        (src, src_old, src_lap, src_base),
        (rec, rec_old, rec_lap, rec_base),
    ):
        for base in range(0, src.shape[0], WHOLE):
            at = pl.ds(base, WHOLE)
            total, centre = inner_sums(now, base, to_y)
            lap[at] = total
            out[at] = 2.0 * centre - old[at]


def wide_interior_kernel(now, src_old, rec_old, rate, far, near, base, old_halo):
    odd = lax.rem(lax.axis_index("slab"), 2) == 1
    mine = jnp.where(odd, 0, 1)
    size_x = src_old.shape[0]
    to_y = along_y_matrix(src_old.shape[2])
    for f, old in enumerate((src_old, rec_old)):
        for start in range(0, size_x, WHOLE):
            at, own = pl.ds(f * size_x + start, WHOLE), pl.ds(start, WHOLE)
            total, centre = flat_sums(around(now.at[pl.ds(f * size_x, size_x)], start), to_y)
            base[at] = 2.0 * centre - old[own] + rate[own] * total
            packed = pl.ds((f * size_x + start) // 2, WHOLE // 2)
            from_far, from_near = far[packed], near[mine, packed]
            left = jnp.where(odd, from_near, from_far)
            right = jnp.where(odd, from_far, from_near)
            old_halo[at] = unpack_pairs(left, right)


def interior_kernel(now, src_old, rec_old, older, rate, base, partial):
    size_x = src_old.shape[0]
    to_y = along_y_matrix(src_old.shape[2])
    for f, old in enumerate((src_old, rec_old)):
        field = now.at[pl.ds(f * size_x, size_x)]
        for start in range(0, size_x, WHOLE):
            at, own = pl.ds(f * size_x + start, WHOLE), pl.ds(start, WHOLE)
            total, centre = inner_sums(field, start, to_y)
            base[at] = 2.0 * centre - old[own] + rate[own] * total
    for start in range(0, size_x, WHOLE):
        at, other = pl.ds(start, WHOLE), pl.ds(size_x + start, WHOLE)
        partial[at] = now[at] * older[other] + src_old[at] * rec_old[at] + older[at] * now[other]


def place_of(tiles, shot, k):
    owner = lax.shift_right_logical(tiles[shot, k], 3)
    before = lax.shift_right_logical(tiles[shot, max(k - 1, 0)], 3)
    slot = (before == owner).astype(jnp.int32) if k else jnp.int32(0)
    return owner, pl.ds(slot * BX, BX)


def halo_sums(f, start, far, near, mine, halo_mat, shape):
    size_x, size_z, size_y = shape
    span = WHOLE // 2
    groups = []
    for g in range(2):
        at = pl.ds((f * size_x + start) // 2 + g * span, span)
        both = jnp.concatenate([far[at], near[mine, at]], axis=0)
        groups.append(both.reshape(2 * span * size_z, size_y))
    lines = split(jnp.concatenate(groups, axis=1), 0)
    sums = jnp.dot(halo_mat[...], lines, preferred_element_type=jnp.float32)
    halves = [sums[:, g * size_y : (g + 1) * size_y] for g in range(2)]
    return jnp.concatenate([h.reshape(WHOLE, size_z, size_y) for h in halves], axis=0)


def first_kernel(
    tiles, wavelet, spot_x, spot_z, spot_y, depth, traces, far, near, halo_mat,
    src_base, rec_base, src_lap, rec_lap, vel_got,
    rate, to_far, to_near, plane_rows,
):
    shot, slab = lax.axis_index("shot"), lax.axis_index("slab")
    odd = lax.rem(slab, 2) == 1
    mine = jnp.where(odd, 0, 1)
    shape = src_base.shape
    size_x = shape[0]
    for k in range(KT):
        owner, at = place_of(tiles, shot, k)
        block = vel_got[owner, at]
        rate[pl.ds(k * BX, BX)] = block * block * (1.0 / SCALE)
    for f, (base, lap) in enumerate(((src_base, src_lap), (rec_base, rec_lap))):
        for start in range(0, size_x, 2 * WHOLE):
            at = pl.ds(start, 2 * WHOLE)
            total = lap[at] + halo_sums(f, start, far, near, mine, halo_mat, shape)
            to_far[pl.ds(f * size_x + start, 2 * WHOLE)] = base[at] + rate[at] * total
    new = [to_far.at[pl.ds(f * size_x, size_x)] for f in range(2)]
    spots = (wavelet, spot_x, spot_z, spot_y, depth, traces)
    add_sources(0, new, spots, plane_rows, slab, shot)
    to_near[pl.ds(0, 2 * size_x)] = to_far[pl.ds(0, 2 * size_x)]
    for start in range(0, size_x, WHOLE):
        packed = pl.ds(2 * size_x + start // 2, WHOLE // 2)
        pack_pairs(rate[pl.ds(start, WHOLE)], to_far, to_near, packed, odd)


def wide_kernel(
    wavelet, spot_x, spot_z, spot_y, depth, traces, far, near, now, base, old_halo, rate,
    src_mid, rec_mid, new, to_far, to_near, halo_now, halo_mid, plane_rows,
):
    shot, slab = lax.axis_index("shot"), lax.axis_index("slab")
    odd = lax.rem(slab, 2) == 1
    size_x, size_z, size_y = src_mid.shape
    to_y = along_y_matrix(size_y)
    from_near = (rows_of((1, size_z, size_y)) < REACH) != odd
    for start in range(0, 2 * size_x, WHOLE):
        at = pl.ds(start, WHOLE)
        halo_now[at] = jnp.where(from_near, near[at], far[at])
    for f, mid in enumerate((src_mid, rec_mid)):
        halo_field = halo_now.at[pl.ds(f * size_x, size_x)]
        for start in range(0, size_x, WHOLE):
            at, own_at = pl.ds(f * size_x + start, WHOLE), pl.ds(start, WHOLE)
            total, halo = flat_sums(around(halo_field, start), to_y)
            own = now[at]
            mid[own_at] = base[at] + rate[own_at] * own_depth_sums(own, halo)
            outer = jnp.where(from_near, far[at], near[at])
            total += halo_depth_sums(own, halo, outer)
            packed = pl.ds(2 * size_x + start // 2, WHOLE // 2)
            rate_far, rate_near = far[packed], near[packed]
            left = jnp.where(odd, rate_near, rate_far)
            right = jnp.where(odd, rate_far, rate_near)
            halo_mid[at] = 2.0 * halo - old_halo[at] + unpack_pairs(left, right) * total
    spots = (wavelet, spot_x, spot_z, spot_y, depth, traces)
    halves = [halo_mid.at[pl.ds(f * size_x, size_x)] for f in range(2)]
    add_sources(1, (src_mid, rec_mid), spots, plane_rows, slab, shot, halves)
    for f, mid in enumerate((src_mid, rec_mid)):
        for start in range(0, size_x, WHOLE):
            at, own_at = pl.ds(f * size_x + start, WHOLE), pl.ds(start, WHOLE)
            total, centre = flat_sums(around(mid, start), to_y)
            total += own_depth_sums(centre, halo_mid[at])
            new[at] = 2.0 * centre - now[at] + rate[own_at] * total
    fields = [new.at[pl.ds(f * size_x, size_x)] for f in range(2)]
    add_sources(2, fields, spots, plane_rows, slab, shot)
    for start in range(0, 2 * size_x, WHOLE):
        packed = pl.ds(start // 2, WHOLE // 2)
        pack_pairs(new[pl.ds(start, WHOLE)], to_far, to_near, packed, odd)


def last_kernel(
    tiles, wavelet, spot_x, spot_z, spot_y, depth, traces, far, near, halo_mat,
    base, rate, partial, src_first, rec_first,
    src_new, rec_new, send, plane_rows,
):
    shot, slab = lax.axis_index("shot"), lax.axis_index("slab")
    mine = jnp.where(lax.rem(slab, 2) == 1, 0, 1)
    shape = src_new.shape
    size_x = shape[0]
    for f, new in enumerate((src_new, rec_new)):
        for start in range(0, size_x, 2 * WHOLE):
            at = pl.ds(start, 2 * WHOLE)
            total = halo_sums(f, start, far, near, mine, halo_mat, shape)
            new[at] = base[pl.ds(f * size_x + start, 2 * WHOLE)] + rate[at] * total
    spots = (wavelet, spot_x, spot_z, spot_y, depth, traces)
    add_sources(STEPS - 1, (src_new, rec_new), spots, plane_rows, slab, shot)
    send[...] = jnp.zeros(send.shape, jnp.float32)
    for k in range(KT):
        owner, slot = place_of(tiles, shot, k)
        at = pl.ds(k * BX, BX)
        image = partial[at] + src_new[at] * rec_first[at] + src_first[at] * rec_new[at]
        send[owner, slot] = image


def gather_kernel(tiles, got, src, rec, out, src_out, rec_out, total, sems):
    shot = lax.axis_index("shot")
    copies = [
        pltpu.make_async_copy(src, src_out, sems.at[0]),
        pltpu.make_async_copy(rec, rec_out, sems.at[1]),
    ]
    for copy in copies:
        copy.start()
    total[...] = jnp.zeros(total.shape, jnp.float32)
    for g in range(got.shape[0]):
        before = jnp.int32(0)
        for k in range(KT):
            before += (tiles[g, k] < shot * BX).astype(jnp.int32)
        for j in range(CAP):
            k = jnp.minimum(before + j, KT - 1)
            own = jnp.clip(tiles[g, k] - shot * BX, 0, total.shape[0] // BX - 1)
            total[pl.ds(own * BX, BX)] += got[g, pl.ds(j * BX, BX)]
    copies.append(pltpu.make_async_copy(total, out, sems.at[2]))
    copies[2].start()
    for copy in copies:
        copy.wait()


def local(
    src_prev,
    src_cur,
    rec_cur,
    rec_next,
    velocity,
    aperture_tiles,
    wavelet,
    src_x,
    src_z,
    src_y,
    rec_depth,
    rec_data,
):
    slabs = lax.axis_size("slab")
    shots = lax.axis_size("shot")
    far_pairs = []
    for i in range(1, slabs - 1, 2):
        far_pairs += [(i, i + 1), (i + 1, i)]
    near_groups = [[i, i + 1] for i in range(0, slabs, 2)]
    near_pairs = [(i, i ^ 1) for i in range(slabs)]

    def exchange(to_far, to_near):
        far = lax.ppermute(to_far, "slab", far_pairs)
        near = lax.all_gather(to_near, "slab", axis_index_groups=near_groups)
        return far, near

    src_old, rec_old = src_prev[0], rec_next[0]
    block = src_old.shape
    both = (2 * block[0],) + block[1:]
    wide = (2 * block[0] + block[0] // 2,) + block[1:]
    buffer = (shots, CAP * BX) + block[1:]
    dma = pltpu.SemaphoreType.DMA
    rows = VMEM((block[0], block[2]), jnp.float32)
    cost = dict(flops=2 * 45 * src_old.size, bytes_accessed=8 * 4 * src_old.size)
    given = (aperture_tiles, velocity, src_cur[0], rec_cur[0])
    send, to_far, to_near, src, rec, tiles = call(
        pack_kernel,
        [buffer, block, block, block, block, (aperture_tiles.shape, VMEM, jnp.int32)],
        [pltpu.HBM] * 4, *[pltpu.with_memory_space_constraint(a, pltpu.HBM) for a in given],
        scratch=[
            VMEM(velocity.shape, jnp.float32),
            SMEM(aperture_tiles.shape, jnp.int32),
            dma((5,)),
        ],
    )
    spots = (wavelet, src_x, src_z, src_y, rec_depth, rec_data[0])

    vel_got = lax.all_to_all(send, "shot", 0, 0)
    far, near = exchange(to_far, to_near)
    src_lap, src_base, rec_lap, rec_base, halo_mat = call(
        first_interior_kernel,
        [block] * 4 + [((WHOLE * block[1], 4 * WHOLE * REACH), VMEM, jnp.bfloat16)],
        [VMEM] * 4, src, src_old, rec, rec_old, **cost,
    )
    rate, now, now_near = call(
        first_kernel, [block, wide, wide], [SMEM] * 6 + [VMEM] * 9,
        tiles, *spots, far, near, halo_mat, src_base, rec_base, src_lap, rec_lap, vel_got,
        scratch=[rows], **cost,
    )

    wide_far = lax.ppermute(now, "slab", far_pairs)
    wide_near = lax.ppermute(now_near, "slab", near_pairs)
    base, old_halo = call(
        wide_interior_kernel, [both] * 2, [VMEM] * 6, now, src, rec, rate, far, near, **cost
    )
    src_mid, rec_mid, new, to_far, to_near = call(
        wide_kernel, [block, block, both, block, block], [SMEM] * 5 + [VMEM] * 7,
        *spots, wide_far, wide_near, now, base, old_halo, rate,
        scratch=[VMEM(both, jnp.float32), VMEM(both, jnp.float32), rows], **cost,
    )

    far, near = exchange(to_far, to_near)
    base, partial = call(
        interior_kernel, [both, block], [VMEM] * 5, new, src_mid, rec_mid, now, rate, **cost
    )
    src, rec, send = call(
        last_kernel, [block, block, buffer], [SMEM] * 6 + [VMEM] * 9,
        tiles, *spots, far, near, halo_mat, base, rate, partial, src, rec,
        scratch=[rows], **cost,
    )
    image_got = lax.all_to_all(send, "shot", 0, 0)
    image, src, rec = call(
        gather_kernel,
        [(velocity.shape, pltpu.HBM), (block, pltpu.HBM), (block, pltpu.HBM)],
        [SMEM] + [VMEM] * 3, tiles, image_got, src, rec,
        scratch=[VMEM(velocity.shape, jnp.float32), dma((3,))],
    )
    return image, src[None], rec[None]


def solution(mesh):
    wave = P("shot", None, "slab", None)
    model = P("shot", "slab", None)
    return jax.shard_map(
        local,
        mesh=mesh,
        in_specs=(wave,) * 4 + (model,) + (P(),) * 6 + (P("shot", None, None, None),),
        out_specs=(model, wave, wave),
        check_vma=False,
    )
```

time: 201 us -> 76.2 us (0.38)
  the two profiles are of different devices: /device:TPU:32 before, /device:TPU:16 now
where the time goes in v2:
time: 76.2 us; the launch traced here: 75.8 us
  starting transfers between devices  34.4 us (45%)
  blocking collectives  16.8 us (22%)
  Pallas kernels  11.5 us (15%)
  waiting for transfers between devices  11.5 us (15%)
  between operations  0.79 us (1%)
  local copies, waits for them, and re-layouts  0.78 us (1%)
    ppermute x2, starting transfers between devices, exchange(): far = lax.ppermute(to_far, 'slab', far_pairs)  17.9 us
    all_to_all x1, blocking collectives, local(): image_got = lax.all_to_all(send, 'shot', 0, 0)  12.3 us
    pallas_call x8, Pallas kernels, call(): pl.pallas_call(body, out_shape=[jax.ShapeDtypeStruct(s, t) for s, _, t in...  11.5 us
    ppermute x1, starting transfers between devices, local(): wide_far = lax.ppermute(now, 'slab', far_pairs)  9.43 us
    ppermute x1, waiting for transfers between devices, local(): wide_far = lax.ppermute(now, 'slab', far_pairs)  7.69 us
    all_to_all x1, starting transfers between devices, local(): vel_got = lax.all_to_all(send, 'shot', 0, 0)  5.16 us
    all_gather x2, blocking collectives, exchange(): near = lax.all_gather(to_near, 'slab', axis_index_groups=near_groups)  4.49 us
    ppermute x2, waiting for transfers between devices, exchange(): far = lax.ppermute(to_far, 'slab', far_pairs)  3.8 us
  transfers between devices with their start and end apart: 5, of which 3 were waited for; matrix products, arithmetic and copies ran while one was open for 0% of the time, Pallas kernels for 3%

profile of v2, /device:TPU:16, one launch (start us, length us, event | category | flops | bytes accessed | tf_op | source)
XLA Modules:
  0.0 75.8 jit_solution(13089495819997425077)
XLA Ops:
  0.6 2.2 %shard_map.139 = (f32[8,16,8,128]{3,2,1,0:T(8,128)}, f32[64,8,128]{2,1,0:T(8,128)S(1)}, f32[64,8,128]{2,1,0:T(8,128)S(1)}, f32[64,8,128]{2,1,0:T(8,128)S(1)}, f3...) custom-call(s32[8,8]{1,0:T(8,128)} %tiles_in.1, f32[64,8,128]{2,1,0:T(8,128)} %vel_in.1, f32[64,8,128]{2,1,0:T(8,128)} %bitcast.17, ...), custom_call_target="tpu_custom_call" | custom-call | tf_op jit(solution)/shard_map/pallas_call | solution.py:26
  2.8 0.0 copy-start.7
  2.8 0.0 copy-start.1
  2.9 0.0 copy-start.2
  2.9 5.2 %all-to-all-start = ((f32[8,16,8,128]{3,2,1,0:T(8,128)}), f32[8,16,8,128]{3,2,1,0:T(8,128)S(1)}, u32[]{:S(2)}, u32[]{:S(2)}) async-start(f32[8,16,8,128]{3,2,1,0:T(8,128)} %get-tuple-element.42), calls=%async_computation | async-start | bytes 1048576 | tf_op jit(solution)/shard_map/all_to_all | solution.py:459
  8.0 10.6 %collective-permute-start = (f32[64,8,128]{2,1,0:T(8,128)S(1)}, f32[64,8,128]{2,1,0:T(8,128)S(1)}, u32[]{:S(2)}, u32[]{:S(2)}) collective-permute-start(f32[64,8,128]{2,1,0:T(8,128)S(1)} %get-tuple-element.33), channel_id=1, source_target_pairs={{1,2},{2,1},{3,4},{4,3},{5,6},{6,5},{7,8},{8,7},{9,10},{10,9},{11,... | collective-permute-start | bytes 786440 | tf_op jit(solution)/shard_map/ppermute | solution.py:434
  18.7 0.0 copy-done.7
  18.7 0.1 copy.20.wavelet
  18.7 0.0 copy-done.1
  18.7 0.9 %shard_map.140 = (f32[64,8,128]{2,1,0:T(8,128)S(1)}, f32[64,8,128]{2,1,0:T(8,128)S(1)}, f32[64,8,128]{2,1,0:T(8,128)S(1)}, f32[64,8,128]{2,1,0:T(8,128)S(1)}, bf16[128,256]{1,0:T(8,128)(2,1)S(1)}) custom-call(f32[64,8,128]{2,1,0:T(8,128)S(1)} %get-tuple-element.35.src.src_old.src_first, f32[64,8,128]{2,1,0:T(8,128)S(1)} %bitcast.15, ...), custom_call_target="tpu_custom_call" | custom-call | flops 5898240 | bytes 2097152 | tf_op jit(solution)/shard_map/pallas_call | solution.py:26
  19.7 0.0 copy-start
  19.7 0.0 copy-start.6
  19.7 2.3 %all-gather = f32[128,8,128]{2,1,0:T(8,128)S(1)} all-gather(f32[64,8,128]{2,1,0:T(8,128)S(1)} %get-tuple-element.34), channel_id=2, replica_groups={{0,1},{2,3},{4,5},{6,7},{8,9},{10,11},{12,13},{14,15},{16,17},{18,19},{..., dimensions={0}, use_global_device_ids=true | all-gather | bytes 786432 | tf_op jit(solution)/shard_map/all_gather | solution.py:435
  22.0 0.8 collective-permute-done.far
  22.8 0.0 all-to-all-done.vel_got
  22.8 0.6 copy-done.3
  23.4 0.0 copy-done.4
  23.5 0.0 copy-done.5
  23.5 1.0 %shard_map.141 = (f32[64,8,128]{2,1,0:T(8,128)S(1)}, f32[160,8,128]{2,1,0:T(8,128)S(1)}, f32[160,8,128]{2,1,0:T(8,128)S(1)}) custom-call(s32[8,8]{1,0:T(8,128)S(1)} %get-tuple-element.32.tiles, f32[8,4]{1,0:T(8,128)S(1)} %copy.20.wavelet, s32[8]{0:T(128)S(1)} %copy-done.3, s32[8]{0:T(128)S(1)} %copy-done.4, s32[8]{0:T(128)S(1)} %copy-done.5, ...), custom_call_target="tpu_custom_call" | custom-call | flops 5898240 | bytes 2097152 | tf_op jit(solution)/shard_map/pallas_call | solution.py:26
  24.5 1.9 %collective-permute-start.2 = (f32[160,8,128]{2,1,0:T(8,128)S(1)}, f32[160,8,128]{2,1,0:T(8,128)S(1)}, u32[]{:S(2)}, u32[]{:S(2)}) collective-permute-start(f32[160,8,128]{2,1,0:T(8,128)S(1)} %get-tuple-element.44), channel_id=1, source_target_pairs={{0,1},{1,0},{2,3},{3,2},{4,5},{5,4},{6,7},{7,6},{8,9},{9,8},{10,11... | collective-permute-start | bytes 1966088 | tf_op jit(solution)/shard_map/ppermute | solution.py:473
  26.4 9.4 %collective-permute-start.1 = (f32[160,8,128]{2,1,0:T(8,128)S(1)}, f32[160,8,128]{2,1,0:T(8,128)S(1)}, u32[]{:S(2)}, u32[]{:S(2)}) collective-permute-start(f32[160,8,128]{2,1,0:T(8,128)S(1)} %get-tuple-element.43.now.older), channel_id=1, source_target_pairs={{1,2},{2,1},{3,4},{4,3},{5,6},{6,5},{7,8},{8,7},{9,10},{10,9},{11,... | collective-permute-start | bytes 1966088 | tf_op jit(solution)/shard_map/ppermute | solution.py:472
  35.9 0.5 shard_map.142
  36.4 0.0 collective-permute-done.2.near
  36.4 7.7 %collective-permute-done.1.far = f32[160,8,128]{2,1,0:T(8,128)S(1)} collective-permute-done((f32[160,8,128]{2,1,0:T(8,128)S(1)}, f32[160,8,128]{2,1,0:T(8,128)S(1)}, u32[]{:S(2)}, u32[]{:S(2)}) %collective-permute-start.1) | collective-permute-done | bytes 655392 | tf_op jit(solution)/shard_map/ppermute | solution.py:472
  44.1 3.3 %shard_map.143 = (f32[64,8,128]{2,1,0:T(8,128)S(1)}, f32[64,8,128]{2,1,0:T(8,128)S(1)}, f32[128,8,128]{2,1,0:T(8,128)S(1)}, f32[64,8,128]{2,1,0:T(8,128)S(1)}, f32[64,8,128]{2,1,0:T(8,128)S(1)}) custom-call(f32[8,4]{1,0:T(8,128)S(1)} %copy.20.wavelet, s32[8]{0:T(128)S(1)} %copy-done.3, s32[8]{0:T(128)S(1)} %copy-done.4, s32[8]{0:T(128)S(1)} %copy-done.5, ...), custom_call_target="tpu_custom_call" | custom-call | flops 5898240 | bytes 2097152 | tf_op jit(solution)/shard_map/pallas_call | solution.py:26
  47.4 7.3 %collective-permute-start.3 = (f32[64,8,128]{2,1,0:T(8,128)S(1)}, f32[64,8,128]{2,1,0:T(8,128)S(1)}, u32[]{:S(2)}, u32[]{:S(2)}) collective-permute-start(f32[64,8,128]{2,1,0:T(8,128)S(1)} %get-tuple-element.48), channel_id=1, source_target_pairs={{1,2},{2,1},{3,4},{4,3},{5,6},{6,5},{7,8},{8,7},{9,10},{10,9},{11,... | collective-permute-start | bytes 786440 | tf_op jit(solution)/shard_map/ppermute | solution.py:434
  54.7 1.0 %shard_map.144 = (f32[128,8,128]{2,1,0:T(8,128)S(1)}, f32[64,8,128]{2,1,0:T(8,128)S(1)}) custom-call(f32[128,8,128]{2,1,0:T(8,128)S(1)} %get-tuple-element.50.now, f32[64,8,128]{2,1,0:T(8,128)S(1)} %get-tuple-element.51.src_old, f32[64,8,128]{2,1,0:T(8,128)S(1)} %get-tuple-element.52.rec_old, f32[160,8,128]{2,1,0:T(8,128)S(1)} %get-tuple-element.43.now.older, ...), custom_call_target="tpu_custom_call" | custom-call | flops 5898240 | bytes 2097152 | tf_op jit(solution)/shard_map/pallas_call | solution.py:26
  55.7 2.2 %all-gather.1 = f32[128,8,128]{2,1,0:T(8,128)S(1)} all-gather(f32[64,8,128]{2,1,0:T(8,128)S(1)} %get-tuple-element.49), channel_id=3, replica_groups={{0,1},{2,3},{4,5},{6,7},{8,9},{10,11},{12,13},{14,15},{16,17},{18,19},{..., dimensions={0}, use_global_device_ids=true | all-gather | bytes 786432 | tf_op jit(solution)/shard_map/all_gather | solution.py:435
  57.9 3.0 %collective-permute-done.3.far = f32[64,8,128]{2,1,0:T(8,128)S(1)} collective-permute-done((f32[64,8,128]{2,1,0:T(8,128)S(1)}, f32[64,8,128]{2,1,0:T(8,128)S(1)}, u32[]{:S(2)}, u32[]{:S(2)}) %collective-permute-start.3) | collective-permute-done | bytes 262176 | tf_op jit(solution)/shard_map/ppermute | solution.py:434
  60.9 1.0 %shard_map.145 = (f32[64,8,128]{2,1,0:T(8,128)S(1)}, f32[64,8,128]{2,1,0:T(8,128)S(1)}, f32[8,16,8,128]{3,2,1,0:T(8,128)S(1)}) custom-call(s32[8,8]{1,0:T(8,128)S(1)} %get-tuple-element.32.tiles, f32[8,4]{1,0:T(8,128)S(1)} %copy.20.wavelet, s32[8]{0:T(128)S(1)} %copy-done.3, s32[8]{0:T(128)S(1)} %copy-done.4, s32[8]{0:T(128)S(1)} %copy-done.5, ...), custom_call_target="tpu_custom_call" | custom-call | flops 5898240 | bytes 2097152 | tf_op jit(solution)/shard_map/pallas_call | solution.py:26
  62.0 12.3 %all_to_all.10.got = f32[8,16,8,128]{3,2,1,0:T(8,128)S(1)} all-to-all(f32[8,16,8,128]{3,2,1,0:T(8,128)S(1)} %get-tuple-element.55), channel_id=1, replica_groups=mesh['shot'=8,'slab'=64] {'shot'}, dimensions={0} | all-to-all | bytes 1048576 | tf_op jit(solution)/shard_map/all_to_all | solution.py:492
  74.3 1.5 %shard_map.146 = (f32[64,8,128]{2,1,0:T(8,128)}, f32[64,8,128]{2,1,0:T(8,128)}, f32[64,8,128]{2,1,0:T(8,128)}) custom-call(s32[8,8]{1,0:T(8,128)S(1)} %get-tuple-element.32.tiles, f32[8,16,8,128]{3,2,1,0:T(8,128)S(1)} %all_to_all.10.got, f32[64,8,128]{2,1,0:T(8,128)S(1)} %get-tuple-element.56.src, f32[64,8,128]{2,1,0:T(8,128)S(1)} %get-tuple-element.57.rec), custom_call_target="tpu_custom_call" | custom-call | tf_op jit(solution)/shard_map/pallas_call | solution.py:26
  (6 shorter events, 0.0 us)
Async XLA Ops:
  2.8 15.8 %copy-start.7 = (f32[8,4]{0,1:T(4,128)S(1)}, f32[8,4]{0,1:T(4,128)}, u32[]{:S(2)}) copy-start(f32[8,4]{0,1:T(4,128)} %param.18) | copy-start | bytes 388
  2.8 15.9 %copy-start.1 = (f32[1,64,8,128]{3,2,1,0:T(8,128)S(1)}, f32[1,64,8,128]{3,2,1,0:T(8,128)}, u32[]{:S(2)}) copy-start(f32[1,64,8,128]{3,2,1,0:T(8,128)} %param.12) | copy-start | bytes 786436
  2.9 15.9 %copy-start.2 = (f32[1,64,8,128]{3,2,1,0:T(8,128)S(1)}, f32[1,64,8,128]{3,2,1,0:T(8,128)}, u32[]{:S(2)}) copy-start(f32[1,64,8,128]{3,2,1,0:T(8,128)} %param.15) | copy-start | bytes 786436
  2.9 19.9 %all-to-all-start = ((f32[8,16,8,128]{3,2,1,0:T(8,128)}), f32[8,16,8,128]{3,2,1,0:T(8,128)S(1)}, u32[]{:S(2)}, u32[]{:S(2)}) async-start(f32[8,16,8,128]{3,2,1,0:T(8,128)} %get-tuple-element.42), calls=%async_computation | async-start | bytes 1048576 | tf_op jit(solution)/shard_map/all_to_all | solution.py:459
  8.0 14.8 %collective-permute-start = (f32[64,8,128]{2,1,0:T(8,128)S(1)}, f32[64,8,128]{2,1,0:T(8,128)S(1)}, u32[]{:S(2)}, u32[]{:S(2)}) collective-permute-start(f32[64,8,128]{2,1,0:T(8,128)S(1)} %get-tuple-element.33), channel_id=1, source_target_pairs={{1,2},{2,1},{3,4},{4,3},{5,6},{6,5},{7,8},{8,7},{9,10},{10,9},{11,... | collective-permute-start | bytes 786440 | tf_op jit(solution)/shard_map/ppermute | solution.py:434
  19.7 3.1 %copy-start = (bf16[1,4,64,128]{3,2,1,0:T(8,128)(2,1)S(1)}, bf16[1,4,64,128]{3,2,1,0:T(8,128)(2,1)}, u32[]{:S(2)}) copy-start(bf16[1,4,64,128]{3,2,1,0:T(8,128)(2,1)} %param.23) | copy-start | bytes 196612
  19.7 3.1 %copy-start.6 = (s32[8]{0:T(128)S(1)}, s32[8]{0:T(128)}, u32[]{:S(2)}) copy-start(s32[8]{0:T(128)} %depth.5) | copy-start | bytes 100
  22.8 0.7 copy-start.3
  22.8 0.7 copy-start.4
  22.8 0.7 copy-start.5
  24.5 11.9 %collective-permute-start.2 = (f32[160,8,128]{2,1,0:T(8,128)S(1)}, f32[160,8,128]{2,1,0:T(8,128)S(1)}, u32[]{:S(2)}, u32[]{:S(2)}) collective-permute-start(f32[160,8,128]{2,1,0:T(8,128)S(1)} %get-tuple-element.44), channel_id=1, source_target_pairs={{0,1},{1,0},{2,3},{3,2},{4,5},{5,4},{6,7},{7,6},{8,9},{9,8},{10,11... | collective-permute-start | bytes 1966088 | tf_op jit(solution)/shard_map/ppermute | solution.py:473
  26.4 17.7 %collective-permute-start.1 = (f32[160,8,128]{2,1,0:T(8,128)S(1)}, f32[160,8,128]{2,1,0:T(8,128)S(1)}, u32[]{:S(2)}, u32[]{:S(2)}) collective-permute-start(f32[160,8,128]{2,1,0:T(8,128)S(1)} %get-tuple-element.43.now.older), channel_id=1, source_target_pairs={{1,2},{2,1},{3,4},{4,3},{5,6},{6,5},{7,8},{8,7},{9,10},{10,9},{11,... | collective-permute-start | bytes 1966088 | tf_op jit(solution)/shard_map/ppermute | solution.py:472
  47.4 13.5 %collective-permute-start.3 = (f32[64,8,128]{2,1,0:T(8,128)S(1)}, f32[64,8,128]{2,1,0:T(8,128)S(1)}, u32[]{:S(2)}, u32[]{:S(2)}) collective-permute-start(f32[64,8,128]{2,1,0:T(8,128)S(1)} %get-tuple-element.48), channel_id=1, source_target_pairs={{1,2},{2,1},{3,4},{4,3},{5,6},{6,5},{7,8},{8,7},{9,10},{10,9},{11,... | collective-permute-start | bytes 786440 | tf_op jit(solution)/shard_map/ppermute | solution.py:434

commit v3 on v2

--- a/solution.py
+++ b/solution.py
@@ -40,22 +40,26 @@
     return lax.broadcasted_iota(jnp.int32, shape, len(shape) - 2)
 
 
-def pack_pairs(field, low_ref, high_ref, at, odd):
+def pack_pairs(field, to_far, to_near, at, odd):
     pairs = field.reshape(field.shape[0] // 2, 2, 8, field.shape[2])
     first, second = pairs[:, 0], pairs[:, 1]
     top = rows_of(first.shape) < REACH
     low = jnp.where(top, first, pltpu.roll(second, REACH, 1))
     high = jnp.where(top, pltpu.roll(first, REACH, 1), second)
-    low_ref[at] = jnp.where(odd, high, low)
-    high_ref[at] = jnp.where(odd, low, high)
+    if to_far is not None:
+        to_far[at] = jnp.where(odd, high, low)
+    if to_near is not None:
+        to_near[at] = jnp.where(odd, low, high)
 
 
 def pack_kernel(
-    tiles_in, vel_in, src_in, rec_in, send, to_far, to_near, src, rec, tiles_out, vel, tiles, sems
+    tiles_in, vel_in, src_in, rec_in, x_in, z_in, y_in, depth_in,
+    send, to_far, to_near, src, rec, tiles_out, x_out, z_out, y_out, depth_out, vel, tiles, sems,
 ):
     shot = lax.axis_index("shot")
     odd = lax.rem(lax.axis_index("slab"), 2) == 1
-    moves = ((src_in, src), (rec_in, rec), (tiles_in, tiles), (tiles_in, tiles_out), (vel_in, vel))
+    moves = [(src_in, src), (rec_in, rec), (tiles_in, tiles), (tiles_in, tiles_out), (vel_in, vel)]
+    moves += [(x_in, x_out), (z_in, z_out), (y_in, y_out), (depth_in, depth_out)]
     copies = [pltpu.make_async_copy(a, b, sems.at[i]) for i, (a, b) in enumerate(moves)]
     for copy in copies:
         copy.start()
@@ -239,11 +243,15 @@
             out[at] = 2.0 * centre - old[at]
 
 
-def wide_interior_kernel(now, src_old, rec_old, rate, far, near, base, old_halo):
+def wide_interior_kernel(now, src_old, rec_old, rate, far, near, base, old_halo, to_near):
     odd = lax.rem(lax.axis_index("slab"), 2) == 1
     mine = jnp.where(odd, 0, 1)
     size_x = src_old.shape[0]
     to_y = along_y_matrix(src_old.shape[2])
+    to_near[pl.ds(0, 2 * size_x)] = now[pl.ds(0, 2 * size_x)]
+    for start in range(0, size_x, WHOLE):
+        packed = pl.ds(2 * size_x + start // 2, WHOLE // 2)
+        pack_pairs(rate[pl.ds(start, WHOLE)], None, to_near, packed, odd)
     for f, old in enumerate((src_old, rec_old)):
         for start in range(0, size_x, WHOLE):
             at, own = pl.ds(f * size_x + start, WHOLE), pl.ds(start, WHOLE)
@@ -294,7 +302,7 @@
 def first_kernel(
     tiles, wavelet, spot_x, spot_z, spot_y, depth, traces, far, near, halo_mat,
     src_base, rec_base, src_lap, rec_lap, vel_got,
-    rate, to_far, to_near, plane_rows,
+    rate, to_far, plane_rows,
 ):
     shot, slab = lax.axis_index("shot"), lax.axis_index("slab")
     odd = lax.rem(slab, 2) == 1
@@ -313,10 +321,9 @@
     new = [to_far.at[pl.ds(f * size_x, size_x)] for f in range(2)]
     spots = (wavelet, spot_x, spot_z, spot_y, depth, traces)
     add_sources(0, new, spots, plane_rows, slab, shot)
-    to_near[pl.ds(0, 2 * size_x)] = to_far[pl.ds(0, 2 * size_x)]
     for start in range(0, size_x, WHOLE):
         packed = pl.ds(2 * size_x + start // 2, WHOLE // 2)
-        pack_pairs(rate[pl.ds(start, WHOLE)], to_far, to_near, packed, odd)
+        pack_pairs(rate[pl.ds(start, WHOLE)], to_far, None, packed, odd)
 
 
 def wide_kernel(
@@ -443,18 +450,18 @@
     dma = pltpu.SemaphoreType.DMA
     rows = VMEM((block[0], block[2]), jnp.float32)
     cost = dict(flops=2 * 45 * src_old.size, bytes_accessed=8 * 4 * src_old.size)
-    given = (aperture_tiles, velocity, src_cur[0], rec_cur[0])
-    send, to_far, to_near, src, rec, tiles = call(
-        pack_kernel,
-        [buffer, block, block, block, block, (aperture_tiles.shape, VMEM, jnp.int32)],
-        [pltpu.HBM] * 4, *[pltpu.with_memory_space_constraint(a, pltpu.HBM) for a in given],
+    given = (aperture_tiles, velocity, src_cur[0], rec_cur[0], src_x, src_z, src_y, rec_depth)
+    whole_numbers = [(a.shape, VMEM, jnp.int32) for a in (aperture_tiles, *given[4:])]
+    send, to_far, to_near, src, rec, tiles, *places = call(
+        pack_kernel, [buffer, block, block, block, block] + whole_numbers,
+        [pltpu.HBM] * 8, *[pltpu.with_memory_space_constraint(a, pltpu.HBM) for a in given],
         scratch=[
             VMEM(velocity.shape, jnp.float32),
             SMEM(aperture_tiles.shape, jnp.int32),
-            dma((5,)),
+            dma((9,)),
         ],
     )
-    spots = (wavelet, src_x, src_z, src_y, rec_depth, rec_data[0])
+    spots = (wavelet, *places, rec_data[0])
 
     vel_got = lax.all_to_all(send, "shot", 0, 0)
     far, near = exchange(to_far, to_near)
@@ -463,17 +470,17 @@
         [block] * 4 + [((WHOLE * block[1], 4 * WHOLE * REACH), VMEM, jnp.bfloat16)],
         [VMEM] * 4, src, src_old, rec, rec_old, **cost,
     )
-    rate, now, now_near = call(
-        first_kernel, [block, wide, wide], [SMEM] * 6 + [VMEM] * 9,
+    rate, now = call(
+        first_kernel, [block, wide], [SMEM] * 6 + [VMEM] * 9,
         tiles, *spots, far, near, halo_mat, src_base, rec_base, src_lap, rec_lap, vel_got,
         scratch=[rows], **cost,
     )
 
     wide_far = lax.ppermute(now, "slab", far_pairs)
+    base, old_halo, now_near = call(
+        wide_interior_kernel, [both, both, wide], [VMEM] * 6, now, src, rec, rate, far, near, **cost
+    )
     wide_near = lax.ppermute(now_near, "slab", near_pairs)
-    base, old_halo = call(
-        wide_interior_kernel, [both] * 2, [VMEM] * 6, now, src, rec, rate, far, near, **cost
-    )
     src_mid, rec_mid, new, to_far, to_near = call(
         wide_kernel, [block, block, both, block, block], [SMEM] * 5 + [VMEM] * 7,
         *spots, wide_far, wide_near, now, base, old_halo, rate,

time: 76.2 us -> 73.4 us (0.963)
  waiting for transfers between devices: 11.5 us -> 9.38 us
    ppermute x1, waiting for transfers between devices: 7.69 us -> 5.75 us  [local(): wide_far = lax.ppermute(now, 'slab', far_pairs)]
where the time goes in v3:
time: 73.4 us; the launch traced here: 73 us
  starting transfers between devices  34.4 us (47%)
  blocking collectives  16.8 us (23%)
  Pallas kernels  11.6 us (16%)
  waiting for transfers between devices  9.38 us (13%)
  between operations  0.76 us (1%)
    ppermute x2, starting transfers between devices, exchange(): far = lax.ppermute(to_far, 'slab', far_pairs)  17.9 us
    all_to_all x1, blocking collectives, local(): image_got = lax.all_to_all(send, 'shot', 0, 0)  12.3 us
    pallas_call x8, Pallas kernels, call(): pl.pallas_call(body, out_shape=[jax.ShapeDtypeStruct(s, t) for s, _, t in...  11.6 us
    ppermute x1, starting transfers between devices, local(): wide_far = lax.ppermute(now, 'slab', far_pairs)  9.42 us
    ppermute x1, waiting for transfers between devices, local(): wide_far = lax.ppermute(now, 'slab', far_pairs)  5.75 us
    all_to_all x1, starting transfers between devices, local(): vel_got = lax.all_to_all(send, 'shot', 0, 0)  5.16 us
    all_gather x2, blocking collectives, exchange(): near = lax.all_gather(to_near, 'slab', axis_index_groups=near_groups)  4.49 us
    ppermute x2, waiting for transfers between devices, exchange(): far = lax.ppermute(to_far, 'slab', far_pairs)  3.62 us
  transfers between devices with their start and end apart: 5, of which 3 were waited for; matrix products, arithmetic and copies ran while one was open for 0% of the time, Pallas kernels for 3%

profile of v3, /device:TPU:16, one launch (start us, length us, event | category | flops | bytes accessed | tf_op | source)
XLA Modules:
  0.0 73.0 jit_solution(4653341997707014508)
XLA Ops:
  0.6 2.3 %shard_map.139 = (f32[8,16,8,128]{3,2,1,0:T(8,128)}, f32[64,8,128]{2,1,0:T(8,128)}, f32[64,8,128]{2,1,0:T(8,128)S(1)}, f32[64,8,128]{2,1,0:T(8,128)S(1)}, f32[64...) custom-call(s32[8,8]{1,0:T(8,128)} %tiles_in.1, ...), custom_call_target="tpu_custom_call" | custom-call | tf_op jit(solution)/shard_map/pallas_call | solution.py:26
  3.0 0.0 copy-start.3
  3.0 0.0 copy-start.1
  3.0 0.0 copy-start.2
  3.0 5.2 %all-to-all-start = ((f32[8,16,8,128]{3,2,1,0:T(8,128)}), f32[8,16,8,128]{3,2,1,0:T(8,128)S(1)}, u32[]{:S(2)}, u32[]{:S(2)}) async-start(f32[8,16,8,128]{3,2,1,0:T(8,128)} %get-tuple-element.50), calls=%async_computation | async-start | bytes 1048576 | tf_op jit(solution)/shard_map/all_to_all | solution.py:466
  8.2 10.6 %collective-permute-start = (f32[64,8,128]{2,1,0:T(8,128)}, f32[64,8,128]{2,1,0:T(8,128)S(1)}, u32[]{:S(2)}, u32[]{:S(2)}) collective-permute-start(f32[64,8,128]{2,1,0:T(8,128)} %get-tuple-element.41), channel_id=1, source_target_pairs={{1,2},{2,1},{3,4},{4,3},{5,6},{6,5},{7,8},{8,7},{9,10},{10,9},{11,... | collective-permute-start | bytes 786440 | tf_op jit(solution)/shard_map/ppermute | solution.py:441
  18.8 0.0 copy-done.3
  18.8 0.1 copy.20.wavelet
  18.9 0.0 copy-done.1
  18.9 0.0 copy-done.2
  18.9 0.9 %shard_map.140 = (f32[64,8,128]{2,1,0:T(8,128)S(1)}, f32[64,8,128]{2,1,0:T(8,128)S(1)}, f32[64,8,128]{2,1,0:T(8,128)S(1)}, f32[64,8,128]{2,1,0:T(8,128)S(1)}, bf16[128,256]{1,0:T(8,128)(2,1)S(1)}) custom-call(f32[64,8,128]{2,1,0:T(8,128)S(1)} %get-tuple-element.43.src.src_old.src_first, f32[64,8,128]{2,1,0:T(8,128)S(1)} %bitcast.15, ...), custom_call_target="tpu_custom_call" | custom-call | flops 5898240 | bytes 2097152 | tf_op jit(solution)/shard_map/pallas_call | solution.py:26
  19.8 0.0 copy-start
  19.8 2.3 %all-gather = f32[128,8,128]{2,1,0:T(8,128)S(1)} all-gather(f32[64,8,128]{2,1,0:T(8,128)S(1)} %get-tuple-element.42), channel_id=2, replica_groups={{0,1},{2,3},{4,5},{6,7},{8,9},{10,11},{12,13},{14,15},{16,17},{18,19},{..., dimensions={0}, use_global_device_ids=true | all-gather | bytes 786432 | tf_op jit(solution)/shard_map/all_gather | solution.py:442
  22.1 1.1 %collective-permute-done.far = f32[64,8,128]{2,1,0:T(8,128)S(1)} collective-permute-done((f32[64,8,128]{2,1,0:T(8,128)}, f32[64,8,128]{2,1,0:T(8,128)S(1)}, u32[]{:S(2)}, u32[]{:S(2)}) %collective-permute-start) | collective-permute-done | bytes 262176 | tf_op jit(solution)/shard_map/ppermute | solution.py:441
  23.2 0.0 all-to-all-done.vel_got
  23.2 0.0 copy-done
  23.2 1.0 %shard_map.141 = (f32[64,8,128]{2,1,0:T(8,128)S(1)}, f32[160,8,128]{2,1,0:T(8,128)S(1)}) custom-call(s32[8,8]{1,0:T(8,128)S(1)} %get-tuple-element.36.tiles, f32[8,4]{1,0:T(8,128)S(1)} %copy.20.wavelet, s32[8]{0:T(128)S(1)} %get-tuple-element.37.spot_x, s32[8]{0:T(128)S(1)} %get-tuple-element.38.spot_z, s32[8]{0:T(128)S(1)} %get-tuple-element.39.spot_y, ...), custom_call_target="tpu_custom_call" | custom-call | flops 5898240 | bytes 2097152 | tf_op jit(solution)/shard_map/pallas_call | solution.py:26
  24.2 9.4 %collective-permute-start.1 = (f32[160,8,128]{2,1,0:T(8,128)S(1)}, f32[160,8,128]{2,1,0:T(8,128)S(1)}, u32[]{:S(2)}, u32[]{:S(2)}) collective-permute-start(f32[160,8,128]{2,1,0:T(8,128)S(1)} %get-tuple-element.51.now.older), channel_id=1, source_target_pairs={{1,2},{2,1},{3,4},{4,3},{5,6},{6,5},{7,8},{8,7},{9,10},{10,9},{11,... | collective-permute-start | bytes 1966088 | tf_op jit(solution)/shard_map/ppermute | solution.py:479
  33.6 0.6 shard_map.142
  34.2 1.9 %collective-permute-start.2 = (f32[160,8,128]{2,1,0:T(8,128)S(1)}, f32[160,8,128]{2,1,0:T(8,128)S(1)}, u32[]{:S(2)}, u32[]{:S(2)}) collective-permute-start(f32[160,8,128]{2,1,0:T(8,128)S(1)} %get-tuple-element.53), channel_id=1, source_target_pairs={{0,1},{1,0},{2,3},{3,2},{4,5},{5,4},{6,7},{7,6},{8,9},{9,8},{10,11... | collective-permute-start | bytes 1966088 | tf_op jit(solution)/shard_map/ppermute | solution.py:483
  36.2 5.7 %collective-permute-done.1.far = f32[160,8,128]{2,1,0:T(8,128)S(1)} collective-permute-done((f32[160,8,128]{2,1,0:T(8,128)S(1)}, f32[160,8,128]{2,1,0:T(8,128)S(1)}, u32[]{:S(2)}, u32[]{:S(2)}) %collective-permute-start.1) | collective-permute-done | bytes 655392 | tf_op jit(solution)/shard_map/ppermute | solution.py:479
  41.9 0.0 collective-permute-done.2.near
  41.9 3.3 %shard_map.143 = (f32[64,8,128]{2,1,0:T(8,128)S(1)}, f32[64,8,128]{2,1,0:T(8,128)S(1)}, f32[128,8,128]{2,1,0:T(8,128)S(1)}, f32[64,8,128]{2,1,0:T(8,128)S(1)}, f32[64,8,128]{2,1,0:T(8,128)S(1)}) custom-call(f32[8,4]{1,0:T(8,128)S(1)} %copy.20.wavelet, s32[8]{0:T(128)S(1)} %get-tuple-element.37.spot_x, s32[8]{0:T(128)S(1)} %get-tuple-element.38.spot_z, ...), custom_call_target="tpu_custom_call" | custom-call | flops 5898240 | bytes 2097152 | tf_op jit(solution)/shard_map/pallas_call | solution.py:26
  45.2 7.2 %collective-permute-start.3 = (f32[64,8,128]{2,1,0:T(8,128)S(1)}, f32[64,8,128]{2,1,0:T(8,128)S(1)}, u32[]{:S(2)}, u32[]{:S(2)}) collective-permute-start(f32[64,8,128]{2,1,0:T(8,128)S(1)} %get-tuple-element.56), channel_id=1, source_target_pairs={{1,2},{2,1},{3,4},{4,3},{5,6},{6,5},{7,8},{8,7},{9,10},{10,9},{11,... | collective-permute-start | bytes 786440 | tf_op jit(solution)/shard_map/ppermute | solution.py:441
  52.5 1.0 %shard_map.144 = (f32[128,8,128]{2,1,0:T(8,128)S(1)}, f32[64,8,128]{2,1,0:T(8,128)S(1)}) custom-call(f32[128,8,128]{2,1,0:T(8,128)S(1)} %get-tuple-element.58.now, f32[64,8,128]{2,1,0:T(8,128)S(1)} %get-tuple-element.59.src_old, f32[64,8,128]{2,1,0:T(8,128)S(1)} %get-tuple-element.60.rec_old, f32[160,8,128]{2,1,0:T(8,128)S(1)} %get-tuple-element.51.now.older, ...), custom_call_target="tpu_custom_call" | custom-call | flops 5898240 | bytes 2097152 | tf_op jit(solution)/shard_map/pallas_call | solution.py:26
  53.5 2.2 %all-gather.1 = f32[128,8,128]{2,1,0:T(8,128)S(1)} all-gather(f32[64,8,128]{2,1,0:T(8,128)S(1)} %get-tuple-element.57), channel_id=3, replica_groups={{0,1},{2,3},{4,5},{6,7},{8,9},{10,11},{12,13},{14,15},{16,17},{18,19},{..., dimensions={0}, use_global_device_ids=true | all-gather | bytes 786432 | tf_op jit(solution)/shard_map/all_gather | solution.py:442
  55.7 2.5 %collective-permute-done.3.far = f32[64,8,128]{2,1,0:T(8,128)S(1)} collective-permute-done((f32[64,8,128]{2,1,0:T(8,128)S(1)}, f32[64,8,128]{2,1,0:T(8,128)S(1)}, u32[]{:S(2)}, u32[]{:S(2)}) %collective-permute-start.3) | collective-permute-done | bytes 262176 | tf_op jit(solution)/shard_map/ppermute | solution.py:441
  58.2 1.0 %shard_map.145 = (f32[64,8,128]{2,1,0:T(8,128)S(1)}, f32[64,8,128]{2,1,0:T(8,128)S(1)}, f32[8,16,8,128]{3,2,1,0:T(8,128)S(1)}) custom-call(s32[8,8]{1,0:T(8,128)S(1)} %get-tuple-element.36.tiles, f32[8,4]{1,0:T(8,128)S(1)} %copy.20.wavelet, s32[8]{0:T(128)S(1)} %get-tuple-element.37.spot_x, s32[8]{0:T(128)S(1)} %get-tuple-element.38.spot_z, ...), custom_call_target="tpu_custom_call" | custom-call | flops 5898240 | bytes 2097152 | tf_op jit(solution)/shard_map/pallas_call | solution.py:26
  59.2 12.3 %all_to_all.10.got = f32[8,16,8,128]{3,2,1,0:T(8,128)S(1)} all-to-all(f32[8,16,8,128]{3,2,1,0:T(8,128)S(1)} %get-tuple-element.63), channel_id=1, replica_groups=mesh['shot'=8,'slab'=64] {'shot'}, dimensions={0} | all-to-all | bytes 1048576 | tf_op jit(solution)/shard_map/all_to_all | solution.py:499
  71.5 1.5 %shard_map.146 = (f32[64,8,128]{2,1,0:T(8,128)}, f32[64,8,128]{2,1,0:T(8,128)}, f32[64,8,128]{2,1,0:T(8,128)}) custom-call(s32[8,8]{1,0:T(8,128)S(1)} %get-tuple-element.36.tiles, f32[8,16,8,128]{3,2,1,0:T(8,128)S(1)} %all_to_all.10.got, f32[64,8,128]{2,1,0:T(8,128)S(1)} %get-tuple-element.64.src, f32[64,8,128]{2,1,0:T(8,128)S(1)} %get-tuple-element.65.rec), custom_call_target="tpu_custom_call" | custom-call | tf_op jit(solution)/shard_map/pallas_call | solution.py:26
Async XLA Ops:
  3.0 15.8 %copy-start.3 = (f32[8,4]{0,1:T(4,128)S(1)}, f32[8,4]{0,1:T(4,128)}, u32[]{:S(2)}) copy-start(f32[8,4]{0,1:T(4,128)} %param.18) | copy-start | bytes 388
  3.0 15.9 %copy-start.1 = (f32[1,64,8,128]{3,2,1,0:T(8,128)S(1)}, f32[1,64,8,128]{3,2,1,0:T(8,128)}, u32[]{:S(2)}) copy-start(f32[1,64,8,128]{3,2,1,0:T(8,128)} %param.12) | copy-start | bytes 786436
  3.0 15.9 %copy-start.2 = (f32[1,64,8,128]{3,2,1,0:T(8,128)S(1)}, f32[1,64,8,128]{3,2,1,0:T(8,128)}, u32[]{:S(2)}) copy-start(f32[1,64,8,128]{3,2,1,0:T(8,128)} %param.15) | copy-start | bytes 786436
  3.0 20.2 %all-to-all-start = ((f32[8,16,8,128]{3,2,1,0:T(8,128)}), f32[8,16,8,128]{3,2,1,0:T(8,128)S(1)}, u32[]{:S(2)}, u32[]{:S(2)}) async-start(f32[8,16,8,128]{3,2,1,0:T(8,128)} %get-tuple-element.50), calls=%async_computation | async-start | bytes 1048576 | tf_op jit(solution)/shard_map/all_to_all | solution.py:466
  8.2 15.1 %collective-permute-start = (f32[64,8,128]{2,1,0:T(8,128)}, f32[64,8,128]{2,1,0:T(8,128)S(1)}, u32[]{:S(2)}, u32[]{:S(2)}) collective-permute-start(f32[64,8,128]{2,1,0:T(8,128)} %get-tuple-element.41), channel_id=1, source_target_pairs={{1,2},{2,1},{3,4},{4,3},{5,6},{6,5},{7,8},{8,7},{9,10},{10,9},{11,... | collective-permute-start | bytes 786440 | tf_op jit(solution)/shard_map/ppermute | solution.py:441
  19.8 3.4 %copy-start = (bf16[1,4,64,128]{3,2,1,0:T(8,128)(2,1)S(1)}, bf16[1,4,64,128]{3,2,1,0:T(8,128)(2,1)}, u32[]{:S(2)}) copy-start(bf16[1,4,64,128]{3,2,1,0:T(8,128)(2,1)} %param.23) | copy-start | bytes 196612
  24.2 17.7 %collective-permute-start.1 = (f32[160,8,128]{2,1,0:T(8,128)S(1)}, f32[160,8,128]{2,1,0:T(8,128)S(1)}, u32[]{:S(2)}, u32[]{:S(2)}) collective-permute-start(f32[160,8,128]{2,1,0:T(8,128)S(1)} %get-tuple-element.51.now.older), channel_id=1, source_target_pairs={{1,2},{2,1},{3,4},{4,3},{5,6},{6,5},{7,8},{8,7},{9,10},{10,9},{11,... | collective-permute-start | bytes 1966088 | tf_op jit(solution)/shard_map/ppermute | solution.py:479
  34.2 7.7 %collective-permute-start.2 = (f32[160,8,128]{2,1,0:T(8,128)S(1)}, f32[160,8,128]{2,1,0:T(8,128)S(1)}, u32[]{:S(2)}, u32[]{:S(2)}) collective-permute-start(f32[160,8,128]{2,1,0:T(8,128)S(1)} %get-tuple-element.53), channel_id=1, source_target_pairs={{0,1},{1,0},{2,3},{3,2},{4,5},{5,4},{6,7},{7,6},{8,9},{9,8},{10,11... | collective-permute-start | bytes 1966088 | tf_op jit(solution)/shard_map/ppermute | solution.py:483
  45.2 13.0 %collective-permute-start.3 = (f32[64,8,128]{2,1,0:T(8,128)S(1)}, f32[64,8,128]{2,1,0:T(8,128)S(1)}, u32[]{:S(2)}, u32[]{:S(2)}) collective-permute-start(f32[64,8,128]{2,1,0:T(8,128)S(1)} %get-tuple-element.56), channel_id=1, source_target_pairs={{1,2},{2,1},{3,4},{4,3},{5,6},{6,5},{7,8},{8,7},{9,10},{10,9},{11,... | collective-permute-start | bytes 786440 | tf_op jit(solution)/shard_map/ppermute | solution.py:441

commit v4 on v0

v4 whole, which is shorter than its diff:
```python
import jax
import jax.numpy as jnp
from jax import lax
from jax.experimental import pallas as pl
from jax.experimental.pallas import tpu as pltpu
from jax.sharding import PartitionSpec as P


BX = 8
KT = 8
STEPS = 4
CAP = 2
REACH = 4
PAD = 8
VMEM = pltpu.VMEM
SMEM = pltpu.SMEM
HBM = pltpu.HBM

SCALE = 5040.0
TAPS = (-43050.0, 8064.0, -1008.0, 128.0, -9.0)


def call(body, outs, in_spaces, *args, scratch=()):
    outs = [o if isinstance(o[0], tuple) else (o, VMEM) for o in outs]
    outs = [o if len(o) == 3 else o + (jnp.float32,) for o in outs]
    size = 8 * 64 * 128
    return pl.pallas_call(
        body,
        out_shape=[jax.ShapeDtypeStruct(s, t) for s, _, t in outs],
        in_specs=[pl.BlockSpec(memory_space=s) for s in in_spaces],
        out_specs=[pl.BlockSpec(memory_space=m) for _, m, _ in outs],
        scratch_shapes=list(scratch),
        compiler_params=pltpu.CompilerParams(vmem_limit_bytes=24 * 1024 * 1024),
        cost_estimate=pl.CostEstimate(
            flops=90 * size, bytes_accessed=32 * size, transcendentals=0
        ),
    )(*args)


def is_odd():
    return lax.rem(lax.axis_index("slab"), 2) == 1


def partner():
    return jnp.where(is_odd(), 0, 1)


def z_of(plane, depth):
    return jnp.where(is_odd(), plane, depth - 1 - plane)


def tap_of(reach):
    weight = jnp.zeros(reach.shape, jnp.float32)
    for r in range(1, REACH + 1):
        weight = jnp.where(reach == r, TAPS[r], weight)
    return weight


def along_y_matrix(size_y):
    shape = (2 * size_y, size_y)
    row = lax.rem(lax.broadcasted_iota(jnp.int32, shape, 0), size_y)
    return tap_of(jnp.abs(row - lax.broadcasted_iota(jnp.int32, shape, 1))).astype(jnp.bfloat16)


def along_y(planes, to_y):
    rows = planes.reshape(-1, planes.shape[2])
    high = rows.astype(jnp.bfloat16)
    low = (rows - high.astype(jnp.float32)).astype(jnp.bfloat16)
    sums = jnp.dot(
        jnp.concatenate([high, low], axis=1), to_y, preferred_element_type=jnp.float32
    )
    return sums.reshape(planes.shape)


def clear_edges(padded):
    count, rows, size_y = padded.shape
    zeros = jnp.zeros((count, PAD, size_y), jnp.float32)
    padded[:, pl.ds(0, PAD)] = zeros
    padded[:, pl.ds(rows - PAD, PAD)] = zeros


def full_sums(padded, planes, first, plane_at, to_y):
    count, size_x, _ = planes.shape
    padded[pl.ds(0, count), pl.ds(PAD, size_x)] = planes
    lines = along_y(planes, to_y)
    sums = []
    for p in range(count):
        total = lines[p] + TAPS[0] * planes[p]
        for r in range(1, REACH + 1):
            terms = padded[p, pl.ds(PAD + r, size_x)] + padded[p, pl.ds(PAD - r, size_x)]
            for other in (plane_at(first + p + r), plane_at(first + p - r)):
                if other is not None:
                    terms += other
            total += TAPS[r] * terms
        sums.append(total)
    return sums


def beyond_sums(plane, plane_at):
    total = 0.0
    for r in range(1, REACH + 1):
        for other in (plane_at(plane + r), plane_at(plane - r)):
            if other is not None:
                total += TAPS[r] * other
    return total


def add_spot(step, fields, places, depth):
    wavelet, spot_x, spot_z, spot_y = places
    shot = lax.axis_index("shot")
    local = spot_z[shot] - lax.axis_index("slab") * depth
    plane = z_of(local, depth)
    x = spot_x[shot]
    for first, last, ref, index in fields:

        @pl.when((plane >= first) & (plane <= last))
        def _():
            row = lax.broadcasted_iota(jnp.int32, (8, ref.shape[2]), 0)
            lane = lax.broadcasted_iota(jnp.int32, (8, ref.shape[2]), 1)
            here = (row == lax.rem(x, 8)) & (lane == spot_y[shot])
            rows = pl.ds(pl.multiple_of(lax.div(x, 8) * 8, 8), 8)
            ref[index(plane), rows] += jnp.where(here, wavelet[shot, step], 0.0)


def add_traces(step, fields, depth_at, traces, depth):
    local = depth_at[lax.axis_index("shot")] - lax.axis_index("slab") * depth
    plane = z_of(local, depth)
    for first, last, ref, index in fields:

        @pl.when((plane >= first) & (plane <= last))
        def _():
            ref[index(plane)] += traces[STEPS - 1 - step].astype(jnp.float32)


def add_sources(step, src_fields, rec_fields, places, depth):
    wavelet, spot_x, spot_z, spot_y, depth_at, traces = places
    add_spot(step, src_fields, (wavelet, spot_x, spot_z, spot_y), depth)
    add_traces(step, rec_fields, depth_at, traces, depth)


def first_slot(tiles, shot, g):
    before = jnp.int32(0)
    for k in range(KT):
        before += (tiles[g, k] < shot * BX).astype(jnp.int32)
    return before


def place_of(tiles, shot, k):
    owner = lax.shift_right_logical(tiles[shot, k], 3)
    before = lax.shift_right_logical(tiles[shot, max(k - 1, 0)], 3)
    slot = (before == owner).astype(jnp.int32) if k else jnp.int32(0)
    return owner, slot


def start_kernel(
    src_in, rec_in, vel_in, tiles_in, x_in, z_in, y_in, depth_in,
    send, to_far, src, rec, tiles_out, x_out, z_out, y_out, depth_out,
    src_raw, rec_raw, vel, tiles, sems,
):
    shot = lax.axis_index("shot")
    moves = [(src_in, src_raw), (rec_in, rec_raw), (vel_in, vel), (tiles_in, tiles)]
    moves += [(tiles_in, tiles_out), (x_in, x_out), (z_in, z_out), (y_in, y_out)]
    moves += [(depth_in, depth_out)]
    copies = [pltpu.make_async_copy(a, b, sems.at[i]) for i, (a, b) in enumerate(moves)]
    for copy in copies:
        copy.start()
    depth, size_x, _ = src.shape
    for f, (raw, field) in enumerate(((src_raw, src), (rec_raw, rec))):
        copies[f].wait()
        for p in range(depth):
            plane = raw[pl.ds(z_of(p, depth), size_x, stride=depth)]
            field[p] = plane
            if p >= depth - REACH:
                to_far[f * REACH + p - (depth - REACH)] = plane
    for copy in copies[2:]:
        copy.wait()
    held = vel.shape[0] // (BX * depth)

    def one_shot(g, _):
        before = first_slot(tiles, shot, g)
        for j in range(CAP):
            k = jnp.minimum(before + j, KT - 1)
            own = jnp.clip(tiles[g, k] - shot * BX, 0, held - 1)
            for p in range(depth):
                at = own * (BX * depth) + z_of(p, depth)
                send[g, j * depth + p] = vel[pl.ds(at, BX, stride=depth)]
        return 0

    lax.fori_loop(0, send.shape[0], one_shot, 0)


def first_interior_kernel(src, rec, src_old, rec_old, to_near, sums, base, to_y, padded):
    depth, size_x, size_y = src.shape
    to_y[...] = along_y_matrix(size_y)
    clear_edges(padded)
    for f, (field, old) in enumerate(((src, src_old), (rec, rec_old))):

        def plane_at(m):
            return field[m] if 0 <= m < depth else None

        for first in range(0, depth, REACH):
            planes = field[pl.ds(first, REACH)]
            if first == 0:
                to_near[pl.ds(f * REACH, REACH)] = planes
            for i, total in enumerate(full_sums(padded, planes, first, plane_at, to_y[...])):
                p = first + i
                sums[f * depth + p] = total
                before = old[pl.ds(z_of(p, depth), size_x, stride=depth)]
                base[f * depth + p] = 2.0 * planes[i] - before


def rate_kernel(tiles, vel_got, near, sums, base, rate, part):
    shot = lax.axis_index("shot")
    mine = partner()
    depth = rate.shape[0]
    for k in range(KT):
        owner, slot = place_of(tiles, shot, k)
        for p in range(depth):
            tile = vel_got[owner, slot * depth + p]
            rate[p, pl.ds(k * BX, BX)] = tile * tile * (1.0 / SCALE)
    for f in range(2):

        def plane_at(m):
            return near[mine, f * REACH - 1 - m] if m < 0 else None

        for p in range(depth):
            total = sums[f * depth + p]
            if p < REACH:
                total += beyond_sums(p, plane_at)
            part[f * depth + p] = base[f * depth + p] + rate[p] * total


def first_kernel(wavelet, spot_x, spot_z, spot_y, depth_at, traces, far, part, rate, now):
    depth = rate.shape[0]
    for f in range(2):

        def plane_at(m):
            return far[f * REACH + REACH - 1 - (m - depth)] if m >= depth else None

        for p in range(depth):
            value = part[f * depth + p]
            if p >= depth - REACH:
                value += rate[p] * beyond_sums(p, plane_at)
            now[f * depth + p] = value
    now[pl.ds(2 * depth, REACH)] = rate[pl.ds(depth - REACH, REACH)]
    places = (wavelet, spot_x, spot_z, spot_y, depth_at, traces)
    own = (0, depth - 1, now)
    add_sources(0, [own + (lambda m: m,)], [own + (lambda m: depth + m,)], places, depth)


def wide_interior_kernel(now, src_old, rec_old, rate, to_y, to_near, base, padded):
    depth = rate.shape[0]
    clear_edges(padded)
    to_near[pl.ds(0, 2 * depth)] = now[pl.ds(0, 2 * depth)]
    to_near[pl.ds(2 * depth, REACH)] = rate[pl.ds(0, REACH)]
    for f, old in enumerate((src_old, rec_old)):

        def plane_at(m):
            return now[f * depth + m] if 0 <= m < depth else None

        for first in range(0, depth, REACH):
            planes = now[pl.ds(f * depth + first, REACH)]
            for i, total in enumerate(full_sums(padded, planes, first, plane_at, to_y[...])):
                p = first + i
                base[f * depth + p] = 2.0 * planes[i] - old[p] + rate[p] * total


def wide_near_kernel(
    wavelet, spot_x, spot_z, spot_y, depth_at, traces, near, near_old, now, base, rate, to_y,
    mid_near, mid_low, mid_part, padded,
):
    depth = rate.shape[0]
    mine = partner()
    clear_edges(padded)
    for f in range(2):

        def plane_at(m):
            if m >= 0:
                return now[f * depth + m]
            return near[f * depth - 1 - m]

        planes = near[pl.ds(f * depth, REACH)]
        totals = full_sums(padded, planes, 0, lambda m: plane_at(-1 - m), to_y[...])
        for i, total in enumerate(totals):
            value = 2.0 * planes[i] - near_old[mine, f * REACH + i]
            mid_near[f * REACH + i] = value + near[2 * depth + i] * total
        for p in range(depth):
            if p < REACH:
                share = beyond_sums(p, lambda m: plane_at(m) if m < 0 else None)
                mid_low[f * REACH + p] = base[f * depth + p] + rate[p] * share
            else:
                mid_part[f * REACH + p - REACH] = base[f * depth + p]
    places = (wavelet, spot_x, spot_z, spot_y, depth_at, traces)
    fields = [
        [
            (0, REACH - 1, mid_low, lambda m, f=f: f * REACH + m),
            (-REACH, -1, mid_near, lambda m, f=f: f * REACH - 1 - m),
        ]
        for f in range(2)
    ]
    add_sources(1, *fields, places, depth)


def wide_far_kernel(
    wavelet, spot_x, spot_z, spot_y, depth_at, traces, far, far_old, now, mid_low, mid_part, rate,
    to_y, mid_high, to_far, mid_far, padded,
):
    depth = rate.shape[0]
    high = depth - REACH
    clear_edges(padded)
    places = (wavelet, spot_x, spot_z, spot_y, depth_at, traces)
    for f in range(2):

        def plane_at(m):
            if m < depth:
                return now[f * depth + m]
            return far[f * depth + 2 * depth - 1 - m]

        planes = jnp.stack([plane_at(depth + i) for i in range(REACH)])
        totals = full_sums(padded, planes, depth, plane_at, to_y[...])
        for i, total in enumerate(totals):
            value = 2.0 * planes[i] - far_old[f * REACH + REACH - 1 - i]
            mid_far[f * REACH + i] = value + far[2 * depth + REACH - 1 - i] * total
        for p in range(high, depth):
            share = beyond_sums(p, lambda m: plane_at(m) if m >= depth else None)
            mid_high[f * REACH + p - high] = mid_part[f * REACH + p - high] + rate[p] * share
    fields = [
        [
            (high, depth - 1, mid_high, lambda m, f=f: f * REACH + m - high),
            (depth, depth + REACH - 1, mid_far, lambda m, f=f: f * REACH + m - depth),
        ]
        for f in range(2)
    ]
    add_sources(1, *fields, places, depth)
    for f in range(2):

        def mid_at(m):
            if m < high:
                return mid_low[f * REACH + m]
            return mid_high[f * REACH + m - high] if m < depth else mid_far[f * REACH + m - depth]

        planes = mid_high[pl.ds(f * REACH, REACH)]
        for i, total in enumerate(full_sums(padded, planes, high, mid_at, to_y[...])):
            p = high + i
            value = 2.0 * planes[i] - now[f * depth + p]
            to_far[f * REACH + i] = value + rate[p] * total
    fields = [
        [(high, depth - 1, to_far, lambda m, f=f: f * REACH + m - high)] for f in range(2)
    ]
    add_sources(2, *fields, places, depth)


def interior_kernel(
    wavelet, spot_x, spot_z, spot_y, depth_at, traces, now, mid_near, mid_low, mid_high, new_high,
    rate, to_y, new_low, base, partial, padded,
):
    depth = rate.shape[0]
    high = depth - REACH
    clear_edges(padded)
    places = (wavelet, spot_x, spot_z, spot_y, depth_at, traces)

    def mid_at(f, m):
        if m < 0:
            return mid_near[f * REACH - 1 - m]
        return mid_low[f * REACH + m] if m < high else mid_high[f * REACH + m - high]

    def new_at(f, m):
        return new_low[f * REACH + m] if m < high else new_high[f * REACH + m - high]

    for f in range(2):
        planes = mid_low[pl.ds(f * REACH, REACH)]
        totals = full_sums(padded, planes, 0, lambda m: mid_at(f, m), to_y[...])
        for p, total in enumerate(totals):
            new_low[f * REACH + p] = 2.0 * planes[p] - now[f * depth + p] + rate[p] * total
    fields = [[(0, high - 1, new_low, lambda m, f=f: f * REACH + m)] for f in range(2)]
    add_sources(2, *fields, places, depth)
    for f in range(2):
        for first, part in ((0, new_low), (high, new_high)):
            planes = part[pl.ds(f * REACH, REACH)]

            def plane_at(m):
                return new_at(f, m) if 0 <= m < depth else None

            for i, total in enumerate(full_sums(padded, planes, first, plane_at, to_y[...])):
                p = first + i
                base[f * depth + p] = 2.0 * planes[i] - mid_at(f, p) + rate[p] * total
    for p in range(depth):
        total = new_at(0, p) * now[depth + p] + mid_at(0, p) * mid_at(1, p)
        partial[p] = total + now[p] * new_at(1, p)


def last_kernel(
    tiles, wavelet, spot_x, spot_z, spot_y, depth_at, traces, far, near, base, rate, partial,
    src_first, rec_first, new, send,
):
    shot = lax.axis_index("shot")
    mine = partner()
    depth = rate.shape[0]
    for f in range(2):

        def plane_at(m):
            if m < 0:
                return near[mine, f * REACH - 1 - m]
            return far[f * REACH + REACH - 1 - (m - depth)] if m >= depth else None

        for p in range(depth):
            new[f * depth + p] = base[f * depth + p] + rate[p] * beyond_sums(p, plane_at)
    places = (wavelet, spot_x, spot_z, spot_y, depth_at, traces)
    own = (0, depth - 1, new)
    add_sources(STEPS - 1, [own + (lambda m: m,)], [own + (lambda m: depth + m,)], places, depth)
    send[...] = jnp.zeros(send.shape, jnp.float32)
    for k in range(KT):
        owner, slot = place_of(tiles, shot, k)
        at = pl.ds(k * BX, BX)
        for p in range(depth):
            total = partial[p, at] + new[p, at] * rec_first[p, at]
            send[owner, slot * depth + p] = total + src_first[p, at] * new[depth + p, at]


def gather_kernel(
    tiles, got, new, out, src_out, rec_out, total, out_rows, src_rows, rec_rows, sems
):
    shot = lax.axis_index("shot")
    depth = new.shape[0] // 2
    size_x = new.shape[1]
    held = total.shape[0] // depth
    total[...] = jnp.zeros(total.shape, jnp.float32)
    for g in range(got.shape[0]):
        before = first_slot(tiles, shot, g)
        for j in range(CAP):
            k = jnp.minimum(before + j, KT - 1)
            own = jnp.clip(tiles[g, k] - shot * BX, 0, held - 1)
            total[pl.ds(own * depth, depth)] += got[g, pl.ds(j * depth, depth)]
    for t in range(held):
        for p in range(depth):
            at = t * BX * depth + z_of(p, depth)
            out_rows[pl.ds(at, BX, stride=depth)] = total[t * depth + p]
    copies = [pltpu.make_async_copy(out_rows, out, sems.at[0])]
    copies[0].start()
    for f, (rows, to) in enumerate(((src_rows, src_out), (rec_rows, rec_out))):
        for p in range(depth):
            rows[pl.ds(z_of(p, depth), size_x, stride=depth)] = new[f * depth + p]
        copies.append(pltpu.make_async_copy(rows, to, sems.at[1 + f]))
        copies[-1].start()
    for copy in copies:
        copy.wait()


def local(
    src_prev,
    src_cur,
    rec_cur,
    rec_next,
    velocity,
    aperture_tiles,
    wavelet,
    src_x,
    src_z,
    src_y,
    rec_depth,
    rec_data,
):
    slabs = lax.axis_size("slab")
    shots = lax.axis_size("shot")
    far_pairs = []
    for i in range(1, slabs - 1, 2):
        far_pairs += [(i, i + 1), (i + 1, i)]
    near_groups = [[i, i + 1] for i in range(0, slabs, 2)]
    near_pairs = [(i, i ^ 1) for i in range(slabs)]

    def flat(array):
        return array.reshape(-1, array.shape[-1])

    _, size_x, depth, size_y = src_cur.shape
    raw = (depth * size_x, size_y)
    model = (velocity.shape[0] * depth, size_y)
    one, two = (depth, size_x, size_y), (2 * depth, size_x, size_y)
    halo = (2 * REACH, size_x, size_y)
    wide = (2 * depth + REACH, size_x, size_y)
    buffer = (shots, CAP * depth, BX, size_y)
    dma = pltpu.SemaphoreType.DMA
    padded = VMEM((REACH, size_x + 2 * PAD, size_y), jnp.float32)
    given = (flat(src_cur), flat(rec_cur), flat(velocity), aperture_tiles)
    given += (src_x, src_z, src_y, rec_depth)
    whole_numbers = [(a.shape, VMEM, jnp.int32) for a in given[3:]]
    send, to_far, src, rec, tiles, *places = call(
        start_kernel, [buffer, halo, one, one] + whole_numbers, [HBM] * 8,
        *[pltpu.with_memory_space_constraint(a, HBM) for a in given],
        scratch=[
            VMEM(raw, jnp.float32), VMEM(raw, jnp.float32), VMEM(model, jnp.float32),
            SMEM(aperture_tiles.shape, jnp.int32), dma((9,)),
        ],
    )
    places = (wavelet, *places, rec_data[0])
    place_spaces = [SMEM] * 5 + [VMEM]

    vel_got = lax.all_to_all(send, "shot", 0, 0)
    far = lax.ppermute(to_far, "slab", far_pairs)
    to_near, sums, base, to_y = call(
        first_interior_kernel, [halo, two, two, ((2 * size_y, size_y), VMEM, jnp.bfloat16)],
        [VMEM] * 4, src, rec, flat(src_prev), flat(rec_next), scratch=[padded],
    )
    near = lax.all_gather(to_near, "slab", axis_index_groups=near_groups)
    rate, part = call(
        rate_kernel, [one, two], [SMEM] + [VMEM] * 4, tiles, vel_got, near, sums, base
    )
    (now,) = call(first_kernel, [wide], place_spaces + [VMEM] * 3, *places, far, part, rate)

    wide_far = lax.ppermute(now, "slab", far_pairs)
    to_near, base = call(
        wide_interior_kernel, [wide, two], [VMEM] * 5, now, src, rec, rate, to_y, scratch=[padded]
    )
    wide_near = lax.ppermute(to_near, "slab", near_pairs)
    mid_near, mid_low, mid_part = call(
        wide_near_kernel, [halo] * 3, place_spaces + [VMEM] * 6,
        *places, wide_near, near, now, base, rate, to_y, scratch=[padded],
    )
    mid_high, new_high = call(
        wide_far_kernel, [halo] * 2, place_spaces + [VMEM] * 7,
        *places, wide_far, far, now, mid_low, mid_part, rate, to_y,
        scratch=[VMEM(halo, jnp.float32), padded],
    )

    far = lax.ppermute(new_high, "slab", far_pairs)
    new_low, base, partial = call(
        interior_kernel, [halo, two, one], place_spaces + [VMEM] * 7,
        *places, now, mid_near, mid_low, mid_high, new_high, rate, to_y, scratch=[padded],
    )
    near = lax.all_gather(new_low, "slab", axis_index_groups=near_groups)
    new, send = call(
        last_kernel, [two, buffer], [SMEM] + place_spaces + [VMEM] * 7,
        tiles, *places, far, near, base, rate, partial, src, rec,
    )
    image_got = lax.all_to_all(send, "shot", 0, 0)
    image, src, rec = call(
        gather_kernel, [(model, HBM), (raw, HBM), (raw, HBM)], [SMEM] + [VMEM] * 2,
        tiles, image_got, new,
        scratch=[
            VMEM((velocity.shape[0] // BX * depth, BX, size_y), jnp.float32),
            VMEM(model, jnp.float32), VMEM(raw, jnp.float32), VMEM(raw, jnp.float32), dma((3,)),
        ],
    )
    return image.reshape(velocity.shape), src.reshape(src_cur.shape), rec.reshape(src_cur.shape)


def solution(mesh):
    wave = P("shot", None, "slab", None)
    model = P("shot", "slab", None)
    return jax.shard_map(
        local,
        mesh=mesh,
        in_specs=(wave,) * 4 + (model,) + (P(),) * 6 + (P("shot", None, None, None),),
        out_specs=(model, wave, wave),
        check_vma=False,
    )
```

time: 201 us -> 75.6 us (0.38)
  the two profiles are of different devices: /device:TPU:32 before, /device:TPU:16 now
where the time goes in v4:
time: 75.6 us; the launch traced here: 75.2 us
  starting transfers between devices  34.4 us (46%)
  blocking collectives  17.4 us (23%)
  Pallas kernels  13.6 us (18%)
  waiting for transfers between devices  8.98 us (12%)
  between operations  0.77 us (1%)
    pallas_call x10, Pallas kernels, call(): pl.pallas_call(body, out_shape=[jax.ShapeDtypeStruct(s, t) for s, _, t in...  13.6 us
    all_to_all x1, blocking collectives, local(): image_got = lax.all_to_all(send, 'shot', 0, 0)  13 us
    ppermute x1, starting transfers between devices, local(): far = lax.ppermute(to_far, 'slab', far_pairs)  10.6 us
    ppermute x1, starting transfers between devices, local(): wide_far = lax.ppermute(now, 'slab', far_pairs)  9.43 us
    ppermute x1, starting transfers between devices, local(): far = lax.ppermute(new_high, 'slab', far_pairs)  7.25 us
    ppermute x1, waiting for transfers between devices, local(): wide_far = lax.ppermute(now, 'slab', far_pairs)  6.98 us
    all_to_all x1, starting transfers between devices, local(): vel_got = lax.all_to_all(send, 'shot', 0, 0)  5.16 us
    all_gather x1, blocking collectives, local(): near = lax.all_gather(to_near, 'slab', axis_index_groups=near_groups)  2.18 us
  transfers between devices with their start and end apart: 5, of which 3 were waited for; matrix products, arithmetic and copies ran while one was open for 0% of the time, Pallas kernels for 7%

profile of v4, /device:TPU:16, one launch (start us, length us, event | category | flops | bytes accessed | tf_op | source)
XLA Modules:
  0.0 75.2 jit_solution(14791153862729973700)
XLA Ops:
  0.6 2.4 %shard_map.139 = (f32[8,16,8,128]{3,2,1,0:T(8,128)}, f32[8,64,128]{2,1,0:T(8,128)S(1)}, f32[8,64,128]{2,1,0:T(8,128)S(1)}, f32[8,64,128]{2,1,0:T(8,128)S(1)}, s3...) custom-call(f32[512,128]{1,0:T(8,128)} %bitcast.21, f32[512,128]{1,0:T(8,128)} %bitcast.22, ...), custom_call_target="tpu_custom_call" | custom-call | flops 5898240 | bytes 2097152 | tf_op jit(solution)/shard_map/pallas_call | solution.py:27
  3.0 0.0 copy-start.3
  3.0 0.0 copy-start.1
  3.0 0.0 copy-start.2
  3.0 5.2 %all-to-all-start = ((f32[8,16,8,128]{3,2,1,0:T(8,128)}), f32[8,16,8,128]{3,2,1,0:T(8,128)S(1)}, u32[]{:S(2)}, u32[]{:S(2)}) async-start(f32[8,16,8,128]{3,2,1,0:T(8,128)} %get-tuple-element.39), calls=%async_computation | async-start | bytes 1048576 | tf_op jit(solution)/shard_map/all_to_all | solution.py:497
  8.2 10.6 %collective-permute-start = (f32[8,64,128]{2,1,0:T(8,128)S(1)}, f32[8,64,128]{2,1,0:T(8,128)S(1)}, u32[]{:S(2)}, u32[]{:S(2)}) collective-permute-start(f32[8,64,128]{2,1,0:T(8,128)S(1)} %get-tuple-element.38), channel_id=1, source_target_pairs={{1,2},{2,1},{3,4},{4,3},{5,6},{6,5},{7,8},{8,7},{9,10},{10,9},{11,... | collective-permute-start | bytes 786440 | tf_op jit(solution)/shard_map/ppermute | solution.py:498
  18.8 0.0 copy-done.3
  18.8 0.1 copy.24.wavelet
  18.9 0.0 copy-done.1
  18.9 0.0 copy-done.2
  18.9 0.9 %shard_map.140 = (f32[8,64,128]{2,1,0:T(8,128)S(1)}, f32[16,64,128]{2,1,0:T(8,128)S(1)}, f32[16,64,128]{2,1,0:T(8,128)S(1)}, bf16[256,128]{1,0:T(8,128)(2,1)S(1)}) custom-call(f32[8,64,128]{2,1,0:T(8,128)S(1)} %get-tuple-element.40.src.src_old.src_first, f32[8,64,128]{2,1,0:T(8,128)S(1)} %get-tuple-element.41.rec.rec_old.rec_first, f32[512,128]{1,0:T(8,128)S(1)} %bitcast.19, ...), custom_call_target="tpu_custom_call" | custom-call | flops 5898240 | bytes 2097152 | tf_op jit(solution)/shard_map/pallas_call | solution.py:27
  19.8 2.2 %all-gather = f32[16,64,128]{2,1,0:T(8,128)S(1)} all-gather(f32[8,64,128]{2,1,0:T(8,128)S(1)} %get-tuple-element.42), channel_id=2, replica_groups={{0,1},{2,3},{4,5},{6,7},{8,9},{10,11},{12,13},{14,15},{16,17},{18,19},{..., dimensions={0}, use_global_device_ids=true | all-gather | bytes 786432 | tf_op jit(solution)/shard_map/all_gather | solution.py:503
  22.0 0.0 all-to-all-done.vel_got
  22.0 0.0 copy-start
  22.0 0.8 %shard_map.141 = (f32[8,64,128]{2,1,0:T(8,128)S(1)}, f32[16,64,128]{2,1,0:T(8,128)S(1)}) custom-call(s32[8,8]{1,0:T(8,128)S(1)} %get-tuple-element.33.tiles, f32[8,16,8,128]{3,2,1,0:T(8,128)S(1)} %all-to-all-done.vel_got, f32[2,8,64,128]{3,2,1,0:T(8,128)S(1)} %bitcast.11, f32[16,64,128]{2,1,0:T(8,128)S(1)} %get-tuple-element.43.sums, ...), custom_call_target="tpu_custom_call" | custom-call | flops 5898240 | bytes 2097152 | tf_op jit(solution)/shard_map/pallas_call | solution.py:27
  22.8 0.2 collective-permute-done.far.far_old
  23.0 0.0 copy-done
  23.0 0.7 shard_map.142.now
  23.7 1.0 %shard_map.143 = (f32[20,64,128]{2,1,0:T(8,128)S(1)}, f32[16,64,128]{2,1,0:T(8,128)S(1)}) custom-call(f32[20,64,128]{2,1,0:T(8,128)S(1)} %shard_map.142.now, f32[8,64,128]{2,1,0:T(8,128)S(1)} %get-tuple-element.40.src.src_old.src_first, f32[8,64,128]{2,1,0:T(8,128)S(1)} %get-tuple-element.41.rec.rec_old.rec_first, f32[8,64,128]{2,1,0:T(8,128)S(1)} %get-tuple-element.46.rate, ...), custom_call_target="tpu_custom_call" | custom-call | flops 5898240 | bytes 2097152 | tf_op jit(solution)/shard_map/pallas_call | solution.py:27
  24.7 1.9 %collective-permute-start.2 = (f32[20,64,128]{2,1,0:T(8,128)S(1)}, f32[20,64,128]{2,1,0:T(8,128)S(1)}, u32[]{:S(2)}, u32[]{:S(2)}) collective-permute-start(f32[20,64,128]{2,1,0:T(8,128)S(1)} %get-tuple-element.48), channel_id=1, source_target_pairs={{0,1},{1,0},{2,3},{3,2},{4,5},{5,4},{6,7},{7,6},{8,9},{9,8},{10,11... | collective-permute-start | bytes 1966088 | tf_op jit(solution)/shard_map/ppermute | solution.py:513
  26.6 9.4 %collective-permute-start.1 = (f32[20,64,128]{2,1,0:T(8,128)S(1)}, f32[20,64,128]{2,1,0:T(8,128)S(1)}, u32[]{:S(2)}, u32[]{:S(2)}) collective-permute-start(f32[20,64,128]{2,1,0:T(8,128)S(1)} %shard_map.142.now), channel_id=1, source_target_pairs={{1,2},{2,1},{3,4},{4,3},{5,6},{6,5},{7,8},{8,7},{9,10},{10,9},{11,... | collective-permute-start | bytes 1966088 | tf_op jit(solution)/shard_map/ppermute | solution.py:509
  36.0 0.0 collective-permute-done.2.near
  36.0 1.3 %shard_map.144 = (f32[8,64,128]{2,1,0:T(8,128)S(1)}, f32[8,64,128]{2,1,0:T(8,128)S(1)}, f32[8,64,128]{2,1,0:T(8,128)S(1)}) custom-call(f32[8,4]{1,0:T(8,128)S(1)} %copy.24.wavelet, s32[8]{0:T(128)S(1)} %get-tuple-element.34.spot_x, s32[8]{0:T(128)S(1)} %get-tuple-element.35.spot_z, s32[8]{0:T(128)S(1)} %get-tuple-element.36.spot_y, ...), custom_call_target="tpu_custom_call" | custom-call | flops 5898240 | bytes 2097152 | tf_op jit(solution)/shard_map/pallas_call | solution.py:27
  37.3 7.0 %collective-permute-done.1.far = f32[20,64,128]{2,1,0:T(8,128)S(1)} collective-permute-done((f32[20,64,128]{2,1,0:T(8,128)S(1)}, f32[20,64,128]{2,1,0:T(8,128)S(1)}, u32[]{:S(2)}, u32[]{:S(2)}) %collective-permute-start.1) | collective-permute-done | bytes 655392 | tf_op jit(solution)/shard_map/ppermute | solution.py:509
  44.3 1.7 %shard_map.145 = (f32[8,64,128]{2,1,0:T(8,128)S(1)}, f32[8,64,128]{2,1,0:T(8,128)S(1)}) custom-call(f32[8,4]{1,0:T(8,128)S(1)} %copy.24.wavelet, s32[8]{0:T(128)S(1)} %get-tuple-element.34.spot_x, s32[8]{0:T(128)S(1)} %get-tuple-element.35.spot_z, s32[8]{0:T(128)S(1)} %get-tuple-element.36.spot_y, s32[8]{0:T(128)S(1)} %get-tuple-element.37.depth_at, ...), custom_call_target="tpu_custom_call" | custom-call | flops 5898240 | bytes 2097152 | tf_op jit(solution)/shard_map/pallas_call | solution.py:27
  46.0 7.3 %collective-permute-start.3 = (f32[8,64,128]{2,1,0:T(8,128)S(1)}, f32[8,64,128]{2,1,0:T(8,128)S(1)}, u32[]{:S(2)}, u32[]{:S(2)}) collective-permute-start(f32[8,64,128]{2,1,0:T(8,128)S(1)} %get-tuple-element.52.new_high), channel_id=1, source_target_pairs={{1,2},{2,1},{3,4},{4,3},{5,6},{6,5},{7,8},{8,7},{9,10},{10,9},{11,... | collective-permute-start | bytes 786440 | tf_op jit(solution)/shard_map/ppermute | solution.py:524
  53.3 2.2 %shard_map.146 = (f32[8,64,128]{2,1,0:T(8,128)S(1)}, f32[16,64,128]{2,1,0:T(8,128)S(1)}, f32[8,64,128]{2,1,0:T(8,128)S(1)}) custom-call(f32[8,4]{1,0:T(8,128)S(1)} %copy.24.wavelet, s32[8]{0:T(128)S(1)} %get-tuple-element.34.spot_x, s32[8]{0:T(128)S(1)} %get-tuple-element.35.spot_z, s32[8]{0:T(128)S(1)} %get-tuple-element.36.spot_y, ...), custom_call_target="tpu_custom_call" | custom-call | flops 5898240 | bytes 2097152 | tf_op jit(solution)/shard_map/pallas_call | solution.py:27
  55.5 2.2 %all-gather.1 = f32[16,64,128]{2,1,0:T(8,128)S(1)} all-gather(f32[8,64,128]{2,1,0:T(8,128)S(1)} %get-tuple-element.55), channel_id=3, replica_groups={{0,1},{2,3},{4,5},{6,7},{8,9},{10,11},{12,13},{14,15},{16,17},{18,19},{..., dimensions={0}, use_global_device_ids=true | all-gather | bytes 786432 | tf_op jit(solution)/shard_map/all_gather | solution.py:529
  57.7 1.8 %collective-permute-done.3.far = f32[8,64,128]{2,1,0:T(8,128)S(1)} collective-permute-done((f32[8,64,128]{2,1,0:T(8,128)S(1)}, f32[8,64,128]{2,1,0:T(8,128)S(1)}, u32[]{:S(2)}, u32[]{:S(2)}) %collective-permute-start.3) | collective-permute-done | bytes 262176 | tf_op jit(solution)/shard_map/ppermute | solution.py:524
  59.4 0.9 %shard_map.147 = (f32[16,64,128]{2,1,0:T(8,128)S(1)}, f32[8,16,8,128]{3,2,1,0:T(8,128)S(1)}) custom-call(s32[8,8]{1,0:T(8,128)S(1)} %get-tuple-element.33.tiles, f32[8,4]{1,0:T(8,128)S(1)} %copy.24.wavelet, s32[8]{0:T(128)S(1)} %get-tuple-element.34.spot_x, s32[8]{0:T(128)S(1)} %get-tuple-element.35.spot_z, s32[8]{0:T(128)S(1)} %get-tuple-element.36.spot_y, ...), custom_call_target="tpu_custom_call" | custom-call | flops 5898240 | bytes 2097152 | tf_op jit(solution)/shard_map/pallas_call | solution.py:27
  60.4 13.0 %all_to_all.10.got = f32[8,16,8,128]{3,2,1,0:T(8,128)S(1)} all-to-all(f32[8,16,8,128]{3,2,1,0:T(8,128)S(1)} %get-tuple-element.58), channel_id=1, replica_groups=mesh['shot'=8,'slab'=64] {'shot'}, dimensions={0} | all-to-all | bytes 1048576 | tf_op jit(solution)/shard_map/all_to_all | solution.py:534
  73.4 1.8 %shard_map.148 = (f32[512,128]{1,0:T(8,128)}, f32[512,128]{1,0:T(8,128)}, f32[512,128]{1,0:T(8,128)}) custom-call(s32[8,8]{1,0:T(8,128)S(1)} %get-tuple-element.33.tiles, f32[8,16,8,128]{3,2,1,0:T(8,128)S(1)} %all_to_all.10.got, f32[16,64,128]{2,1,0:T(8,128)S(1)} %get-tuple-element.59.new), custom_call_target="tpu_custom_call" | custom-call | flops 5898240 | bytes 2097152 | tf_op jit(solution)/shard_map/pallas_call | solution.py:27
Async XLA Ops:
  3.0 15.8 %copy-start.3 = (f32[8,4]{0,1:T(4,128)S(1)}, f32[8,4]{0,1:T(4,128)}, u32[]{:S(2)}) copy-start(f32[8,4]{0,1:T(4,128)} %param.18) | copy-start | bytes 388
  3.0 15.9 %copy-start.1 = (f32[1,64,8,128]{3,2,1,0:T(8,128)S(1)}, f32[1,64,8,128]{3,2,1,0:T(8,128)}, u32[]{:S(2)}) copy-start(f32[1,64,8,128]{3,2,1,0:T(8,128)} %param.12) | copy-start | bytes 786436
  3.0 15.9 %copy-start.2 = (f32[1,64,8,128]{3,2,1,0:T(8,128)S(1)}, f32[1,64,8,128]{3,2,1,0:T(8,128)}, u32[]{:S(2)}) copy-start(f32[1,64,8,128]{3,2,1,0:T(8,128)} %param.15) | copy-start | bytes 786436
  3.0 18.9 %all-to-all-start = ((f32[8,16,8,128]{3,2,1,0:T(8,128)}), f32[8,16,8,128]{3,2,1,0:T(8,128)S(1)}, u32[]{:S(2)}, u32[]{:S(2)}) async-start(f32[8,16,8,128]{3,2,1,0:T(8,128)} %get-tuple-element.39), calls=%async_computation | async-start | bytes 1048576 | tf_op jit(solution)/shard_map/all_to_all | solution.py:497
  8.2 14.8 %collective-permute-start = (f32[8,64,128]{2,1,0:T(8,128)S(1)}, f32[8,64,128]{2,1,0:T(8,128)S(1)}, u32[]{:S(2)}, u32[]{:S(2)}) collective-permute-start(f32[8,64,128]{2,1,0:T(8,128)S(1)} %get-tuple-element.38), channel_id=1, source_target_pairs={{1,2},{2,1},{3,4},{4,3},{5,6},{6,5},{7,8},{8,7},{9,10},{10,9},{11,... | collective-permute-start | bytes 786440 | tf_op jit(solution)/shard_map/ppermute | solution.py:498
  22.0 1.0 %copy-start = (bf16[1,4,64,128]{3,2,1,0:T(8,128)(2,1)S(1)}, bf16[1,4,64,128]{3,2,1,0:T(8,128)(2,1)}, u32[]{:S(2)}) copy-start(bf16[1,4,64,128]{3,2,1,0:T(8,128)(2,1)} %param.23) | copy-start | bytes 196612
  24.7 11.4 %collective-permute-start.2 = (f32[20,64,128]{2,1,0:T(8,128)S(1)}, f32[20,64,128]{2,1,0:T(8,128)S(1)}, u32[]{:S(2)}, u32[]{:S(2)}) collective-permute-start(f32[20,64,128]{2,1,0:T(8,128)S(1)} %get-tuple-element.48), channel_id=1, source_target_pairs={{0,1},{1,0},{2,3},{3,2},{4,5},{5,4},{6,7},{7,6},{8,9},{9,8},{10,11... | collective-permute-start | bytes 1966088 | tf_op jit(solution)/shard_map/ppermute | solution.py:513
  26.6 17.7 %collective-permute-start.1 = (f32[20,64,128]{2,1,0:T(8,128)S(1)}, f32[20,64,128]{2,1,0:T(8,128)S(1)}, u32[]{:S(2)}, u32[]{:S(2)}) collective-permute-start(f32[20,64,128]{2,1,0:T(8,128)S(1)} %shard_map.142.now), channel_id=1, source_target_pairs={{1,2},{2,1},{3,4},{4,3},{5,6},{6,5},{7,8},{8,7},{9,10},{10,9},{11,... | collective-permute-start | bytes 1966088 | tf_op jit(solution)/shard_map/ppermute | solution.py:509
  46.0 13.4 %collective-permute-start.3 = (f32[8,64,128]{2,1,0:T(8,128)S(1)}, f32[8,64,128]{2,1,0:T(8,128)S(1)}, u32[]{:S(2)}, u32[]{:S(2)}) collective-permute-start(f32[8,64,128]{2,1,0:T(8,128)S(1)} %get-tuple-element.52.new_high), channel_id=1, source_target_pairs={{1,2},{2,1},{3,4},{4,3},{5,6},{6,5},{7,8},{8,7},{9,10},{10,9},{11,... | collective-permute-start | bytes 786440 | tf_op jit(solution)/shard_map/ppermute | solution.py:524

commit v5 on v4

v5 whole, which is shorter than its diff:
```python
import jax
import jax.numpy as jnp
from jax import lax
from jax.experimental import pallas as pl
from jax.experimental.pallas import tpu as pltpu
from jax.sharding import PartitionSpec as P


BX = 8
KT = 8
STEPS = 4
CAP = 2
REACH = 4
PAD = 8
VMEM = pltpu.VMEM
SMEM = pltpu.SMEM
HBM = pltpu.HBM

SCALE = 5040.0
TAPS = (-43050.0, 8064.0, -1008.0, 128.0, -9.0)


def call(body, outs, in_spaces, *args, scratch=()):
    outs = [o if isinstance(o[0], tuple) else (o, VMEM) for o in outs]
    outs = [o if len(o) == 3 else o + (jnp.float32,) for o in outs]
    size = 8 * 64 * 128
    return pl.pallas_call(
        body,
        out_shape=[jax.ShapeDtypeStruct(s, t) for s, _, t in outs],
        in_specs=[pl.BlockSpec(memory_space=s) for s in in_spaces],
        out_specs=[pl.BlockSpec(memory_space=m) for _, m, _ in outs],
        scratch_shapes=list(scratch),
        compiler_params=pltpu.CompilerParams(vmem_limit_bytes=24 * 1024 * 1024),
        cost_estimate=pl.CostEstimate(
            flops=90 * size, bytes_accessed=32 * size, transcendentals=0
        ),
    )(*args)


def is_odd():
    return lax.rem(lax.axis_index("slab"), 2) == 1


def partner():
    return jnp.where(is_odd(), 0, 1)


def z_of(plane, depth):
    return jnp.where(is_odd(), plane, depth - 1 - plane)


def tap_of(reach):
    weight = jnp.zeros(reach.shape, jnp.float32)
    for r in range(1, REACH + 1):
        weight = jnp.where(reach == r, TAPS[r], weight)
    return weight


def along_y_matrix(size_y):
    shape = (2 * size_y, size_y)
    row = lax.rem(lax.broadcasted_iota(jnp.int32, shape, 0), size_y)
    return tap_of(jnp.abs(row - lax.broadcasted_iota(jnp.int32, shape, 1))).astype(jnp.bfloat16)


def along_y(planes, to_y):
    rows = planes.reshape(-1, planes.shape[2])
    high = rows.astype(jnp.bfloat16)
    low = (rows - high.astype(jnp.float32)).astype(jnp.bfloat16)
    sums = jnp.dot(
        jnp.concatenate([high, low], axis=1), to_y, preferred_element_type=jnp.float32
    )
    return sums.reshape(planes.shape)


def clear_edges(padded):
    count, rows, size_y = padded.shape
    zeros = jnp.zeros((count, PAD, size_y), jnp.float32)
    padded[:, pl.ds(0, PAD)] = zeros
    padded[:, pl.ds(rows - PAD, PAD)] = zeros


def full_sums(padded, planes, first, plane_at, to_y):
    count, size_x, _ = planes.shape
    padded[pl.ds(0, count), pl.ds(PAD, size_x)] = planes
    lines = along_y(planes, to_y)
    sums = []
    for p in range(count):
        total = lines[p] + TAPS[0] * planes[p]
        for r in range(1, REACH + 1):
            terms = padded[p, pl.ds(PAD + r, size_x)] + padded[p, pl.ds(PAD - r, size_x)]
            for other in (plane_at(first + p + r), plane_at(first + p - r)):
                if other is not None:
                    terms += other
            total += TAPS[r] * terms
        sums.append(total)
    return sums


def beyond_sums(plane, plane_at):
    total = 0.0
    for r in range(1, REACH + 1):
        for other in (plane_at(plane + r), plane_at(plane - r)):
            if other is not None:
                total += TAPS[r] * other
    return total


def sources_at(f, number, step, sources):
    where, spots, traces = sources
    added = traces[STEPS - 1 - step].astype(jnp.float32) if f else spots[step]
    here = (where[f] == float(number))[None]
    return jnp.where(here, added.reshape(-1, 8, added.shape[1]), 0.0).reshape(added.shape)


def start_kernel(
    src_in, rec_in, vel_in, tiles_in, x_in, z_in, y_in, depth_in, wavelet_in,
    send, to_far, src, rec, pick, put, where, spots,
    src_raw, rec_raw, vel, tiles, spot_x, spot_z, spot_y, depth_at, wavelet, sems, send_sems,
):
    shot = lax.axis_index("shot")
    moves = [(tiles_in, tiles), (vel_in, vel), (src_in, src_raw), (rec_in, rec_raw)]
    moves += [(x_in, spot_x), (z_in, spot_z), (y_in, spot_y), (depth_in, depth_at)]
    moves += [(wavelet_in, wavelet)]
    copies = [pltpu.make_async_copy(a, b, sems.at[i]) for i, (a, b) in enumerate(moves)]
    for copy in copies:
        copy.start()
    depth, size_x, size_y = src.shape
    rows = BX * depth
    held = vel.shape[0] // rows
    copies[0].wait()
    copies[1].wait()
    places = []
    for g in range(send.shape[0]):
        before = jnp.int32(0)
        for k in range(KT):
            before += (tiles[g, k] < shot * BX).astype(jnp.int32)
        for j in range(CAP):
            own = tiles[g, jnp.minimum(before + j, KT - 1)] - shot * BX
            filled = (before + j < KT) & (own >= 0) & (own < held)
            places.append(jnp.where(filled, own, -1))
            at = pl.multiple_of(jnp.clip(own, 0, held - 1) * rows, rows)
            copy = pltpu.make_async_copy(
                vel.at[pl.ds(at, rows)], send.at[g, j], send_sems.at[g * CAP + j]
            )
            copy.start()
            copies.append(copy)
    for f, (raw, field) in enumerate(((src_raw, src), (rec_raw, rec))):
        copies[2 + f].wait()
        for p in range(depth):
            plane = raw[pl.ds(z_of(p, depth), size_x, stride=depth)]
            field[p] = plane
            if p >= depth - REACH:
                to_far[f * REACH + p - (depth - REACH)] = plane
    tile = (8, size_y)
    for c, own in enumerate(places):
        own = jnp.full(tile, own)
        for t in range(held):
            put[c, t] = jnp.where(own == t, 1.0, 0.0)
    previous = jnp.int32(-1)
    for k in range(KT):
        owner = lax.shift_right_logical(tiles[shot, k], 3)
        place = owner * CAP + (previous == owner).astype(jnp.int32)
        previous = owner
        place = jnp.full(tile, place)
        for c in range(pick.shape[1]):
            pick[k, c] = jnp.where(place == c, 1.0, 0.0)
    for copy in copies[4:9]:
        copy.wait()
    first = lax.axis_index("slab") * depth
    for f, local in enumerate((spot_z[shot] - first, depth_at[shot] - first)):
        where[f] = jnp.full(tile, z_of(local, depth)).astype(jnp.float32)
    row = lax.broadcasted_iota(jnp.int32, (size_x, size_y), 0)
    lane = lax.broadcasted_iota(jnp.int32, (size_x, size_y), 1)
    here = (row == spot_x[shot]) & (lane == spot_y[shot])
    for step in range(STEPS):
        spots[step] = jnp.where(here, wavelet[step, shot], 0.0)
    for copy in copies[9:]:
        copy.wait()


def first_interior_kernel(src, rec, src_old, rec_old, to_near, sums, base, to_y, padded):
    depth, size_x, size_y = src.shape
    to_y[...] = along_y_matrix(size_y)
    clear_edges(padded)
    for f, (field, old) in enumerate(((src, src_old), (rec, rec_old))):

        def plane_at(m):
            return field[m] if 0 <= m < depth else None

        for first in range(0, depth, REACH):
            planes = field[pl.ds(first, REACH)]
            if first == 0:
                to_near[pl.ds(f * REACH, REACH)] = planes
            for i, total in enumerate(full_sums(padded, planes, first, plane_at, to_y[...])):
                p = first + i
                sums[f * depth + p] = total
                before = old[pl.ds(z_of(p, depth), size_x, stride=depth)]
                base[f * depth + p] = 2.0 * planes[i] - before


def rate_kernel(pick, vel_got, near, sums, base, where, spots, traces, rate, part):
    mine = partner()
    depth = rate.shape[0]
    count = pick.shape[1]
    for p in range(depth):
        at = pl.ds(z_of(p, depth), BX, stride=depth)
        tiles = [vel_got[c // CAP, c % CAP, at] for c in range(count)]
        for k in range(KT):
            tile = 0.0
            for c in range(k, count - (KT - 1 - k)):
                tile += pick[k, c] * tiles[c]
            rate[p, pl.ds(k * BX, BX)] = tile * tile * (1.0 / SCALE)
    for f in range(2):

        def plane_at(m):
            return near[mine, f * REACH - 1 - m] if m < 0 else None

        for p in range(depth):
            total = sums[f * depth + p]
            if p < REACH:
                total += beyond_sums(p, plane_at)
            added = sources_at(f, p, 0, (where, spots, traces))
            part[f * depth + p] = base[f * depth + p] + rate[p] * total + added


def first_kernel(far, part, rate, now):
    depth = rate.shape[0]
    for f in range(2):

        def plane_at(m):
            return far[f * REACH + REACH - 1 - (m - depth)] if m >= depth else None

        for p in range(depth):
            value = part[f * depth + p]
            if p >= depth - REACH:
                value += rate[p] * beyond_sums(p, plane_at)
            now[f * depth + p] = value
    now[pl.ds(2 * depth, REACH)] = rate[pl.ds(depth - REACH, REACH)]


def wide_interior_kernel(
    now, src_old, rec_old, rate, to_y, src_near, rec_near, base, padded
):
    depth = rate.shape[0]
    clear_edges(padded)
    src_near[pl.ds(0, depth)] = now[pl.ds(0, depth)]
    src_near[pl.ds(depth, REACH)] = rate[pl.ds(0, REACH)]
    rec_near[...] = now[pl.ds(depth, depth)]
    for f, old in enumerate((src_old, rec_old)):

        def plane_at(m):
            return now[f * depth + m] if 0 <= m < depth else None

        for first in range(0, depth, REACH):
            planes = now[pl.ds(f * depth + first, REACH)]
            for i, total in enumerate(full_sums(padded, planes, first, plane_at, to_y[...])):
                p = first + i
                base[f * depth + p] = 2.0 * planes[i] - old[p] + rate[p] * total


def wide_near_kernel(
    where, spots, traces, src_near, rec_near, near_old, now, base, rate, to_y,
    mid_near, mid_low, mid_part, padded,
):
    depth = rate.shape[0]
    mine = partner()
    sources = (where, spots, traces)
    clear_edges(padded)
    for f, near in enumerate((src_near, rec_near)):

        def plane_at(m):
            if m >= 0:
                return now[f * depth + m]
            return near[mine, -1 - m]

        planes = near[mine, pl.ds(0, REACH)]
        totals = full_sums(padded, planes, 0, lambda m: plane_at(-1 - m), to_y[...])
        for i, total in enumerate(totals):
            value = 2.0 * planes[i] - near_old[mine, f * REACH + i]
            value += src_near[mine, depth + i] * total
            mid_near[f * REACH + i] = value + sources_at(f, -1 - i, 1, sources)
        for p in range(depth):
            value = base[f * depth + p] + sources_at(f, p, 1, sources)
            if p < REACH:
                share = beyond_sums(p, lambda m: plane_at(m) if m < 0 else None)
                mid_low[f * REACH + p] = value + rate[p] * share
            else:
                mid_part[f * REACH + p - REACH] = value


def wide_far_kernel(
    where, spots, traces, far, far_old, now, mid_low, mid_part, rate, to_y,
    mid_high, to_far, mid_far, padded,
):
    depth = rate.shape[0]
    high = depth - REACH
    sources = (where, spots, traces)
    clear_edges(padded)
    for f in range(2):

        def plane_at(m):
            if m < depth:
                return now[f * depth + m]
            return far[f * depth + 2 * depth - 1 - m]

        def mid_at(m):
            if m < high:
                return mid_low[f * REACH + m]
            return mid_high[f * REACH + m - high] if m < depth else mid_far[f * REACH + m - depth]

        planes = jnp.stack([plane_at(depth + i) for i in range(REACH)])
        totals = full_sums(padded, planes, depth, plane_at, to_y[...])
        for i, total in enumerate(totals):
            value = 2.0 * planes[i] - far_old[f * REACH + REACH - 1 - i]
            value += far[2 * depth + REACH - 1 - i] * total
            mid_far[f * REACH + i] = value + sources_at(f, depth + i, 1, sources)
        for p in range(high, depth):
            share = beyond_sums(p, lambda m: plane_at(m) if m >= depth else None)
            mid_high[f * REACH + p - high] = mid_part[f * REACH + p - high] + rate[p] * share
        planes = mid_high[pl.ds(f * REACH, REACH)]
        for i, total in enumerate(full_sums(padded, planes, high, mid_at, to_y[...])):
            p = high + i
            value = 2.0 * planes[i] - now[f * depth + p] + rate[p] * total
            to_far[f * REACH + i] = value + sources_at(f, p, 2, sources)


def interior_kernel(
    where, spots, traces, now, mid_near, mid_low, mid_high, new_high, rate, to_y,
    new_low, base, partial, padded,
):
    depth = rate.shape[0]
    high = depth - REACH
    sources = (where, spots, traces)
    clear_edges(padded)

    def mid_at(f, m):
        if m < 0:
            return mid_near[f * REACH - 1 - m]
        return mid_low[f * REACH + m] if m < high else mid_high[f * REACH + m - high]

    def new_at(f, m):
        return new_low[f * REACH + m] if m < high else new_high[f * REACH + m - high]

    for f in range(2):
        planes = mid_low[pl.ds(f * REACH, REACH)]
        totals = full_sums(padded, planes, 0, lambda m: mid_at(f, m), to_y[...])
        for p, total in enumerate(totals):
            value = 2.0 * planes[p] - now[f * depth + p] + rate[p] * total
            new_low[f * REACH + p] = value + sources_at(f, p, 2, sources)
    for f in range(2):
        for first, part in ((0, new_low), (high, new_high)):
            planes = part[pl.ds(f * REACH, REACH)]

            def plane_at(m):
                return new_at(f, m) if 0 <= m < depth else None

            for i, total in enumerate(full_sums(padded, planes, first, plane_at, to_y[...])):
                p = first + i
                value = 2.0 * planes[i] - mid_at(f, p) + rate[p] * total
                base[f * depth + p] = value + sources_at(f, p, 3, sources)
    for p in range(depth):
        total = new_at(0, p) * now[depth + p] + mid_at(0, p) * mid_at(1, p)
        partial[p] = total + now[p] * new_at(1, p)


def last_kernel(pick, far, near, base, rate, partial, src_first, rec_first, new, send):
    mine = partner()
    depth = rate.shape[0]
    count = pick.shape[1]
    for p in range(depth):
        fields = []
        for f in range(2):

            def plane_at(m):
                if m < 0:
                    return near[mine, f * REACH - 1 - m]
                return far[f * REACH + REACH - 1 - (m - depth)] if m >= depth else None

            value = base[f * depth + p] + rate[p] * beyond_sums(p, plane_at)
            new[f * depth + p] = value
            fields.append(value)
        image = partial[p] + fields[0] * rec_first[p] + src_first[p] * fields[1]
        for c in range(count):
            total = 0.0
            for k in range(max(0, c - (count - KT)), min(KT - 1, c) + 1):
                total += pick[k, c] * image[k * BX : (k + 1) * BX]
            send[c // CAP, (c % CAP) * depth + p] = total


def gather_kernel(put, got, new, out, src_out, rec_out, out_rows, src_rows, rec_rows, sems):
    depth = new.shape[0] // 2
    size_x = new.shape[1]
    count, held = put.shape[:2]
    copies = []
    for f, (rows, to) in enumerate(((src_rows, src_out), (rec_rows, rec_out))):
        for p in range(depth):
            rows[pl.ds(z_of(p, depth), size_x, stride=depth)] = new[f * depth + p]
        copies.append(pltpu.make_async_copy(rows, to, sems.at[f]))
        copies[-1].start()
    for t in range(held):
        for p in range(depth):
            total = 0.0
            for c in range(count):
                total += put[c, t] * got[c // CAP, (c % CAP) * depth + p]
            out_rows[pl.ds(t * BX * depth + z_of(p, depth), BX, stride=depth)] = total
    copies.append(pltpu.make_async_copy(out_rows, out, sems.at[2]))
    copies[-1].start()
    for copy in copies:
        copy.wait()


def local(
    src_prev,
    src_cur,
    rec_cur,
    rec_next,
    velocity,
    aperture_tiles,
    wavelet,
    src_x,
    src_z,
    src_y,
    rec_depth,
    rec_data,
):
    slabs = lax.axis_size("slab")
    shots = lax.axis_size("shot")
    far_pairs = []
    for i in range(1, slabs - 1, 2):
        far_pairs += [(i, i + 1), (i + 1, i)]
    near_groups = [[i, i + 1] for i in range(0, slabs, 2)]

    def flat(array):
        return array.reshape(-1, array.shape[-1])

    _, size_x, depth, size_y = src_cur.shape
    raw = (depth * size_x, size_y)
    model = (velocity.shape[0] * depth, size_y)
    one, two = (depth, size_x, size_y), (2 * depth, size_x, size_y)
    halo = (2 * REACH, size_x, size_y)
    wide = (2 * depth + REACH, size_x, size_y)
    buffer = (shots, CAP * depth, BX, size_y)
    dma = pltpu.SemaphoreType.DMA
    padded = VMEM((REACH, size_x + 2 * PAD, size_y), jnp.float32)
    count = shots * CAP
    held = velocity.shape[0] // BX
    given = (flat(src_cur), flat(rec_cur), flat(velocity), aperture_tiles)
    given += (src_x, src_z, src_y, rec_depth, wavelet.T)
    scalars = [SMEM(a.shape, a.dtype) for a in given[3:]]
    send, to_far, src, rec, pick, put, where, spots = call(
        start_kernel,
        [
            ((shots, CAP, BX * depth, size_y), HBM), halo, one, one, (KT, count, 8, size_y),
            (count, held, 8, size_y), (2, 8, size_y), (STEPS, size_x, size_y),
        ],
        [HBM] * 9, *[pltpu.with_memory_space_constraint(a, HBM) for a in given],
        scratch=[
            VMEM(raw, jnp.float32), VMEM(raw, jnp.float32), VMEM(model, jnp.float32), *scalars,
            dma((9,)), dma((count,)),
        ],
    )
    sources = (where, spots, rec_data[0])

    vel_got = lax.all_to_all(send, "shot", 0, 0)
    far = lax.ppermute(to_far, "slab", far_pairs)
    to_near, sums, base, to_y = call(
        first_interior_kernel, [halo, two, two, ((2 * size_y, size_y), VMEM, jnp.bfloat16)],
        [VMEM] * 4, src, rec, flat(src_prev), flat(rec_next), scratch=[padded],
    )
    near = lax.all_gather(to_near, "slab", axis_index_groups=near_groups)
    rate, part = call(
        rate_kernel, [one, two], [VMEM] * 8, pick, vel_got, near, sums, base, *sources
    )
    (now,) = call(first_kernel, [wide], [VMEM] * 3, far, part, rate)

    wide_far = lax.ppermute(now, "slab", far_pairs)
    src_near, rec_near, base = call(
        wide_interior_kernel, [(depth + REACH, size_x, size_y), one, two], [VMEM] * 5,
        now, src, rec, rate, to_y, scratch=[padded],
    )
    src_near = lax.all_gather(src_near, "slab", axis_index_groups=near_groups)
    rec_near = lax.all_gather(rec_near, "slab", axis_index_groups=near_groups)
    mid_near, mid_low, mid_part = call(
        wide_near_kernel, [halo] * 3, [VMEM] * 10,
        *sources, src_near, rec_near, near, now, base, rate, to_y, scratch=[padded],
    )
    mid_high, new_high = call(
        wide_far_kernel, [halo] * 2, [VMEM] * 10,
        *sources, wide_far, far, now, mid_low, mid_part, rate, to_y,
        scratch=[VMEM(halo, jnp.float32), padded],
    )

    far = lax.ppermute(new_high, "slab", far_pairs)
    new_low, base, partial = call(
        interior_kernel, [halo, two, one], [VMEM] * 10,
        *sources, now, mid_near, mid_low, mid_high, new_high, rate, to_y, scratch=[padded],
    )
    near = lax.all_gather(new_low, "slab", axis_index_groups=near_groups)
    new, send = call(
        last_kernel, [two, buffer], [VMEM] * 8,
        pick, far, near, base, rate, partial, src, rec,
    )
    image_got = lax.all_to_all(send, "shot", 0, 0)
    image, src, rec = call(
        gather_kernel, [(model, HBM), (raw, HBM), (raw, HBM)], [VMEM] * 3, put, image_got, new,
        scratch=[
            VMEM(model, jnp.float32), VMEM(raw, jnp.float32), VMEM(raw, jnp.float32), dma((3,)),
        ],
    )
    return image.reshape(velocity.shape), src.reshape(src_cur.shape), rec.reshape(src_cur.shape)


def solution(mesh):
    wave = P("shot", None, "slab", None)
    model = P("shot", "slab", None)
    return jax.shard_map(
        local,
        mesh=mesh,
        in_specs=(wave,) * 4 + (model,) + (P(),) * 6 + (P("shot", None, None, None),),
        out_specs=(model, wave, wave),
        check_vma=False,
    )
```

time: 75.6 us -> 71.8 us (0.950)
  starting transfers between devices: 34.4 us -> 28.3 us
  blocking collectives: 17.4 us -> 22.5 us
  Pallas kernels: 13.6 us -> 9.24 us
  local copies, waits for them, and re-layouts: 0.1 us -> 3.7 us
  waiting for transfers between devices: 8.98 us -> 6.79 us
    all_gather x0 -> x2, blocking collectives: none -> 4.54 us  [the longest x1 2.36 us: local(): src_near = lax.all_gather(src_near, 'slab', axis_index_groups=near_groups)]
    pallas_call x10, Pallas kernels: 13.6 us -> 9.24 us  [call(): pl.pallas_call(body, out_shape=[jax.ShapeDtypeStruct(s, t) for s, _, t in...]
    ppermute x1, waiting for transfers between devices: 6.98 us -> 3.02 us  [local(): wide_far = lax.ppermute(now, 'slab', far_pairs)]
    unnamed x9 -> x14, local copies, waits for them, and re-layouts: 0.1 us -> 3.7 us
    ppermute x1, starting transfers between devices: 9.43 us -> 6.24 us  [local(): wide_far = lax.ppermute(now, 'slab', far_pairs)]
    ppermute x1, waiting for transfers between devices: 1.78 us -> 3.76 us  [local(): far = lax.ppermute(new_high, 'slab', far_pairs)]
    ppermute x1 -> x0, starting transfers between devices: 1.92 us -> none  [local(): wide_near = lax.ppermute(to_near, 'slab', near_pairs)]
    ppermute x1, starting transfers between devices: 7.25 us -> 6.25 us  [local(): far = lax.ppermute(new_high, 'slab', far_pairs)]
  transfers between devices with their start and end apart: 5 -> 4, of which waited for: 3 -> 2; matrix products, arithmetic and copies ran while one was open for 0% -> 0% of each run, Pallas kernels for 7% -> 6%
where the time goes in v5:
time: 71.8 us; the launch traced here: 71.3 us
  starting transfers between devices  28.3 us (39%)
  blocking collectives  22.5 us (31%)
  Pallas kernels  9.24 us (13%)
  waiting for transfers between devices  6.79 us (9%)
  local copies, waits for them, and re-layouts  3.7 us (5%)
  between operations  0.77 us (1%)
    all_to_all x1, blocking collectives, local(): image_got = lax.all_to_all(send, 'shot', 0, 0)  13.5 us
    ppermute x1, starting transfers between devices, local(): far = lax.ppermute(to_far, 'slab', far_pairs)  10.6 us
    pallas_call x10, Pallas kernels, call(): pl.pallas_call(body, out_shape=[jax.ShapeDtypeStruct(s, t) for s, _, t in...  9.24 us
    ppermute x1, starting transfers between devices, local(): far = lax.ppermute(new_high, 'slab', far_pairs)  6.25 us
    ppermute x1, starting transfers between devices, local(): wide_far = lax.ppermute(now, 'slab', far_pairs)  6.24 us
    all_to_all x1, starting transfers between devices, local(): vel_got = lax.all_to_all(send, 'shot', 0, 0)  5.16 us
    ppermute x1, waiting for transfers between devices, local(): far = lax.ppermute(new_high, 'slab', far_pairs)  3.76 us
    unnamed x14, local copies, waits for them, and re-layouts  3.7 us
  transfers between devices with their start and end apart: 4, of which 2 were waited for; matrix products, arithmetic and copies ran while one was open for 0% of the time, Pallas kernels for 6%

profile of v5, /device:TPU:16, one launch (start us, length us, event | category | flops | bytes accessed | tf_op | source)
XLA Modules:
  0.0 71.3 jit_solution(17471875519802652473)
XLA Ops:
  0.6 2.0 %shard_map.139 = (f32[8,2,64,128]{3,2,1,0:T(8,128)}, f32[8,64,128]{2,1,0:T(8,128)S(1)}, f32[8,64,128]{2,1,0:T(8,128)S(1)}, f32[8,64,128]{2,1,0:T(8,128)S(1)}, f3...) custom-call(f32[512,128]{1,0:T(8,128)} %bitcast.25, ...), custom_call_target="tpu_custom_call" | custom-call | flops 5898240 | bytes 2097152 | tf_op jit(solution)/shard_map/pallas_call | solution.py:27
  2.6 0.0 copy-start.5
  2.6 0.0 copy-start.6
  2.6 5.2 %all-to-all-start = ((f32[8,2,64,128]{3,2,1,0:T(8,128)}), f32[8,2,64,128]{3,2,1,0:T(8,128)S(1)}, u32[]{:S(2)}, u32[]{:S(2)}) async-start(f32[8,2,64,128]{3,2,1,0:T(8,128)} %get-tuple-element.38), calls=%async_computation | async-start | bytes 1048576 | tf_op jit(solution)/shard_map/all_to_all | solution.py:464
  7.8 10.6 %collective-permute-start = (f32[8,64,128]{2,1,0:T(8,128)S(1)}, f32[8,64,128]{2,1,0:T(8,128)S(1)}, u32[]{:S(2)}, u32[]{:S(2)}) collective-permute-start(f32[8,64,128]{2,1,0:T(8,128)S(1)} %get-tuple-element.37), channel_id=1, source_target_pairs={{1,2},{2,1},{3,4},{4,3},{5,6},{6,5},{7,8},{8,7},{9,10},{10,9},{11,... | collective-permute-start | bytes 786440 | tf_op jit(solution)/shard_map/ppermute | solution.py:465
  18.4 0.0 copy-done.5
  18.4 0.9 %shard_map.140 = (f32[8,64,128]{2,1,0:T(8,128)S(1)}, f32[16,64,128]{2,1,0:T(8,128)S(1)}, f32[16,64,128]{2,1,0:T(8,128)S(1)}, bf16[256,128]{1,0:T(8,128)(2,1)S(1)}) custom-call(f32[8,64,128]{2,1,0:T(8,128)S(1)} %get-tuple-element.39.src.src_old.src_first, f32[8,64,128]{2,1,0:T(8,128)S(1)} %get-tuple-element.40.rec.rec_old.rec_first, f32[512,128]{1,0:T(8,128)S(1)} %bitcast.23, ...), custom_call_target="tpu_custom_call" | custom-call | flops 5898240 | bytes 2097152 | tf_op jit(solution)/shard_map/pallas_call | solution.py:27
  19.3 0.0 copy-start.1
  19.3 0.8 %copy-done.1 = f32[16,64,128]{2,1,0:T(8,128)} copy-done((f32[16,64,128]{2,1,0:T(8,128)}, f32[16,64,128]{2,1,0:T(8,128)S(1)}, u32[]{:S(2)}) %copy-start.1) | copy-done | bytes 524312
  20.1 0.8 %copy-done.3 = f32[16,64,128]{2,1,0:T(8,128)} copy-done((f32[16,64,128]{2,1,0:T(8,128)}, f32[16,64,128]{2,1,0:T(8,128)S(1)}, u32[]{:S(2)}) %copy-start.3) | copy-done | bytes 524312
  20.9 2.3 %all-gather = f32[16,64,128]{2,1,0:T(8,128)S(1)} all-gather(f32[8,64,128]{2,1,0:T(8,128)S(1)} %get-tuple-element.41), channel_id=2, replica_groups={{0,1},{2,3},{4,5},{6,7},{8,9},{10,11},{12,13},{14,15},{16,17},{18,19},{..., dimensions={0}, use_global_device_ids=true | all-gather | bytes 786432 | tf_op jit(solution)/shard_map/all_gather | solution.py:470
  23.2 0.0 all-to-all-done.vel_got
  23.2 0.0 copy-done
  23.2 1.0 %copy-done.2 = f32[16,64,128]{2,1,0:T(8,128)S(1)} copy-done((f32[16,64,128]{2,1,0:T(8,128)S(1)}, f32[16,64,128]{2,1,0:T(8,128)}, u32[]{:S(2)}) %copy-start.2) | copy-done | bytes 524312
  24.3 1.0 %copy-done.4 = f32[16,64,128]{2,1,0:T(8,128)S(1)} copy-done((f32[16,64,128]{2,1,0:T(8,128)S(1)}, f32[16,64,128]{2,1,0:T(8,128)}, u32[]{:S(2)}) %copy-start.4) | copy-done | bytes 524312
  25.3 0.4 shard_map.141
  25.7 0.0 collective-permute-done.far.far_old
  25.7 0.1 shard_map.142.now
  25.8 6.2 %collective-permute-start.1 = (f32[20,64,128]{2,1,0:T(8,128)S(1)}, f32[20,64,128]{2,1,0:T(8,128)S(1)}, u32[]{:S(2)}, u32[]{:S(2)}) collective-permute-start(f32[20,64,128]{2,1,0:T(8,128)S(1)} %shard_map.142.now), channel_id=1, source_target_pairs={{1,2},{2,1},{3,4},{4,3},{5,6},{6,5},{7,8},{8,7},{9,10},{10,9},{11,... | collective-permute-start | bytes 1966088 | tf_op jit(solution)/shard_map/ppermute | solution.py:476
  32.1 1.0 %shard_map.143 = (f32[12,64,128]{2,1,0:T(8,128)S(1)}, f32[8,64,128]{2,1,0:T(8,128)S(1)}, f32[16,64,128]{2,1,0:T(8,128)S(1)}) custom-call(f32[20,64,128]{2,1,0:T(8,128)S(1)} %shard_map.142.now, f32[8,64,128]{2,1,0:T(8,128)S(1)} %get-tuple-element.39.src.src_old.src_first, f32[8,64,128]{2,1,0:T(8,128)S(1)} %get-tuple-element.40.rec.rec_old.rec_first, ...), custom_call_target="tpu_custom_call" | custom-call | flops 5898240 | bytes 2097152 | tf_op jit(solution)/shard_map/pallas_call | solution.py:27
  33.1 2.2 %all-gather.2 = f32[16,64,128]{2,1,0:T(8,128)S(1)} all-gather(f32[8,64,128]{2,1,0:T(8,128)S(1)} %get-tuple-element.48), channel_id=4, replica_groups={{0,1},{2,3},{4,5},{6,7},{8,9},{10,11},{12,13},{14,15},{16,17},{18,19},{..., dimensions={0}, use_global_device_ids=true | all-gather | bytes 786432 | tf_op jit(solution)/shard_map/all_gather | solution.py:482
  35.3 2.4 %all-gather.1 = f32[24,64,128]{2,1,0:T(8,128)S(1)} all-gather(f32[12,64,128]{2,1,0:T(8,128)S(1)} %get-tuple-element.47), channel_id=3, replica_groups={{0,1},{2,3},{4,5},{6,7},{8,9},{10,11},{12,13},{14,15},{16,17},{18,19},{..., dimensions={0}, use_global_device_ids=true | all-gather | bytes 1179648 | tf_op jit(solution)/shard_map/all_gather | solution.py:481
  37.6 0.7 shard_map.144
  38.3 3.0 %collective-permute-done.1.far = f32[20,64,128]{2,1,0:T(8,128)S(1)} collective-permute-done((f32[20,64,128]{2,1,0:T(8,128)S(1)}, f32[20,64,128]{2,1,0:T(8,128)S(1)}, u32[]{:S(2)}, u32[]{:S(2)}) %collective-permute-start.1) | collective-permute-done | bytes 655392 | tf_op jit(solution)/shard_map/ppermute | solution.py:476
  41.3 1.2 %shard_map.145 = (f32[8,64,128]{2,1,0:T(8,128)S(1)}, f32[8,64,128]{2,1,0:T(8,128)S(1)}) custom-call(f32[2,8,128]{2,1,0:T(8,128)S(1)} %get-tuple-element.35.where, f32[4,64,128]{2,1,0:T(8,128)S(1)} %get-tuple-element.36.spots, bf16[4,64,128]{2,1,0:T(8,128)(2,1)S(1)} %bitcast.21, f32[20,64,128]{2,1,0:T(8,128)S(1)} %collective-permute-done.1.far, ...), custom_call_target="tpu_custom_call" | custom-call | flops 5898240 | bytes 2097152 | tf_op jit(solution)/shard_map/pallas_call | solution.py:27
  42.5 6.2 %collective-permute-start.2 = (f32[8,64,128]{2,1,0:T(8,128)S(1)}, f32[8,64,128]{2,1,0:T(8,128)S(1)}, u32[]{:S(2)}, u32[]{:S(2)}) collective-permute-start(f32[8,64,128]{2,1,0:T(8,128)S(1)} %get-tuple-element.52.new_high), channel_id=1, source_target_pairs={{1,2},{2,1},{3,4},{4,3},{5,6},{6,5},{7,8},{8,7},{9,10},{10,9},{11,... | collective-permute-start | bytes 786440 | tf_op jit(solution)/shard_map/ppermute | solution.py:493
  48.8 1.6 %shard_map.146 = (f32[8,64,128]{2,1,0:T(8,128)S(1)}, f32[16,64,128]{2,1,0:T(8,128)S(1)}, f32[8,64,128]{2,1,0:T(8,128)S(1)}) custom-call(f32[2,8,128]{2,1,0:T(8,128)S(1)} %get-tuple-element.35.where, f32[4,64,128]{2,1,0:T(8,128)S(1)} %get-tuple-element.36.spots, bf16[4,64,128]{2,1,0:T(8,128)(2,1)S(1)} %bitcast.22, f32[20,64,128]{2,1,0:T(8,128)S(1)} %shard_map.142.now, ...), custom_call_target="tpu_custom_call" | custom-call | flops 5898240 | bytes 2097152 | tf_op jit(solution)/shard_map/pallas_call | solution.py:27
  50.4 2.2 %all-gather.3 = f32[16,64,128]{2,1,0:T(8,128)S(1)} all-gather(f32[8,64,128]{2,1,0:T(8,128)S(1)} %get-tuple-element.55), channel_id=5, replica_groups={{0,1},{2,3},{4,5},{6,7},{8,9},{10,11},{12,13},{14,15},{16,17},{18,19},{..., dimensions={0}, use_global_device_ids=true | all-gather | bytes 786432 | tf_op jit(solution)/shard_map/all_gather | solution.py:498
  52.5 3.8 %collective-permute-done.2.far = f32[8,64,128]{2,1,0:T(8,128)S(1)} collective-permute-done((f32[8,64,128]{2,1,0:T(8,128)S(1)}, f32[8,64,128]{2,1,0:T(8,128)S(1)}, u32[]{:S(2)}, u32[]{:S(2)}) %collective-permute-start.2) | collective-permute-done | bytes 262176 | tf_op jit(solution)/shard_map/ppermute | solution.py:493
  56.3 0.3 shard_map.147
  56.6 13.5 %all_to_all.10.got = f32[8,16,8,128]{3,2,1,0:T(8,128)S(1)} all-to-all(f32[8,16,8,128]{3,2,1,0:T(8,128)S(1)} %get-tuple-element.58), channel_id=1, replica_groups=mesh['shot'=8,'slab'=64] {'shot'}, dimensions={0} | all-to-all | bytes 1048576 | tf_op jit(solution)/shard_map/all_to_all | solution.py:503
  70.1 1.1 %shard_map.148 = (f32[512,128]{1,0:T(8,128)}, f32[512,128]{1,0:T(8,128)}, f32[512,128]{1,0:T(8,128)}) custom-call(f32[16,8,8,128]{3,2,1,0:T(8,128)S(1)} %get-tuple-element.33.put, f32[8,16,8,128]{3,2,1,0:T(8,128)S(1)} %all_to_all.10.got, f32[16,64,128]{2,1,0:T(8,128)S(1)} %get-tuple-element.59.new), custom_call_target="tpu_custom_call" | custom-call | flops 5898240 | bytes 2097152 | tf_op jit(solution)/shard_map/pallas_call | solution.py:27
  (5 shorter events, 0.0 us)
Async XLA Ops:
  2.6 15.8 %copy-start.5 = (f32[1,64,8,128]{3,2,1,0:T(8,128)S(1)}, f32[1,64,8,128]{3,2,1,0:T(8,128)}, u32[]{:S(2)}) copy-start(f32[1,64,8,128]{3,2,1,0:T(8,128)} %param.12) | copy-start | bytes 786436
  2.6 15.8 %copy-start.6 = (f32[1,64,8,128]{3,2,1,0:T(8,128)S(1)}, f32[1,64,8,128]{3,2,1,0:T(8,128)}, u32[]{:S(2)}) copy-start(f32[1,64,8,128]{3,2,1,0:T(8,128)} %param.15) | copy-start | bytes 786436
  2.6 20.6 %all-to-all-start = ((f32[8,2,64,128]{3,2,1,0:T(8,128)}), f32[8,2,64,128]{3,2,1,0:T(8,128)S(1)}, u32[]{:S(2)}, u32[]{:S(2)}) async-start(f32[8,2,64,128]{3,2,1,0:T(8,128)} %get-tuple-element.38), calls=%async_computation | async-start | bytes 1048576 | tf_op jit(solution)/shard_map/all_to_all | solution.py:464
  7.8 17.9 %collective-permute-start = (f32[8,64,128]{2,1,0:T(8,128)S(1)}, f32[8,64,128]{2,1,0:T(8,128)S(1)}, u32[]{:S(2)}, u32[]{:S(2)}) collective-permute-start(f32[8,64,128]{2,1,0:T(8,128)S(1)} %get-tuple-element.37), channel_id=1, source_target_pairs={{1,2},{2,1},{3,4},{4,3},{5,6},{6,5},{7,8},{8,7},{9,10},{10,9},{11,... | collective-permute-start | bytes 786440 | tf_op jit(solution)/shard_map/ppermute | solution.py:465
  19.3 0.8 %copy-start.1 = (f32[16,64,128]{2,1,0:T(8,128)}, f32[16,64,128]{2,1,0:T(8,128)S(1)}, u32[]{:S(2)}) copy-start(f32[16,64,128]{2,1,0:T(8,128)S(1)} %get-tuple-element.42.sums) | copy-start | bytes 1572868
  20.1 0.8 %copy-start.3 = (f32[16,64,128]{2,1,0:T(8,128)}, f32[16,64,128]{2,1,0:T(8,128)S(1)}, u32[]{:S(2)}) copy-start(f32[16,64,128]{2,1,0:T(8,128)S(1)} %get-tuple-element.43.base) | copy-start | bytes 1572868
  20.9 2.3 %copy-start = (bf16[1,4,64,128]{3,2,1,0:T(8,128)(2,1)S(1)}, bf16[1,4,64,128]{3,2,1,0:T(8,128)(2,1)}, u32[]{:S(2)}) copy-start(bf16[1,4,64,128]{3,2,1,0:T(8,128)(2,1)} %param.23) | copy-start | bytes 196612
  23.2 1.0 %copy-start.2 = (f32[16,64,128]{2,1,0:T(8,128)S(1)}, f32[16,64,128]{2,1,0:T(8,128)}, u32[]{:S(2)}) copy-start(f32[16,64,128]{2,1,0:T(8,128)} %copy-done.1) | copy-start | bytes 1572868
  24.3 1.0 %copy-start.4 = (f32[16,64,128]{2,1,0:T(8,128)S(1)}, f32[16,64,128]{2,1,0:T(8,128)}, u32[]{:S(2)}) copy-start(f32[16,64,128]{2,1,0:T(8,128)} %copy-done.3) | copy-start | bytes 1572868
  25.8 15.5 %collective-permute-start.1 = (f32[20,64,128]{2,1,0:T(8,128)S(1)}, f32[20,64,128]{2,1,0:T(8,128)S(1)}, u32[]{:S(2)}, u32[]{:S(2)}) collective-permute-start(f32[20,64,128]{2,1,0:T(8,128)S(1)} %shard_map.142.now), channel_id=1, source_target_pairs={{1,2},{2,1},{3,4},{4,3},{5,6},{6,5},{7,8},{8,7},{9,10},{10,9},{11,... | collective-permute-start | bytes 1966088 | tf_op jit(solution)/shard_map/ppermute | solution.py:476
  42.5 13.8 %collective-permute-start.2 = (f32[8,64,128]{2,1,0:T(8,128)S(1)}, f32[8,64,128]{2,1,0:T(8,128)S(1)}, u32[]{:S(2)}, u32[]{:S(2)}) collective-permute-start(f32[8,64,128]{2,1,0:T(8,128)S(1)} %get-tuple-element.52.new_high), channel_id=1, source_target_pairs={{1,2},{2,1},{3,4},{4,3},{5,6},{6,5},{7,8},{8,7},{9,10},{10,9},{11,... | collective-permute-start | bytes 786440 | tf_op jit(solution)/shard_map/ppermute | solution.py:493

commit v6 on v5

--- a/solution.py
+++ b/solution.py
@@ -153,17 +153,13 @@
                 to_far[f * REACH + p - (depth - REACH)] = plane
     tile = (8, size_y)
     for c, own in enumerate(places):
-        own = jnp.full(tile, own)
-        for t in range(held):
-            put[c, t] = jnp.where(own == t, 1.0, 0.0)
+        put[c] = jnp.full(tile, own)
     previous = jnp.int32(-1)
     for k in range(KT):
         owner = lax.shift_right_logical(tiles[shot, k], 3)
         place = owner * CAP + (previous == owner).astype(jnp.int32)
         previous = owner
-        place = jnp.full(tile, place)
-        for c in range(pick.shape[1]):
-            pick[k, c] = jnp.where(place == c, 1.0, 0.0)
+        pick[k] = jnp.full(tile, place)
     for copy in copies[4:9]:
         copy.wait()
     first = lax.axis_index("slab") * depth
@@ -201,14 +197,17 @@
 def rate_kernel(pick, vel_got, near, sums, base, where, spots, traces, rate, part):
     mine = partner()
     depth = rate.shape[0]
-    count = pick.shape[1]
-    for p in range(depth):
-        at = pl.ds(z_of(p, depth), BX, stride=depth)
-        tiles = [vel_got[c // CAP, c % CAP, at] for c in range(count)]
-        for k in range(KT):
-            tile = 0.0
-            for c in range(k, count - (KT - 1 - k)):
-                tile += pick[k, c] * tiles[c]
+    count = vel_got.shape[0] * CAP
+    rows = [pl.ds(z_of(p, depth), BX, stride=depth) for p in range(depth)]
+    for k in range(KT):
+        tiles = [vel_got[k // CAP, k % CAP, at] for at in rows]
+        for c in range(k + 1, count - (KT - 1 - k)):
+            here = pick[k] == c
+            tiles = [
+                jnp.where(here, vel_got[c // CAP, c % CAP, at], tile)
+                for at, tile in zip(rows, tiles, strict=True)
+            ]
+        for p, tile in enumerate(tiles):
             rate[p, pl.ds(k * BX, BX)] = tile * tile * (1.0 / SCALE)
     for f in range(2):
 
@@ -363,10 +362,10 @@
         partial[p] = total + now[p] * new_at(1, p)
 
 
-def last_kernel(pick, far, near, base, rate, partial, src_first, rec_first, new, send):
+def last_kernel(pick, far, near, base, rate, partial, src_first, rec_first, new, send, image):
     mine = partner()
     depth = rate.shape[0]
-    count = pick.shape[1]
+    count = send.shape[0] * CAP
     for p in range(depth):
         fields = []
         for f in range(2):
@@ -379,18 +378,22 @@
             value = base[f * depth + p] + rate[p] * beyond_sums(p, plane_at)
             new[f * depth + p] = value
             fields.append(value)
-        image = partial[p] + fields[0] * rec_first[p] + src_first[p] * fields[1]
-        for c in range(count):
-            total = 0.0
-            for k in range(max(0, c - (count - KT)), min(KT - 1, c) + 1):
-                total += pick[k, c] * image[k * BX : (k + 1) * BX]
-            send[c // CAP, (c % CAP) * depth + p] = total
+        image[p] = partial[p] + fields[0] * rec_first[p] + src_first[p] * fields[1]
+    for c in range(count):
+        tiles = [jnp.zeros(send.shape[2:], jnp.float32)] * depth
+        for k in range(max(0, c - (count - KT)), min(KT - 1, c) + 1):
+            here = pick[k] == c
+            at = pl.ds(k * BX, BX)
+            tiles = [jnp.where(here, image[p, at], tile) for p, tile in enumerate(tiles)]
+        for p, tile in enumerate(tiles):
+            send[c // CAP, (c % CAP) * depth + p] = tile
 
 
 def gather_kernel(put, got, new, out, src_out, rec_out, out_rows, src_rows, rec_rows, sems):
     depth = new.shape[0] // 2
     size_x = new.shape[1]
-    count, held = put.shape[:2]
+    count = put.shape[0]
+    held = out_rows.shape[0] // (BX * depth)
     copies = []
     for f, (rows, to) in enumerate(((src_rows, src_out), (rec_rows, rec_out))):
         for p in range(depth):
@@ -398,10 +401,15 @@
         copies.append(pltpu.make_async_copy(rows, to, sems.at[f]))
         copies[-1].start()
     for t in range(held):
-        for p in range(depth):
-            total = 0.0
-            for c in range(count):
-                total += put[c, t] * got[c // CAP, (c % CAP) * depth + p]
+        totals = [jnp.zeros(got.shape[2:], jnp.float32)] * depth
+        for c in range(count):
+            here = put[c] == t
+            first = (c % CAP) * depth
+            totals = [
+                total + jnp.where(here, got[c // CAP, first + p], 0.0)
+                for p, total in enumerate(totals)
+            ]
+        for p, total in enumerate(totals):
             out_rows[pl.ds(t * BX * depth + z_of(p, depth), BX, stride=depth)] = total
     copies.append(pltpu.make_async_copy(out_rows, out, sems.at[2]))
     copies[-1].start()
@@ -443,15 +451,14 @@
     dma = pltpu.SemaphoreType.DMA
     padded = VMEM((REACH, size_x + 2 * PAD, size_y), jnp.float32)
     count = shots * CAP
-    held = velocity.shape[0] // BX
     given = (flat(src_cur), flat(rec_cur), flat(velocity), aperture_tiles)
     given += (src_x, src_z, src_y, rec_depth, wavelet.T)
     scalars = [SMEM(a.shape, a.dtype) for a in given[3:]]
     send, to_far, src, rec, pick, put, where, spots = call(
         start_kernel,
         [
-            ((shots, CAP, BX * depth, size_y), HBM), halo, one, one, (KT, count, 8, size_y),
-            (count, held, 8, size_y), (2, 8, size_y), (STEPS, size_x, size_y),
+            ((shots, CAP, BX * depth, size_y), HBM), halo, one, one, ((KT, 8, size_y), VMEM, jnp.int32),
+            ((count, 8, size_y), VMEM, jnp.int32), (2, 8, size_y), (STEPS, size_x, size_y),
         ],
         [HBM] * 9, *[pltpu.with_memory_space_constraint(a, HBM) for a in given],
         scratch=[
@@ -498,7 +505,7 @@
     near = lax.all_gather(new_low, "slab", axis_index_groups=near_groups)
     new, send = call(
         last_kernel, [two, buffer], [VMEM] * 8,
-        pick, far, near, base, rate, partial, src, rec,
+        pick, far, near, base, rate, partial, src, rec, scratch=[VMEM(one, jnp.float32)],
     )
     image_got = lax.all_to_all(send, "shot", 0, 0)
     image, src, rec = call(

time: 71.8 us -> 68.7 us (0.957)
  starting transfers between devices: 28.3 us -> 32.5 us
  local copies, waits for them, and re-layouts: 3.7 us -> 0.02 us
  waiting for transfers between devices: 6.79 us -> 4.04 us
  blocking collectives: 22.5 us -> 21.7 us
    unnamed x14 -> x6, local copies, waits for them, and re-layouts: 3.7 us -> 0.02 us
    ppermute x1, starting transfers between devices: 6.24 us -> 9.43 us  [local(): wide_far = lax.ppermute(now, 'slab', far_pairs)]
    ppermute x1, waiting for transfers between devices: 3.76 us -> 1.63 us  [local(): far = lax.ppermute(new_high, 'slab', far_pairs)]
    ppermute x1, waiting for transfers between devices: 3.02 us -> 2.01 us  [local(): wide_far = lax.ppermute(now, 'slab', far_pairs)]
    ppermute x1, starting transfers between devices: 6.25 us -> 7.25 us  [local(): far = lax.ppermute(new_high, 'slab', far_pairs)]
    all_to_all x1, blocking collectives: 13.5 us -> 12.7 us  [local(): image_got = lax.all_to_all(send, 'shot', 0, 0)]
  transfers between devices with their start and end apart: 4 -> 4, of which waited for: 2 -> 3; matrix products, arithmetic and copies ran while one was open for 0% -> 0% of each run, Pallas kernels for 6% -> 7%
where the time goes in v6:
time: 68.7 us; the launch traced here: 68.4 us
  starting transfers between devices  32.5 us (47%)
  blocking collectives  21.7 us (32%)
  Pallas kernels  9.4 us (14%)
  waiting for transfers between devices  4.04 us (6%)
  between operations  0.75 us (1%)
    all_to_all x1, blocking collectives, local(): image_got = lax.all_to_all(send, 'shot', 0, 0)  12.7 us
    ppermute x1, starting transfers between devices, local(): far = lax.ppermute(to_far, 'slab', far_pairs)  10.6 us
    ppermute x1, starting transfers between devices, local(): wide_far = lax.ppermute(now, 'slab', far_pairs)  9.43 us
    pallas_call x10, Pallas kernels, call(): pl.pallas_call(body, out_shape=[jax.ShapeDtypeStruct(s, t) for s, _, t in...  9.4 us
    ppermute x1, starting transfers between devices, local(): far = lax.ppermute(new_high, 'slab', far_pairs)  7.25 us
    all_to_all x1, starting transfers between devices, local(): vel_got = lax.all_to_all(send, 'shot', 0, 0)  5.16 us
    all_gather x1, blocking collectives, local(): src_near = lax.all_gather(src_near, 'slab', axis_index_groups=near_groups)  2.36 us
    all_gather x1, blocking collectives, local(): near = lax.all_gather(to_near, 'slab', axis_index_groups=near_groups)  2.31 us
  transfers between devices with their start and end apart: 4, of which 3 were waited for; matrix products, arithmetic and copies ran while one was open for 0% of the time, Pallas kernels for 7%

profile of v6, /device:TPU:16, one launch (start us, length us, event | category | flops | bytes accessed | tf_op | source)
XLA Modules:
  0.0 68.4 jit_solution(810444777130799841)
XLA Ops:
  0.6 2.0 %shard_map.139 = (f32[8,2,64,128]{3,2,1,0:T(8,128)}, f32[8,64,128]{2,1,0:T(8,128)S(1)}, f32[8,64,128]{2,1,0:T(8,128)S(1)}, f32[8,64,128]{2,1,0:T(8,128)S(1)}, s3...) custom-call(f32[512,128]{1,0:T(8,128)} %bitcast.25, ...), custom_call_target="tpu_custom_call" | custom-call | flops 5898240 | bytes 2097152 | tf_op jit(solution)/shard_map/pallas_call | solution.py:27
  2.6 0.0 copy-start.1
  2.6 0.0 copy-start.2
  2.6 5.2 %all-to-all-start = ((f32[8,2,64,128]{3,2,1,0:T(8,128)}), f32[8,2,64,128]{3,2,1,0:T(8,128)S(1)}, u32[]{:S(2)}, u32[]{:S(2)}) async-start(f32[8,2,64,128]{3,2,1,0:T(8,128)} %get-tuple-element.38), calls=%async_computation | async-start | bytes 1048576 | tf_op jit(solution)/shard_map/all_to_all | solution.py:471
  7.8 10.6 %collective-permute-start = (f32[8,64,128]{2,1,0:T(8,128)S(1)}, f32[8,64,128]{2,1,0:T(8,128)S(1)}, u32[]{:S(2)}, u32[]{:S(2)}) collective-permute-start(f32[8,64,128]{2,1,0:T(8,128)S(1)} %get-tuple-element.37), channel_id=1, source_target_pairs={{1,2},{2,1},{3,4},{4,3},{5,6},{6,5},{7,8},{8,7},{9,10},{10,9},{11,... | collective-permute-start | bytes 786440 | tf_op jit(solution)/shard_map/ppermute | solution.py:472
  18.4 0.0 copy-done.1
  18.4 0.0 copy-done.2
  18.4 0.9 %shard_map.140 = (f32[8,64,128]{2,1,0:T(8,128)S(1)}, f32[16,64,128]{2,1,0:T(8,128)S(1)}, f32[16,64,128]{2,1,0:T(8,128)S(1)}, bf16[256,128]{1,0:T(8,128)(2,1)S(1)}) custom-call(f32[8,64,128]{2,1,0:T(8,128)S(1)} %get-tuple-element.39.src.src_old.src_first, f32[8,64,128]{2,1,0:T(8,128)S(1)} %get-tuple-element.40.rec.rec_old.rec_first, f32[512,128]{1,0:T(8,128)S(1)} %bitcast.23, ...), custom_call_target="tpu_custom_call" | custom-call | flops 5898240 | bytes 2097152 | tf_op jit(solution)/shard_map/pallas_call | solution.py:27
  19.3 0.0 copy-start
  19.3 2.3 %all-gather = f32[16,64,128]{2,1,0:T(8,128)S(1)} all-gather(f32[8,64,128]{2,1,0:T(8,128)S(1)} %get-tuple-element.41), channel_id=2, replica_groups={{0,1},{2,3},{4,5},{6,7},{8,9},{10,11},{12,13},{14,15},{16,17},{18,19},{..., dimensions={0}, use_global_device_ids=true | all-gather | bytes 786432 | tf_op jit(solution)/shard_map/all_gather | solution.py:477
  21.7 0.0 all-to-all-done.vel_got
  21.7 0.0 copy-done
  21.7 0.5 shard_map.141
  22.2 0.4 collective-permute-done.far.far_old
  22.6 0.1 shard_map.142.now
  22.6 9.4 %collective-permute-start.1 = (f32[20,64,128]{2,1,0:T(8,128)S(1)}, f32[20,64,128]{2,1,0:T(8,128)S(1)}, u32[]{:S(2)}, u32[]{:S(2)}) collective-permute-start(f32[20,64,128]{2,1,0:T(8,128)S(1)} %shard_map.142.now), channel_id=1, source_target_pairs={{1,2},{2,1},{3,4},{4,3},{5,6},{6,5},{7,8},{8,7},{9,10},{10,9},{11,... | collective-permute-start | bytes 1966088 | tf_op jit(solution)/shard_map/ppermute | solution.py:483
  32.1 1.0 %shard_map.143 = (f32[12,64,128]{2,1,0:T(8,128)S(1)}, f32[8,64,128]{2,1,0:T(8,128)S(1)}, f32[16,64,128]{2,1,0:T(8,128)S(1)}) custom-call(f32[20,64,128]{2,1,0:T(8,128)S(1)} %shard_map.142.now, f32[8,64,128]{2,1,0:T(8,128)S(1)} %get-tuple-element.39.src.src_old.src_first, f32[8,64,128]{2,1,0:T(8,128)S(1)} %get-tuple-element.40.rec.rec_old.rec_first, ...), custom_call_target="tpu_custom_call" | custom-call | flops 5898240 | bytes 2097152 | tf_op jit(solution)/shard_map/pallas_call | solution.py:27
  33.1 2.2 %all-gather.2 = f32[16,64,128]{2,1,0:T(8,128)S(1)} all-gather(f32[8,64,128]{2,1,0:T(8,128)S(1)} %get-tuple-element.48), channel_id=4, replica_groups={{0,1},{2,3},{4,5},{6,7},{8,9},{10,11},{12,13},{14,15},{16,17},{18,19},{..., dimensions={0}, use_global_device_ids=true | all-gather | bytes 786432 | tf_op jit(solution)/shard_map/all_gather | solution.py:489
  35.3 2.4 %all-gather.1 = f32[24,64,128]{2,1,0:T(8,128)S(1)} all-gather(f32[12,64,128]{2,1,0:T(8,128)S(1)} %get-tuple-element.47), channel_id=3, replica_groups={{0,1},{2,3},{4,5},{6,7},{8,9},{10,11},{12,13},{14,15},{16,17},{18,19},{..., dimensions={0}, use_global_device_ids=true | all-gather | bytes 1179648 | tf_op jit(solution)/shard_map/all_gather | solution.py:488
  37.6 0.7 %shard_map.144 = (f32[8,64,128]{2,1,0:T(8,128)S(1)}, f32[8,64,128]{2,1,0:T(8,128)S(1)}, f32[8,64,128]{2,1,0:T(8,128)S(1)}) custom-call(f32[2,8,128]{2,1,0:T(8,128)S(1)} %get-tuple-element.35.where, f32[4,64,128]{2,1,0:T(8,128)S(1)} %get-tuple-element.36.spots, bf16[4,64,128]{2,1,0:T(8,128)(2,1)S(1)} %bitcast.20, f32[2,12,64,128]{3,2,1,0:T(8,128)S(1)} %bitcast.16, ...), custom_call_target="tpu_custom_call" | custom-call | flops 5898240 | bytes 2097152 | tf_op jit(solution)/shard_map/pallas_call | solution.py:27
  38.3 2.0 %collective-permute-done.1.far = f32[20,64,128]{2,1,0:T(8,128)S(1)} collective-permute-done((f32[20,64,128]{2,1,0:T(8,128)S(1)}, f32[20,64,128]{2,1,0:T(8,128)S(1)}, u32[]{:S(2)}, u32[]{:S(2)}) %collective-permute-start.1) | collective-permute-done | bytes 655392 | tf_op jit(solution)/shard_map/ppermute | solution.py:483
  40.3 1.2 %shard_map.145 = (f32[8,64,128]{2,1,0:T(8,128)S(1)}, f32[8,64,128]{2,1,0:T(8,128)S(1)}) custom-call(f32[2,8,128]{2,1,0:T(8,128)S(1)} %get-tuple-element.35.where, f32[4,64,128]{2,1,0:T(8,128)S(1)} %get-tuple-element.36.spots, bf16[4,64,128]{2,1,0:T(8,128)(2,1)S(1)} %bitcast.21, f32[20,64,128]{2,1,0:T(8,128)S(1)} %collective-permute-done.1.far, ...), custom_call_target="tpu_custom_call" | custom-call | flops 5898240 | bytes 2097152 | tf_op jit(solution)/shard_map/pallas_call | solution.py:27
  41.5 7.2 %collective-permute-start.2 = (f32[8,64,128]{2,1,0:T(8,128)S(1)}, f32[8,64,128]{2,1,0:T(8,128)S(1)}, u32[]{:S(2)}, u32[]{:S(2)}) collective-permute-start(f32[8,64,128]{2,1,0:T(8,128)S(1)} %get-tuple-element.52.new_high), channel_id=1, source_target_pairs={{1,2},{2,1},{3,4},{4,3},{5,6},{6,5},{7,8},{8,7},{9,10},{10,9},{11,... | collective-permute-start | bytes 786440 | tf_op jit(solution)/shard_map/ppermute | solution.py:500
  48.8 1.6 %shard_map.146 = (f32[8,64,128]{2,1,0:T(8,128)S(1)}, f32[16,64,128]{2,1,0:T(8,128)S(1)}, f32[8,64,128]{2,1,0:T(8,128)S(1)}) custom-call(f32[2,8,128]{2,1,0:T(8,128)S(1)} %get-tuple-element.35.where, f32[4,64,128]{2,1,0:T(8,128)S(1)} %get-tuple-element.36.spots, bf16[4,64,128]{2,1,0:T(8,128)(2,1)S(1)} %bitcast.22, f32[20,64,128]{2,1,0:T(8,128)S(1)} %shard_map.142.now, ...), custom_call_target="tpu_custom_call" | custom-call | flops 5898240 | bytes 2097152 | tf_op jit(solution)/shard_map/pallas_call | solution.py:27
  50.4 2.2 %all-gather.3 = f32[16,64,128]{2,1,0:T(8,128)S(1)} all-gather(f32[8,64,128]{2,1,0:T(8,128)S(1)} %get-tuple-element.55), channel_id=5, replica_groups={{0,1},{2,3},{4,5},{6,7},{8,9},{10,11},{12,13},{14,15},{16,17},{18,19},{..., dimensions={0}, use_global_device_ids=true | all-gather | bytes 786432 | tf_op jit(solution)/shard_map/all_gather | solution.py:505
  52.6 1.6 %collective-permute-done.2.far = f32[8,64,128]{2,1,0:T(8,128)S(1)} collective-permute-done((f32[8,64,128]{2,1,0:T(8,128)S(1)}, f32[8,64,128]{2,1,0:T(8,128)S(1)}, u32[]{:S(2)}, u32[]{:S(2)}) %collective-permute-start.2) | collective-permute-done | bytes 262176 | tf_op jit(solution)/shard_map/ppermute | solution.py:500
  54.2 0.2 shard_map.147
  54.5 12.7 %all_to_all.10.got = f32[8,16,8,128]{3,2,1,0:T(8,128)S(1)} all-to-all(f32[8,16,8,128]{3,2,1,0:T(8,128)S(1)} %get-tuple-element.58), channel_id=1, replica_groups=mesh['shot'=8,'slab'=64] {'shot'}, dimensions={0} | all-to-all | bytes 1048576 | tf_op jit(solution)/shard_map/all_to_all | solution.py:510
  67.2 1.2 %shard_map.148 = (f32[512,128]{1,0:T(8,128)}, f32[512,128]{1,0:T(8,128)}, f32[512,128]{1,0:T(8,128)}) custom-call(s32[16,8,128]{2,1,0:T(8,128)S(1)} %get-tuple-element.33.put, f32[8,16,8,128]{3,2,1,0:T(8,128)S(1)} %all_to_all.10.got, f32[16,64,128]{2,1,0:T(8,128)S(1)} %get-tuple-element.59.new), custom_call_target="tpu_custom_call" | custom-call | flops 5898240 | bytes 2097152 | tf_op jit(solution)/shard_map/pallas_call | solution.py:27
Async XLA Ops:
  2.6 15.8 %copy-start.1 = (f32[1,64,8,128]{3,2,1,0:T(8,128)S(1)}, f32[1,64,8,128]{3,2,1,0:T(8,128)}, u32[]{:S(2)}) copy-start(f32[1,64,8,128]{3,2,1,0:T(8,128)} %param.12) | copy-start | bytes 786436
  2.6 15.8 %copy-start.2 = (f32[1,64,8,128]{3,2,1,0:T(8,128)S(1)}, f32[1,64,8,128]{3,2,1,0:T(8,128)}, u32[]{:S(2)}) copy-start(f32[1,64,8,128]{3,2,1,0:T(8,128)} %param.15) | copy-start | bytes 786436
  2.6 19.0 %all-to-all-start = ((f32[8,2,64,128]{3,2,1,0:T(8,128)}), f32[8,2,64,128]{3,2,1,0:T(8,128)S(1)}, u32[]{:S(2)}, u32[]{:S(2)}) async-start(f32[8,2,64,128]{3,2,1,0:T(8,128)} %get-tuple-element.38), calls=%async_computation | async-start | bytes 1048576 | tf_op jit(solution)/shard_map/all_to_all | solution.py:471
  7.8 14.8 %collective-permute-start = (f32[8,64,128]{2,1,0:T(8,128)S(1)}, f32[8,64,128]{2,1,0:T(8,128)S(1)}, u32[]{:S(2)}, u32[]{:S(2)}) collective-permute-start(f32[8,64,128]{2,1,0:T(8,128)S(1)} %get-tuple-element.37), channel_id=1, source_target_pairs={{1,2},{2,1},{3,4},{4,3},{5,6},{6,5},{7,8},{8,7},{9,10},{10,9},{11,... | collective-permute-start | bytes 786440 | tf_op jit(solution)/shard_map/ppermute | solution.py:472
  19.3 2.3 %copy-start = (bf16[1,4,64,128]{3,2,1,0:T(8,128)(2,1)S(1)}, bf16[1,4,64,128]{3,2,1,0:T(8,128)(2,1)}, u32[]{:S(2)}) copy-start(bf16[1,4,64,128]{3,2,1,0:T(8,128)(2,1)} %param.23) | copy-start | bytes 196612
  22.6 17.7 %collective-permute-start.1 = (f32[20,64,128]{2,1,0:T(8,128)S(1)}, f32[20,64,128]{2,1,0:T(8,128)S(1)}, u32[]{:S(2)}, u32[]{:S(2)}) collective-permute-start(f32[20,64,128]{2,1,0:T(8,128)S(1)} %shard_map.142.now), channel_id=1, source_target_pairs={{1,2},{2,1},{3,4},{4,3},{5,6},{6,5},{7,8},{8,7},{9,10},{10,9},{11,... | collective-permute-start | bytes 1966088 | tf_op jit(solution)/shard_map/ppermute | solution.py:483
  41.5 12.7 %collective-permute-start.2 = (f32[8,64,128]{2,1,0:T(8,128)S(1)}, f32[8,64,128]{2,1,0:T(8,128)S(1)}, u32[]{:S(2)}, u32[]{:S(2)}) collective-permute-start(f32[8,64,128]{2,1,0:T(8,128)S(1)} %get-tuple-element.52.new_high), channel_id=1, source_target_pairs={{1,2},{2,1},{3,4},{4,3},{5,6},{6,5},{7,8},{8,7},{9,10},{10,9},{11,... | collective-permute-start | bytes 786440 | tf_op jit(solution)/shard_map/ppermute | solution.py:500

commit v7 on v6

--- a/solution.py
+++ b/solution.py
@@ -128,7 +128,6 @@
     rows = BX * depth
     held = vel.shape[0] // rows
     copies[0].wait()
-    copies[1].wait()
     places = []
     for g in range(send.shape[0]):
         before = jnp.int32(0)
@@ -138,12 +137,14 @@
             own = tiles[g, jnp.minimum(before + j, KT - 1)] - shot * BX
             filled = (before + j < KT) & (own >= 0) & (own < held)
             places.append(jnp.where(filled, own, -1))
-            at = pl.multiple_of(jnp.clip(own, 0, held - 1) * rows, rows)
-            copy = pltpu.make_async_copy(
-                vel.at[pl.ds(at, rows)], send.at[g, j], send_sems.at[g * CAP + j]
-            )
-            copy.start()
-            copies.append(copy)
+    copies[1].wait()
+    for c, own in enumerate(places):
+        at = pl.multiple_of(jnp.maximum(own, 0) * rows, rows)
+        copy = pltpu.make_async_copy(
+            vel.at[pl.ds(at, rows)], send.at[c // CAP, c % CAP], send_sems.at[c]
+        )
+        copy.start()
+        copies.append(copy)
     for f, (raw, field) in enumerate(((src_raw, src), (rec_raw, rec))):
         copies[2 + f].wait()
         for p in range(depth):
@@ -295,6 +296,13 @@
     high = depth - REACH
     sources = (where, spots, traces)
     clear_edges(padded)
+    work = [padded.at[pl.ds(i * REACH, REACH)] for i in range(4)]
+
+    def mid_at(f, m):
+        if m < high:
+            return mid_low[f * REACH + m]
+        return mid_high[f * REACH + m - high] if m < depth else mid_far[f * REACH + m - depth]
+
     for f in range(2):
 
         def plane_at(m):
@@ -302,22 +310,19 @@
                 return now[f * depth + m]
             return far[f * depth + 2 * depth - 1 - m]
 
-        def mid_at(m):
-            if m < high:
-                return mid_low[f * REACH + m]
-            return mid_high[f * REACH + m - high] if m < depth else mid_far[f * REACH + m - depth]
-
+        for p in range(high, depth):
+            share = beyond_sums(p, lambda m: plane_at(m) if m >= depth else None)
+            mid_high[f * REACH + p - high] = mid_part[f * REACH + p - high] + rate[p] * share
         planes = jnp.stack([plane_at(depth + i) for i in range(REACH)])
-        totals = full_sums(padded, planes, depth, plane_at, to_y[...])
+        totals = full_sums(work[f], planes, depth, plane_at, to_y[...])
         for i, total in enumerate(totals):
             value = 2.0 * planes[i] - far_old[f * REACH + REACH - 1 - i]
             value += far[2 * depth + REACH - 1 - i] * total
             mid_far[f * REACH + i] = value + sources_at(f, depth + i, 1, sources)
-        for p in range(high, depth):
-            share = beyond_sums(p, lambda m: plane_at(m) if m >= depth else None)
-            mid_high[f * REACH + p - high] = mid_part[f * REACH + p - high] + rate[p] * share
+    for f in range(2):
         planes = mid_high[pl.ds(f * REACH, REACH)]
-        for i, total in enumerate(full_sums(padded, planes, high, mid_at, to_y[...])):
+        totals = full_sums(work[2 + f], planes, high, lambda m: mid_at(f, m), to_y[...])
+        for i, total in enumerate(totals):
             p = high + i
             value = 2.0 * planes[i] - now[f * depth + p] + rate[p] * total
             to_far[f * REACH + i] = value + sources_at(f, p, 2, sources)
@@ -362,13 +367,16 @@
         partial[p] = total + now[p] * new_at(1, p)
 
 
-def last_kernel(pick, far, near, base, rate, partial, src_first, rec_first, new, send, image):
+def last_kernel(
+    pick, far, near, base, rate, partial, src_first, rec_first, src_rows, rec_rows, send, image
+):
     mine = partner()
     depth = rate.shape[0]
     count = send.shape[0] * CAP
     for p in range(depth):
         fields = []
-        for f in range(2):
+        at = pl.ds(z_of(p, depth), rate.shape[1], stride=depth)
+        for f, rows in enumerate((src_rows, rec_rows)):
 
             def plane_at(m):
                 if m < 0:
@@ -376,7 +384,7 @@
                 return far[f * REACH + REACH - 1 - (m - depth)] if m >= depth else None
 
             value = base[f * depth + p] + rate[p] * beyond_sums(p, plane_at)
-            new[f * depth + p] = value
+            rows[at] = value
             fields.append(value)
         image[p] = partial[p] + fields[0] * rec_first[p] + src_first[p] * fields[1]
     for c in range(count):
@@ -389,15 +397,12 @@
             send[c // CAP, (c % CAP) * depth + p] = tile
 
 
-def gather_kernel(put, got, new, out, src_out, rec_out, out_rows, src_rows, rec_rows, sems):
-    depth = new.shape[0] // 2
-    size_x = new.shape[1]
+def gather_kernel(put, got, src_rows, rec_rows, out, src_out, rec_out, out_rows, sems):
+    depth = got.shape[1] // CAP
     count = put.shape[0]
     held = out_rows.shape[0] // (BX * depth)
     copies = []
     for f, (rows, to) in enumerate(((src_rows, src_out), (rec_rows, rec_out))):
-        for p in range(depth):
-            rows[pl.ds(z_of(p, depth), size_x, stride=depth)] = new[f * depth + p]
         copies.append(pltpu.make_async_copy(rows, to, sems.at[f]))
         copies[-1].start()
     for t in range(held):
@@ -411,8 +416,10 @@
             ]
         for p, total in enumerate(totals):
             out_rows[pl.ds(t * BX * depth + z_of(p, depth), BX, stride=depth)] = total
-    copies.append(pltpu.make_async_copy(out_rows, out, sems.at[2]))
-    copies[-1].start()
+        if t % 2:
+            part = pl.ds((t - 1) * BX * depth, 2 * BX * depth)
+            copies.append(pltpu.make_async_copy(out_rows.at[part], out.at[part], sems.at[2 + t // 2]))
+            copies[-1].start()
     for copy in copies:
         copy.wait()
 
@@ -494,7 +501,10 @@
     mid_high, new_high = call(
         wide_far_kernel, [halo] * 2, [VMEM] * 10,
         *sources, wide_far, far, now, mid_low, mid_part, rate, to_y,
-        scratch=[VMEM(halo, jnp.float32), padded],
+        scratch=[
+            VMEM(halo, jnp.float32),
+            VMEM((4 * REACH, size_x + 2 * PAD, size_y), jnp.float32),
+        ],
     )
 
     far = lax.ppermute(new_high, "slab", far_pairs)
@@ -503,16 +513,15 @@
         *sources, now, mid_near, mid_low, mid_high, new_high, rate, to_y, scratch=[padded],
     )
     near = lax.all_gather(new_low, "slab", axis_index_groups=near_groups)
-    new, send = call(
-        last_kernel, [two, buffer], [VMEM] * 8,
+    src_rows, rec_rows, send = call(
+        last_kernel, [raw, raw, buffer], [VMEM] * 8,
         pick, far, near, base, rate, partial, src, rec, scratch=[VMEM(one, jnp.float32)],
     )
     image_got = lax.all_to_all(send, "shot", 0, 0)
     image, src, rec = call(
-        gather_kernel, [(model, HBM), (raw, HBM), (raw, HBM)], [VMEM] * 3, put, image_got, new,
-        scratch=[
-            VMEM(model, jnp.float32), VMEM(raw, jnp.float32), VMEM(raw, jnp.float32), dma((3,)),
-        ],
+        gather_kernel, [(model, HBM), (raw, HBM), (raw, HBM)], [VMEM] * 4,
+        put, image_got, src_rows, rec_rows,
+        scratch=[VMEM(model, jnp.float32), dma((2 + velocity.shape[0] // BX // 2,))],
     )
     return image.reshape(velocity.shape), src.reshape(src_cur.shape), rec.reshape(src_cur.shape)
 

time: 68.7 us -> 68.6 us (level)
  no operation moved by 1% of the time
where the time goes in v7:
time: 68.6 us; the launch traced here: 68.2 us
  starting transfers between devices  32.5 us (47%)
  blocking collectives  21.7 us (32%)
  Pallas kernels  9.21 us (13%)
  waiting for transfers between devices  4.03 us (6%)
  between operations  0.76 us (1%)
    all_to_all x1, blocking collectives, local(): image_got = lax.all_to_all(send, 'shot', 0, 0)  12.7 us
    ppermute x1, starting transfers between devices, local(): far = lax.ppermute(to_far, 'slab', far_pairs)  10.6 us
    ppermute x1, starting transfers between devices, local(): wide_far = lax.ppermute(now, 'slab', far_pairs)  9.43 us
    pallas_call x10, Pallas kernels, call(): pl.pallas_call(body, out_shape=[jax.ShapeDtypeStruct(s, t) for s, _, t in...  9.21 us
    ppermute x1, starting transfers between devices, local(): far = lax.ppermute(new_high, 'slab', far_pairs)  7.26 us
    all_to_all x1, starting transfers between devices, local(): vel_got = lax.all_to_all(send, 'shot', 0, 0)  5.16 us
    all_gather x1, blocking collectives, local(): src_near = lax.all_gather(src_near, 'slab', axis_index_groups=near_groups)  2.36 us
    all_gather x1, blocking collectives, local(): near = lax.all_gather(to_near, 'slab', axis_index_groups=near_groups)  2.31 us
  transfers between devices with their start and end apart: 4, of which 3 were waited for; matrix products, arithmetic and copies ran while one was open for 0% of the time, Pallas kernels for 7%

profile of v7, /device:TPU:16, one launch (start us, length us, event | category | flops | bytes accessed | tf_op | source)
XLA Modules:
  0.0 68.2 jit_solution(14350803964605637903)
XLA Ops:
  0.6 2.0 %shard_map.139 = (f32[8,2,64,128]{3,2,1,0:T(8,128)}, f32[8,64,128]{2,1,0:T(8,128)S(1)}, f32[8,64,128]{2,1,0:T(8,128)S(1)}, f32[8,64,128]{2,1,0:T(8,128)S(1)}, s3...) custom-call(f32[512,128]{1,0:T(8,128)} %bitcast.25, ...), custom_call_target="tpu_custom_call" | custom-call | flops 5898240 | bytes 2097152 | tf_op jit(solution)/shard_map/pallas_call | solution.py:27
  2.6 0.0 copy-start.1
  2.6 0.0 copy-start.2
  2.6 5.2 %all-to-all-start = ((f32[8,2,64,128]{3,2,1,0:T(8,128)}), f32[8,2,64,128]{3,2,1,0:T(8,128)S(1)}, u32[]{:S(2)}, u32[]{:S(2)}) async-start(f32[8,2,64,128]{3,2,1,0:T(8,128)} %get-tuple-element.39), calls=%async_computation | async-start | bytes 1048576 | tf_op jit(solution)/shard_map/all_to_all | solution.py:478
  7.8 10.6 %collective-permute-start = (f32[8,64,128]{2,1,0:T(8,128)S(1)}, f32[8,64,128]{2,1,0:T(8,128)S(1)}, u32[]{:S(2)}, u32[]{:S(2)}) collective-permute-start(f32[8,64,128]{2,1,0:T(8,128)S(1)} %get-tuple-element.38), channel_id=1, source_target_pairs={{1,2},{2,1},{3,4},{4,3},{5,6},{6,5},{7,8},{8,7},{9,10},{10,9},{11,... | collective-permute-start | bytes 786440 | tf_op jit(solution)/shard_map/ppermute | solution.py:479
  18.4 0.0 copy-done.1
  18.4 0.0 copy-done.2
  18.4 0.9 %shard_map.140 = (f32[8,64,128]{2,1,0:T(8,128)S(1)}, f32[16,64,128]{2,1,0:T(8,128)S(1)}, f32[16,64,128]{2,1,0:T(8,128)S(1)}, bf16[256,128]{1,0:T(8,128)(2,1)S(1)}) custom-call(f32[8,64,128]{2,1,0:T(8,128)S(1)} %get-tuple-element.40.src.src_old.src_first, f32[8,64,128]{2,1,0:T(8,128)S(1)} %get-tuple-element.41.rec.rec_old.rec_first, f32[512,128]{1,0:T(8,128)S(1)} %bitcast.23, ...), custom_call_target="tpu_custom_call" | custom-call | flops 5898240 | bytes 2097152 | tf_op jit(solution)/shard_map/pallas_call | solution.py:27
  19.3 0.0 copy-start
  19.3 2.3 %all-gather = f32[16,64,128]{2,1,0:T(8,128)S(1)} all-gather(f32[8,64,128]{2,1,0:T(8,128)S(1)} %get-tuple-element.42), channel_id=2, replica_groups={{0,1},{2,3},{4,5},{6,7},{8,9},{10,11},{12,13},{14,15},{16,17},{18,19},{..., dimensions={0}, use_global_device_ids=true | all-gather | bytes 786432 | tf_op jit(solution)/shard_map/all_gather | solution.py:484
  21.7 0.0 all-to-all-done.vel_got
  21.7 0.0 copy-done
  21.7 0.5 shard_map.141
  22.2 0.4 collective-permute-done.far.far_old
  22.6 0.1 shard_map.142.now
  22.6 9.4 %collective-permute-start.1 = (f32[20,64,128]{2,1,0:T(8,128)S(1)}, f32[20,64,128]{2,1,0:T(8,128)S(1)}, u32[]{:S(2)}, u32[]{:S(2)}) collective-permute-start(f32[20,64,128]{2,1,0:T(8,128)S(1)} %shard_map.142.now), channel_id=1, source_target_pairs={{1,2},{2,1},{3,4},{4,3},{5,6},{6,5},{7,8},{8,7},{9,10},{10,9},{11,... | collective-permute-start | bytes 1966088 | tf_op jit(solution)/shard_map/ppermute | solution.py:490
  32.1 1.0 %shard_map.143 = (f32[12,64,128]{2,1,0:T(8,128)S(1)}, f32[8,64,128]{2,1,0:T(8,128)S(1)}, f32[16,64,128]{2,1,0:T(8,128)S(1)}) custom-call(f32[20,64,128]{2,1,0:T(8,128)S(1)} %shard_map.142.now, f32[8,64,128]{2,1,0:T(8,128)S(1)} %get-tuple-element.40.src.src_old.src_first, f32[8,64,128]{2,1,0:T(8,128)S(1)} %get-tuple-element.41.rec.rec_old.rec_first, ...), custom_call_target="tpu_custom_call" | custom-call | flops 5898240 | bytes 2097152 | tf_op jit(solution)/shard_map/pallas_call | solution.py:27
  33.1 2.2 %all-gather.2 = f32[16,64,128]{2,1,0:T(8,128)S(1)} all-gather(f32[8,64,128]{2,1,0:T(8,128)S(1)} %get-tuple-element.49), channel_id=4, replica_groups={{0,1},{2,3},{4,5},{6,7},{8,9},{10,11},{12,13},{14,15},{16,17},{18,19},{..., dimensions={0}, use_global_device_ids=true | all-gather | bytes 786432 | tf_op jit(solution)/shard_map/all_gather | solution.py:496
  35.3 2.4 %all-gather.1 = f32[24,64,128]{2,1,0:T(8,128)S(1)} all-gather(f32[12,64,128]{2,1,0:T(8,128)S(1)} %get-tuple-element.48), channel_id=3, replica_groups={{0,1},{2,3},{4,5},{6,7},{8,9},{10,11},{12,13},{14,15},{16,17},{18,19},{..., dimensions={0}, use_global_device_ids=true | all-gather | bytes 1179648 | tf_op jit(solution)/shard_map/all_gather | solution.py:495
  37.6 0.7 %shard_map.144 = (f32[8,64,128]{2,1,0:T(8,128)S(1)}, f32[8,64,128]{2,1,0:T(8,128)S(1)}, f32[8,64,128]{2,1,0:T(8,128)S(1)}) custom-call(f32[2,8,128]{2,1,0:T(8,128)S(1)} %get-tuple-element.36.where, f32[4,64,128]{2,1,0:T(8,128)S(1)} %get-tuple-element.37.spots, bf16[4,64,128]{2,1,0:T(8,128)(2,1)S(1)} %bitcast.20, f32[2,12,64,128]{3,2,1,0:T(8,128)S(1)} %bitcast.16, ...), custom_call_target="tpu_custom_call" | custom-call | flops 5898240 | bytes 2097152 | tf_op jit(solution)/shard_map/pallas_call | solution.py:27
  38.3 2.0 %collective-permute-done.1.far = f32[20,64,128]{2,1,0:T(8,128)S(1)} collective-permute-done((f32[20,64,128]{2,1,0:T(8,128)S(1)}, f32[20,64,128]{2,1,0:T(8,128)S(1)}, u32[]{:S(2)}, u32[]{:S(2)}) %collective-permute-start.1) | collective-permute-done | bytes 655392 | tf_op jit(solution)/shard_map/ppermute | solution.py:490
  40.3 1.1 %shard_map.145 = (f32[8,64,128]{2,1,0:T(8,128)S(1)}, f32[8,64,128]{2,1,0:T(8,128)S(1)}) custom-call(f32[2,8,128]{2,1,0:T(8,128)S(1)} %get-tuple-element.36.where, f32[4,64,128]{2,1,0:T(8,128)S(1)} %get-tuple-element.37.spots, bf16[4,64,128]{2,1,0:T(8,128)(2,1)S(1)} %bitcast.21, f32[20,64,128]{2,1,0:T(8,128)S(1)} %collective-permute-done.1.far, ...), custom_call_target="tpu_custom_call" | custom-call | flops 5898240 | bytes 2097152 | tf_op jit(solution)/shard_map/pallas_call | solution.py:27
  41.5 7.3 %collective-permute-start.2 = (f32[8,64,128]{2,1,0:T(8,128)S(1)}, f32[8,64,128]{2,1,0:T(8,128)S(1)}, u32[]{:S(2)}, u32[]{:S(2)}) collective-permute-start(f32[8,64,128]{2,1,0:T(8,128)S(1)} %get-tuple-element.53.new_high), channel_id=1, source_target_pairs={{1,2},{2,1},{3,4},{4,3},{5,6},{6,5},{7,8},{8,7},{9,10},{10,9},{11,... | collective-permute-start | bytes 786440 | tf_op jit(solution)/shard_map/ppermute | solution.py:510
  48.7 1.6 %shard_map.146 = (f32[8,64,128]{2,1,0:T(8,128)S(1)}, f32[16,64,128]{2,1,0:T(8,128)S(1)}, f32[8,64,128]{2,1,0:T(8,128)S(1)}) custom-call(f32[2,8,128]{2,1,0:T(8,128)S(1)} %get-tuple-element.36.where, f32[4,64,128]{2,1,0:T(8,128)S(1)} %get-tuple-element.37.spots, bf16[4,64,128]{2,1,0:T(8,128)(2,1)S(1)} %bitcast.22, f32[20,64,128]{2,1,0:T(8,128)S(1)} %shard_map.142.now, ...), custom_call_target="tpu_custom_call" | custom-call | flops 5898240 | bytes 2097152 | tf_op jit(solution)/shard_map/pallas_call | solution.py:27
  50.4 2.2 %all-gather.3 = f32[16,64,128]{2,1,0:T(8,128)S(1)} all-gather(f32[8,64,128]{2,1,0:T(8,128)S(1)} %get-tuple-element.56), channel_id=5, replica_groups={{0,1},{2,3},{4,5},{6,7},{8,9},{10,11},{12,13},{14,15},{16,17},{18,19},{..., dimensions={0}, use_global_device_ids=true | all-gather | bytes 786432 | tf_op jit(solution)/shard_map/all_gather | solution.py:515
  52.6 1.6 %collective-permute-done.2.far = f32[8,64,128]{2,1,0:T(8,128)S(1)} collective-permute-done((f32[8,64,128]{2,1,0:T(8,128)S(1)}, f32[8,64,128]{2,1,0:T(8,128)S(1)}, u32[]{:S(2)}, u32[]{:S(2)}) %collective-permute-start.2) | collective-permute-done | bytes 262176 | tf_op jit(solution)/shard_map/ppermute | solution.py:510
  54.2 0.3 shard_map.147
  54.5 12.7 %all_to_all.10.got = f32[8,16,8,128]{3,2,1,0:T(8,128)S(1)} all-to-all(f32[8,16,8,128]{3,2,1,0:T(8,128)S(1)} %get-tuple-element.59), channel_id=1, replica_groups=mesh['shot'=8,'slab'=64] {'shot'}, dimensions={0} | all-to-all | bytes 1048576 | tf_op jit(solution)/shard_map/all_to_all | solution.py:520
  67.2 1.0 %shard_map.148 = (f32[512,128]{1,0:T(8,128)}, f32[512,128]{1,0:T(8,128)}, f32[512,128]{1,0:T(8,128)}) custom-call(s32[16,8,128]{2,1,0:T(8,128)S(1)} %get-tuple-element.34.put, f32[8,16,8,128]{3,2,1,0:T(8,128)S(1)} %all_to_all.10.got, f32[512,128]{1,0:T(8,128)S(1)} %get-tuple-element.60.src_rows, f32[512,128]{1,0:T(8,128)S(1)} %get-tuple-element.61.rec_rows), custom_call_target="tpu_custom_call" | custom-call | flops 5898240 | bytes 2097152 | tf_op jit(solution)/shard_map/pallas_call | solution.py:27
Async XLA Ops:
  2.6 15.8 %copy-start.1 = (f32[1,64,8,128]{3,2,1,0:T(8,128)S(1)}, f32[1,64,8,128]{3,2,1,0:T(8,128)}, u32[]{:S(2)}) copy-start(f32[1,64,8,128]{3,2,1,0:T(8,128)} %param.12) | copy-start | bytes 786436
  2.6 15.8 %copy-start.2 = (f32[1,64,8,128]{3,2,1,0:T(8,128)S(1)}, f32[1,64,8,128]{3,2,1,0:T(8,128)}, u32[]{:S(2)}) copy-start(f32[1,64,8,128]{3,2,1,0:T(8,128)} %param.15) | copy-start | bytes 786436
  2.6 19.0 %all-to-all-start = ((f32[8,2,64,128]{3,2,1,0:T(8,128)}), f32[8,2,64,128]{3,2,1,0:T(8,128)S(1)}, u32[]{:S(2)}, u32[]{:S(2)}) async-start(f32[8,2,64,128]{3,2,1,0:T(8,128)} %get-tuple-element.39), calls=%async_computation | async-start | bytes 1048576 | tf_op jit(solution)/shard_map/all_to_all | solution.py:478
  7.8 14.8 %collective-permute-start = (f32[8,64,128]{2,1,0:T(8,128)S(1)}, f32[8,64,128]{2,1,0:T(8,128)S(1)}, u32[]{:S(2)}, u32[]{:S(2)}) collective-permute-start(f32[8,64,128]{2,1,0:T(8,128)S(1)} %get-tuple-element.38), channel_id=1, source_target_pairs={{1,2},{2,1},{3,4},{4,3},{5,6},{6,5},{7,8},{8,7},{9,10},{10,9},{11,... | collective-permute-start | bytes 786440 | tf_op jit(solution)/shard_map/ppermute | solution.py:479
  19.3 2.3 %copy-start = (bf16[1,4,64,128]{3,2,1,0:T(8,128)(2,1)S(1)}, bf16[1,4,64,128]{3,2,1,0:T(8,128)(2,1)}, u32[]{:S(2)}) copy-start(bf16[1,4,64,128]{3,2,1,0:T(8,128)(2,1)} %param.23) | copy-start | bytes 196612
  22.6 17.7 %collective-permute-start.1 = (f32[20,64,128]{2,1,0:T(8,128)S(1)}, f32[20,64,128]{2,1,0:T(8,128)S(1)}, u32[]{:S(2)}, u32[]{:S(2)}) collective-permute-start(f32[20,64,128]{2,1,0:T(8,128)S(1)} %shard_map.142.now), channel_id=1, source_target_pairs={{1,2},{2,1},{3,4},{4,3},{5,6},{6,5},{7,8},{8,7},{9,10},{10,9},{11,... | collective-permute-start | bytes 1966088 | tf_op jit(solution)/shard_map/ppermute | solution.py:490
  41.5 12.7 %collective-permute-start.2 = (f32[8,64,128]{2,1,0:T(8,128)S(1)}, f32[8,64,128]{2,1,0:T(8,128)S(1)}, u32[]{:S(2)}, u32[]{:S(2)}) collective-permute-start(f32[8,64,128]{2,1,0:T(8,128)S(1)} %get-tuple-element.53.new_high), channel_id=1, source_target_pairs={{1,2},{2,1},{3,4},{4,3},{5,6},{6,5},{7,8},{8,7},{9,10},{10,9},{11,... | collective-permute-start | bytes 786440 | tf_op jit(solution)/shard_map/ppermute | solution.py:510

commit v8 on v7

--- a/solution.py
+++ b/solution.py
@@ -138,13 +138,14 @@
             filled = (before + j < KT) & (own >= 0) & (own < held)
             places.append(jnp.where(filled, own, -1))
     copies[1].wait()
+    sends = []
     for c, own in enumerate(places):
         at = pl.multiple_of(jnp.maximum(own, 0) * rows, rows)
         copy = pltpu.make_async_copy(
             vel.at[pl.ds(at, rows)], send.at[c // CAP, c % CAP], send_sems.at[c]
         )
-        copy.start()
-        copies.append(copy)
+        pl.when(own >= 0)(copy.start)
+        sends.append((own, copy))
     for f, (raw, field) in enumerate(((src_raw, src), (rec_raw, rec))):
         copies[2 + f].wait()
         for p in range(depth):
@@ -171,8 +172,8 @@
     here = (row == spot_x[shot]) & (lane == spot_y[shot])
     for step in range(STEPS):
         spots[step] = jnp.where(here, wavelet[step, shot], 0.0)
-    for copy in copies[9:]:
-        copy.wait()
+    for own, copy in sends:
+        pl.when(own >= 0)(copy.wait)
 
 
 def first_interior_kernel(src, rec, src_old, rec_old, to_near, sums, base, to_y, padded):

time: 68.6 us -> 68.5 us (level)
  no operation moved by 1% of the time
where the time goes in v8:
time: 68.5 us; the launch traced here: 68.1 us
  starting transfers between devices  32.5 us (47%)
  blocking collectives  21.7 us (32%)
  Pallas kernels  9.13 us (13%)
  waiting for transfers between devices  4.03 us (6%)
  between operations  0.76 us (1%)
    all_to_all x1, blocking collectives, local(): image_got = lax.all_to_all(send, 'shot', 0, 0)  12.7 us
    ppermute x1, starting transfers between devices, local(): far = lax.ppermute(to_far, 'slab', far_pairs)  10.6 us
    ppermute x1, starting transfers between devices, local(): wide_far = lax.ppermute(now, 'slab', far_pairs)  9.43 us
    pallas_call x10, Pallas kernels, call(): pl.pallas_call(body, out_shape=[jax.ShapeDtypeStruct(s, t) for s, _, t in...  9.13 us
    ppermute x1, starting transfers between devices, local(): far = lax.ppermute(new_high, 'slab', far_pairs)  7.25 us
    all_to_all x1, starting transfers between devices, local(): vel_got = lax.all_to_all(send, 'shot', 0, 0)  5.18 us
    all_gather x1, blocking collectives, local(): src_near = lax.all_gather(src_near, 'slab', axis_index_groups=near_groups)  2.36 us
    all_gather x1, blocking collectives, local(): near = lax.all_gather(to_near, 'slab', axis_index_groups=near_groups)  2.31 us
  transfers between devices with their start and end apart: 4, of which 3 were waited for; matrix products, arithmetic and copies ran while one was open for 0% of the time, Pallas kernels for 7%

profile of v8, /device:TPU:16, one launch (start us, length us, event | category | flops | bytes accessed | tf_op | source)
XLA Modules:
  0.0 68.1 jit_solution(13706748632293452250)
XLA Ops:
  0.6 1.9 %shard_map.139 = (f32[8,2,64,128]{3,2,1,0:T(8,128)}, f32[8,64,128]{2,1,0:T(8,128)S(1)}, f32[8,64,128]{2,1,0:T(8,128)S(1)}, f32[8,64,128]{2,1,0:T(8,128)S(1)}, s3...) custom-call(f32[512,128]{1,0:T(8,128)} %bitcast.25, ...), custom_call_target="tpu_custom_call" | custom-call | flops 5898240 | bytes 2097152 | tf_op jit(solution)/shard_map/pallas_call | solution.py:27
  2.5 0.0 copy-start.1
  2.5 0.0 copy-start.2
  2.6 5.2 %all-to-all-start = ((f32[8,2,64,128]{3,2,1,0:T(8,128)}), f32[8,2,64,128]{3,2,1,0:T(8,128)S(1)}, u32[]{:S(2)}, u32[]{:S(2)}) async-start(f32[8,2,64,128]{3,2,1,0:T(8,128)} %get-tuple-element.39), calls=%async_computation | async-start | bytes 1048576 | tf_op jit(solution)/shard_map/all_to_all | solution.py:479
  7.7 10.6 %collective-permute-start = (f32[8,64,128]{2,1,0:T(8,128)S(1)}, f32[8,64,128]{2,1,0:T(8,128)S(1)}, u32[]{:S(2)}, u32[]{:S(2)}) collective-permute-start(f32[8,64,128]{2,1,0:T(8,128)S(1)} %get-tuple-element.38), channel_id=1, source_target_pairs={{1,2},{2,1},{3,4},{4,3},{5,6},{6,5},{7,8},{8,7},{9,10},{10,9},{11,... | collective-permute-start | bytes 786440 | tf_op jit(solution)/shard_map/ppermute | solution.py:480
  18.4 0.0 copy-done.1
  18.4 0.0 copy-done.2
  18.4 0.9 %shard_map.140 = (f32[8,64,128]{2,1,0:T(8,128)S(1)}, f32[16,64,128]{2,1,0:T(8,128)S(1)}, f32[16,64,128]{2,1,0:T(8,128)S(1)}, bf16[256,128]{1,0:T(8,128)(2,1)S(1)}) custom-call(f32[8,64,128]{2,1,0:T(8,128)S(1)} %get-tuple-element.40.src.src_old.src_first, f32[8,64,128]{2,1,0:T(8,128)S(1)} %get-tuple-element.41.rec.rec_old.rec_first, f32[512,128]{1,0:T(8,128)S(1)} %bitcast.23, ...), custom_call_target="tpu_custom_call" | custom-call | flops 5898240 | bytes 2097152 | tf_op jit(solution)/shard_map/pallas_call | solution.py:27
  19.3 0.0 copy-start
  19.3 2.3 %all-gather = f32[16,64,128]{2,1,0:T(8,128)S(1)} all-gather(f32[8,64,128]{2,1,0:T(8,128)S(1)} %get-tuple-element.42), channel_id=2, replica_groups={{0,1},{2,3},{4,5},{6,7},{8,9},{10,11},{12,13},{14,15},{16,17},{18,19},{..., dimensions={0}, use_global_device_ids=true | all-gather | bytes 786432 | tf_op jit(solution)/shard_map/all_gather | solution.py:485
  21.6 0.0 all-to-all-done.vel_got
  21.6 0.0 copy-done
  21.6 0.5 shard_map.141
  22.1 0.4 collective-permute-done.far.far_old
  22.5 0.1 shard_map.142.now
  22.6 9.4 %collective-permute-start.1 = (f32[20,64,128]{2,1,0:T(8,128)S(1)}, f32[20,64,128]{2,1,0:T(8,128)S(1)}, u32[]{:S(2)}, u32[]{:S(2)}) collective-permute-start(f32[20,64,128]{2,1,0:T(8,128)S(1)} %shard_map.142.now), channel_id=1, source_target_pairs={{1,2},{2,1},{3,4},{4,3},{5,6},{6,5},{7,8},{8,7},{9,10},{10,9},{11,... | collective-permute-start | bytes 1966088 | tf_op jit(solution)/shard_map/ppermute | solution.py:491
  32.0 1.0 %shard_map.143 = (f32[12,64,128]{2,1,0:T(8,128)S(1)}, f32[8,64,128]{2,1,0:T(8,128)S(1)}, f32[16,64,128]{2,1,0:T(8,128)S(1)}) custom-call(f32[20,64,128]{2,1,0:T(8,128)S(1)} %shard_map.142.now, f32[8,64,128]{2,1,0:T(8,128)S(1)} %get-tuple-element.40.src.src_old.src_first, f32[8,64,128]{2,1,0:T(8,128)S(1)} %get-tuple-element.41.rec.rec_old.rec_first, ...), custom_call_target="tpu_custom_call" | custom-call | flops 5898240 | bytes 2097152 | tf_op jit(solution)/shard_map/pallas_call | solution.py:27
  33.0 2.2 %all-gather.2 = f32[16,64,128]{2,1,0:T(8,128)S(1)} all-gather(f32[8,64,128]{2,1,0:T(8,128)S(1)} %get-tuple-element.49), channel_id=4, replica_groups={{0,1},{2,3},{4,5},{6,7},{8,9},{10,11},{12,13},{14,15},{16,17},{18,19},{..., dimensions={0}, use_global_device_ids=true | all-gather | bytes 786432 | tf_op jit(solution)/shard_map/all_gather | solution.py:497
  35.2 2.4 %all-gather.1 = f32[24,64,128]{2,1,0:T(8,128)S(1)} all-gather(f32[12,64,128]{2,1,0:T(8,128)S(1)} %get-tuple-element.48), channel_id=3, replica_groups={{0,1},{2,3},{4,5},{6,7},{8,9},{10,11},{12,13},{14,15},{16,17},{18,19},{..., dimensions={0}, use_global_device_ids=true | all-gather | bytes 1179648 | tf_op jit(solution)/shard_map/all_gather | solution.py:496
  37.6 0.7 %shard_map.144 = (f32[8,64,128]{2,1,0:T(8,128)S(1)}, f32[8,64,128]{2,1,0:T(8,128)S(1)}, f32[8,64,128]{2,1,0:T(8,128)S(1)}) custom-call(f32[2,8,128]{2,1,0:T(8,128)S(1)} %get-tuple-element.36.where, f32[4,64,128]{2,1,0:T(8,128)S(1)} %get-tuple-element.37.spots, bf16[4,64,128]{2,1,0:T(8,128)(2,1)S(1)} %bitcast.20, f32[2,12,64,128]{3,2,1,0:T(8,128)S(1)} %bitcast.16, ...), custom_call_target="tpu_custom_call" | custom-call | flops 5898240 | bytes 2097152 | tf_op jit(solution)/shard_map/pallas_call | solution.py:27
  38.3 2.0 %collective-permute-done.1.far = f32[20,64,128]{2,1,0:T(8,128)S(1)} collective-permute-done((f32[20,64,128]{2,1,0:T(8,128)S(1)}, f32[20,64,128]{2,1,0:T(8,128)S(1)}, u32[]{:S(2)}, u32[]{:S(2)}) %collective-permute-start.1) | collective-permute-done | bytes 655392 | tf_op jit(solution)/shard_map/ppermute | solution.py:491
  40.3 1.1 %shard_map.145 = (f32[8,64,128]{2,1,0:T(8,128)S(1)}, f32[8,64,128]{2,1,0:T(8,128)S(1)}) custom-call(f32[2,8,128]{2,1,0:T(8,128)S(1)} %get-tuple-element.36.where, f32[4,64,128]{2,1,0:T(8,128)S(1)} %get-tuple-element.37.spots, bf16[4,64,128]{2,1,0:T(8,128)(2,1)S(1)} %bitcast.21, f32[20,64,128]{2,1,0:T(8,128)S(1)} %collective-permute-done.1.far, ...), custom_call_target="tpu_custom_call" | custom-call | flops 5898240 | bytes 2097152 | tf_op jit(solution)/shard_map/pallas_call | solution.py:27
  41.4 7.3 %collective-permute-start.2 = (f32[8,64,128]{2,1,0:T(8,128)S(1)}, f32[8,64,128]{2,1,0:T(8,128)S(1)}, u32[]{:S(2)}, u32[]{:S(2)}) collective-permute-start(f32[8,64,128]{2,1,0:T(8,128)S(1)} %get-tuple-element.53.new_high), channel_id=1, source_target_pairs={{1,2},{2,1},{3,4},{4,3},{5,6},{6,5},{7,8},{8,7},{9,10},{10,9},{11,... | collective-permute-start | bytes 786440 | tf_op jit(solution)/shard_map/ppermute | solution.py:511
  48.7 1.6 %shard_map.146 = (f32[8,64,128]{2,1,0:T(8,128)S(1)}, f32[16,64,128]{2,1,0:T(8,128)S(1)}, f32[8,64,128]{2,1,0:T(8,128)S(1)}) custom-call(f32[2,8,128]{2,1,0:T(8,128)S(1)} %get-tuple-element.36.where, f32[4,64,128]{2,1,0:T(8,128)S(1)} %get-tuple-element.37.spots, bf16[4,64,128]{2,1,0:T(8,128)(2,1)S(1)} %bitcast.22, f32[20,64,128]{2,1,0:T(8,128)S(1)} %shard_map.142.now, ...), custom_call_target="tpu_custom_call" | custom-call | flops 5898240 | bytes 2097152 | tf_op jit(solution)/shard_map/pallas_call | solution.py:27
  50.3 2.2 %all-gather.3 = f32[16,64,128]{2,1,0:T(8,128)S(1)} all-gather(f32[8,64,128]{2,1,0:T(8,128)S(1)} %get-tuple-element.56), channel_id=5, replica_groups={{0,1},{2,3},{4,5},{6,7},{8,9},{10,11},{12,13},{14,15},{16,17},{18,19},{..., dimensions={0}, use_global_device_ids=true | all-gather | bytes 786432 | tf_op jit(solution)/shard_map/all_gather | solution.py:516
  52.5 1.6 %collective-permute-done.2.far = f32[8,64,128]{2,1,0:T(8,128)S(1)} collective-permute-done((f32[8,64,128]{2,1,0:T(8,128)S(1)}, f32[8,64,128]{2,1,0:T(8,128)S(1)}, u32[]{:S(2)}, u32[]{:S(2)}) %collective-permute-start.2) | collective-permute-done | bytes 262176 | tf_op jit(solution)/shard_map/ppermute | solution.py:511
  54.1 0.3 shard_map.147
  54.4 12.7 %all_to_all.10.got = f32[8,16,8,128]{3,2,1,0:T(8,128)S(1)} all-to-all(f32[8,16,8,128]{3,2,1,0:T(8,128)S(1)} %get-tuple-element.59), channel_id=1, replica_groups=mesh['shot'=8,'slab'=64] {'shot'}, dimensions={0} | all-to-all | bytes 1048576 | tf_op jit(solution)/shard_map/all_to_all | solution.py:521
  67.1 1.0 %shard_map.148 = (f32[512,128]{1,0:T(8,128)}, f32[512,128]{1,0:T(8,128)}, f32[512,128]{1,0:T(8,128)}) custom-call(s32[16,8,128]{2,1,0:T(8,128)S(1)} %get-tuple-element.34.put, f32[8,16,8,128]{3,2,1,0:T(8,128)S(1)} %all_to_all.10.got, f32[512,128]{1,0:T(8,128)S(1)} %get-tuple-element.60.src_rows, f32[512,128]{1,0:T(8,128)S(1)} %get-tuple-element.61.rec_rows), custom_call_target="tpu_custom_call" | custom-call | flops 5898240 | bytes 2097152 | tf_op jit(solution)/shard_map/pallas_call | solution.py:27
Async XLA Ops:
  2.5 15.8 %copy-start.1 = (f32[1,64,8,128]{3,2,1,0:T(8,128)S(1)}, f32[1,64,8,128]{3,2,1,0:T(8,128)}, u32[]{:S(2)}) copy-start(f32[1,64,8,128]{3,2,1,0:T(8,128)} %param.12) | copy-start | bytes 786436
  2.5 15.8 %copy-start.2 = (f32[1,64,8,128]{3,2,1,0:T(8,128)S(1)}, f32[1,64,8,128]{3,2,1,0:T(8,128)}, u32[]{:S(2)}) copy-start(f32[1,64,8,128]{3,2,1,0:T(8,128)} %param.15) | copy-start | bytes 786436
  2.6 19.0 %all-to-all-start = ((f32[8,2,64,128]{3,2,1,0:T(8,128)}), f32[8,2,64,128]{3,2,1,0:T(8,128)S(1)}, u32[]{:S(2)}, u32[]{:S(2)}) async-start(f32[8,2,64,128]{3,2,1,0:T(8,128)} %get-tuple-element.39), calls=%async_computation | async-start | bytes 1048576 | tf_op jit(solution)/shard_map/all_to_all | solution.py:479
  7.7 14.8 %collective-permute-start = (f32[8,64,128]{2,1,0:T(8,128)S(1)}, f32[8,64,128]{2,1,0:T(8,128)S(1)}, u32[]{:S(2)}, u32[]{:S(2)}) collective-permute-start(f32[8,64,128]{2,1,0:T(8,128)S(1)} %get-tuple-element.38), channel_id=1, source_target_pairs={{1,2},{2,1},{3,4},{4,3},{5,6},{6,5},{7,8},{8,7},{9,10},{10,9},{11,... | collective-permute-start | bytes 786440 | tf_op jit(solution)/shard_map/ppermute | solution.py:480
  19.3 2.3 %copy-start = (bf16[1,4,64,128]{3,2,1,0:T(8,128)(2,1)S(1)}, bf16[1,4,64,128]{3,2,1,0:T(8,128)(2,1)}, u32[]{:S(2)}) copy-start(bf16[1,4,64,128]{3,2,1,0:T(8,128)(2,1)} %param.23) | copy-start | bytes 196612
  22.6 17.7 %collective-permute-start.1 = (f32[20,64,128]{2,1,0:T(8,128)S(1)}, f32[20,64,128]{2,1,0:T(8,128)S(1)}, u32[]{:S(2)}, u32[]{:S(2)}) collective-permute-start(f32[20,64,128]{2,1,0:T(8,128)S(1)} %shard_map.142.now), channel_id=1, source_target_pairs={{1,2},{2,1},{3,4},{4,3},{5,6},{6,5},{7,8},{8,7},{9,10},{10,9},{11,... | collective-permute-start | bytes 1966088 | tf_op jit(solution)/shard_map/ppermute | solution.py:491
  41.4 12.7 %collective-permute-start.2 = (f32[8,64,128]{2,1,0:T(8,128)S(1)}, f32[8,64,128]{2,1,0:T(8,128)S(1)}, u32[]{:S(2)}, u32[]{:S(2)}) collective-permute-start(f32[8,64,128]{2,1,0:T(8,128)S(1)} %get-tuple-element.53.new_high), channel_id=1, source_target_pairs={{1,2},{2,1},{3,4},{4,3},{5,6},{6,5},{7,8},{8,7},{9,10},{10,9},{11,... | collective-permute-start | bytes 786440 | tf_op jit(solution)/shard_map/ppermute | solution.py:511

commit v9 on v7

--- a/solution.py
+++ b/solution.py
@@ -79,10 +79,11 @@
     padded[:, pl.ds(rows - PAD, PAD)] = zeros
 
 
-def full_sums(padded, planes, first, plane_at, to_y):
+def full_sums(padded, planes, first, plane_at, to_y, lines=None):
     count, size_x, _ = planes.shape
     padded[pl.ds(0, count), pl.ds(PAD, size_x)] = planes
-    lines = along_y(planes, to_y)
+    if lines is None:
+        lines = along_y(planes, to_y)
     sums = []
     for p in range(count):
         total = lines[p] + TAPS[0] * planes[p]
@@ -303,6 +304,8 @@
             return mid_low[f * REACH + m]
         return mid_high[f * REACH + m - high] if m < depth else mid_far[f * REACH + m - depth]
 
+    outside = [[far[f * depth + depth - 1 - i] for i in range(REACH)] for f in range(2)]
+    lines = along_y(jnp.stack(outside[0] + outside[1]), to_y[...])
     for f in range(2):
 
         def plane_at(m):
@@ -313,15 +316,18 @@
         for p in range(high, depth):
             share = beyond_sums(p, lambda m: plane_at(m) if m >= depth else None)
             mid_high[f * REACH + p - high] = mid_part[f * REACH + p - high] + rate[p] * share
-        planes = jnp.stack([plane_at(depth + i) for i in range(REACH)])
-        totals = full_sums(work[f], planes, depth, plane_at, to_y[...])
+        planes = jnp.stack(outside[f])
+        own_lines = lines[f * REACH : (f + 1) * REACH]
+        totals = full_sums(work[f], planes, depth, plane_at, None, own_lines)
         for i, total in enumerate(totals):
             value = 2.0 * planes[i] - far_old[f * REACH + REACH - 1 - i]
             value += far[2 * depth + REACH - 1 - i] * total
             mid_far[f * REACH + i] = value + sources_at(f, depth + i, 1, sources)
+    lines = along_y(mid_high[...], to_y[...])
     for f in range(2):
         planes = mid_high[pl.ds(f * REACH, REACH)]
-        totals = full_sums(work[2 + f], planes, high, lambda m: mid_at(f, m), to_y[...])
+        own_lines = lines[f * REACH : (f + 1) * REACH]
+        totals = full_sums(work[2 + f], planes, high, lambda m: mid_at(f, m), None, own_lines)
         for i, total in enumerate(totals):
             p = high + i
             value = 2.0 * planes[i] - now[f * depth + p] + rate[p] * total

time: 68.6 us -> 68.5 us (level)
  no operation moved by 1% of the time
where the time goes in v9:
time: 68.5 us; the launch traced here: 68.1 us
  starting transfers between devices  32.5 us (47%)
  blocking collectives  21.7 us (32%)
  Pallas kernels  9.13 us (13%)
  waiting for transfers between devices  4.03 us (6%)
  between operations  0.76 us (1%)
    all_to_all x1, blocking collectives, local(): image_got = lax.all_to_all(send, 'shot', 0, 0)  12.7 us
    ppermute x1, starting transfers between devices, local(): far = lax.ppermute(to_far, 'slab', far_pairs)  10.6 us
    ppermute x1, starting transfers between devices, local(): wide_far = lax.ppermute(now, 'slab', far_pairs)  9.43 us
    pallas_call x10, Pallas kernels, call(): pl.pallas_call(body, out_shape=[jax.ShapeDtypeStruct(s, t) for s, _, t in...  9.13 us
    ppermute x1, starting transfers between devices, local(): far = lax.ppermute(new_high, 'slab', far_pairs)  7.26 us
    all_to_all x1, starting transfers between devices, local(): vel_got = lax.all_to_all(send, 'shot', 0, 0)  5.16 us
    all_gather x1, blocking collectives, local(): src_near = lax.all_gather(src_near, 'slab', axis_index_groups=near_groups)  2.36 us
    all_gather x1, blocking collectives, local(): near = lax.all_gather(to_near, 'slab', axis_index_groups=near_groups)  2.31 us
  transfers between devices with their start and end apart: 4, of which 3 were waited for; matrix products, arithmetic and copies ran while one was open for 0% of the time, Pallas kernels for 7%

profile of v9, /device:TPU:16, one launch (start us, length us, event | category | flops | bytes accessed | tf_op | source)
XLA Modules:
  0.0 68.1 jit_solution(8264580807188613637)
XLA Ops:
  0.6 2.0 %shard_map.139 = (f32[8,2,64,128]{3,2,1,0:T(8,128)}, f32[8,64,128]{2,1,0:T(8,128)S(1)}, f32[8,64,128]{2,1,0:T(8,128)S(1)}, f32[8,64,128]{2,1,0:T(8,128)S(1)}, s3...) custom-call(f32[512,128]{1,0:T(8,128)} %bitcast.25, ...), custom_call_target="tpu_custom_call" | custom-call | flops 5898240 | bytes 2097152 | tf_op jit(solution)/shard_map/pallas_call | solution.py:27
  2.6 0.0 copy-start.1
  2.6 0.0 copy-start.2
  2.6 5.2 %all-to-all-start = ((f32[8,2,64,128]{3,2,1,0:T(8,128)}), f32[8,2,64,128]{3,2,1,0:T(8,128)S(1)}, u32[]{:S(2)}, u32[]{:S(2)}) async-start(f32[8,2,64,128]{3,2,1,0:T(8,128)} %get-tuple-element.39), calls=%async_computation | async-start | bytes 1048576 | tf_op jit(solution)/shard_map/all_to_all | solution.py:484
  7.8 10.6 %collective-permute-start = (f32[8,64,128]{2,1,0:T(8,128)S(1)}, f32[8,64,128]{2,1,0:T(8,128)S(1)}, u32[]{:S(2)}, u32[]{:S(2)}) collective-permute-start(f32[8,64,128]{2,1,0:T(8,128)S(1)} %get-tuple-element.38), channel_id=1, source_target_pairs={{1,2},{2,1},{3,4},{4,3},{5,6},{6,5},{7,8},{8,7},{9,10},{10,9},{11,... | collective-permute-start | bytes 786440 | tf_op jit(solution)/shard_map/ppermute | solution.py:485
  18.4 0.0 copy-done.1
  18.4 0.0 copy-done.2
  18.4 0.9 %shard_map.140 = (f32[8,64,128]{2,1,0:T(8,128)S(1)}, f32[16,64,128]{2,1,0:T(8,128)S(1)}, f32[16,64,128]{2,1,0:T(8,128)S(1)}, bf16[256,128]{1,0:T(8,128)(2,1)S(1)}) custom-call(f32[8,64,128]{2,1,0:T(8,128)S(1)} %get-tuple-element.40.src.src_old.src_first, f32[8,64,128]{2,1,0:T(8,128)S(1)} %get-tuple-element.41.rec.rec_old.rec_first, f32[512,128]{1,0:T(8,128)S(1)} %bitcast.23, ...), custom_call_target="tpu_custom_call" | custom-call | flops 5898240 | bytes 2097152 | tf_op jit(solution)/shard_map/pallas_call | solution.py:27
  19.3 0.0 copy-start
  19.3 2.3 %all-gather = f32[16,64,128]{2,1,0:T(8,128)S(1)} all-gather(f32[8,64,128]{2,1,0:T(8,128)S(1)} %get-tuple-element.42), channel_id=2, replica_groups={{0,1},{2,3},{4,5},{6,7},{8,9},{10,11},{12,13},{14,15},{16,17},{18,19},{..., dimensions={0}, use_global_device_ids=true | all-gather | bytes 786432 | tf_op jit(solution)/shard_map/all_gather | solution.py:490
  21.7 0.0 all-to-all-done.vel_got
  21.7 0.0 copy-done
  21.7 0.5 shard_map.141
  22.2 0.4 collective-permute-done.far.far_old
  22.6 0.1 shard_map.142.now
  22.6 9.4 %collective-permute-start.1 = (f32[20,64,128]{2,1,0:T(8,128)S(1)}, f32[20,64,128]{2,1,0:T(8,128)S(1)}, u32[]{:S(2)}, u32[]{:S(2)}) collective-permute-start(f32[20,64,128]{2,1,0:T(8,128)S(1)} %shard_map.142.now), channel_id=1, source_target_pairs={{1,2},{2,1},{3,4},{4,3},{5,6},{6,5},{7,8},{8,7},{9,10},{10,9},{11,... | collective-permute-start | bytes 1966088 | tf_op jit(solution)/shard_map/ppermute | solution.py:496
  32.1 1.0 %shard_map.143 = (f32[12,64,128]{2,1,0:T(8,128)S(1)}, f32[8,64,128]{2,1,0:T(8,128)S(1)}, f32[16,64,128]{2,1,0:T(8,128)S(1)}) custom-call(f32[20,64,128]{2,1,0:T(8,128)S(1)} %shard_map.142.now, f32[8,64,128]{2,1,0:T(8,128)S(1)} %get-tuple-element.40.src.src_old.src_first, f32[8,64,128]{2,1,0:T(8,128)S(1)} %get-tuple-element.41.rec.rec_old.rec_first, ...), custom_call_target="tpu_custom_call" | custom-call | flops 5898240 | bytes 2097152 | tf_op jit(solution)/shard_map/pallas_call | solution.py:27
  33.1 2.2 %all-gather.2 = f32[16,64,128]{2,1,0:T(8,128)S(1)} all-gather(f32[8,64,128]{2,1,0:T(8,128)S(1)} %get-tuple-element.49), channel_id=4, replica_groups={{0,1},{2,3},{4,5},{6,7},{8,9},{10,11},{12,13},{14,15},{16,17},{18,19},{..., dimensions={0}, use_global_device_ids=true | all-gather | bytes 786432 | tf_op jit(solution)/shard_map/all_gather | solution.py:502
  35.3 2.4 %all-gather.1 = f32[24,64,128]{2,1,0:T(8,128)S(1)} all-gather(f32[12,64,128]{2,1,0:T(8,128)S(1)} %get-tuple-element.48), channel_id=3, replica_groups={{0,1},{2,3},{4,5},{6,7},{8,9},{10,11},{12,13},{14,15},{16,17},{18,19},{..., dimensions={0}, use_global_device_ids=true | all-gather | bytes 1179648 | tf_op jit(solution)/shard_map/all_gather | solution.py:501
  37.6 0.7 %shard_map.144 = (f32[8,64,128]{2,1,0:T(8,128)S(1)}, f32[8,64,128]{2,1,0:T(8,128)S(1)}, f32[8,64,128]{2,1,0:T(8,128)S(1)}) custom-call(f32[2,8,128]{2,1,0:T(8,128)S(1)} %get-tuple-element.36.where, f32[4,64,128]{2,1,0:T(8,128)S(1)} %get-tuple-element.37.spots, bf16[4,64,128]{2,1,0:T(8,128)(2,1)S(1)} %bitcast.20, f32[2,12,64,128]{3,2,1,0:T(8,128)S(1)} %bitcast.16, ...), custom_call_target="tpu_custom_call" | custom-call | flops 5898240 | bytes 2097152 | tf_op jit(solution)/shard_map/pallas_call | solution.py:27
  38.3 2.0 %collective-permute-done.1.far = f32[20,64,128]{2,1,0:T(8,128)S(1)} collective-permute-done((f32[20,64,128]{2,1,0:T(8,128)S(1)}, f32[20,64,128]{2,1,0:T(8,128)S(1)}, u32[]{:S(2)}, u32[]{:S(2)}) %collective-permute-start.1) | collective-permute-done | bytes 655392 | tf_op jit(solution)/shard_map/ppermute | solution.py:496
  40.3 1.1 %shard_map.145 = (f32[8,64,128]{2,1,0:T(8,128)S(1)}, f32[8,64,128]{2,1,0:T(8,128)S(1)}) custom-call(f32[2,8,128]{2,1,0:T(8,128)S(1)} %get-tuple-element.36.where, f32[4,64,128]{2,1,0:T(8,128)S(1)} %get-tuple-element.37.spots, bf16[4,64,128]{2,1,0:T(8,128)(2,1)S(1)} %bitcast.21, f32[20,64,128]{2,1,0:T(8,128)S(1)} %collective-permute-done.1.far, ...), custom_call_target="tpu_custom_call" | custom-call | flops 5898240 | bytes 2097152 | tf_op jit(solution)/shard_map/pallas_call | solution.py:27
  41.4 7.3 %collective-permute-start.2 = (f32[8,64,128]{2,1,0:T(8,128)S(1)}, f32[8,64,128]{2,1,0:T(8,128)S(1)}, u32[]{:S(2)}, u32[]{:S(2)}) collective-permute-start(f32[8,64,128]{2,1,0:T(8,128)S(1)} %get-tuple-element.53.new_high), channel_id=1, source_target_pairs={{1,2},{2,1},{3,4},{4,3},{5,6},{6,5},{7,8},{8,7},{9,10},{10,9},{11,... | collective-permute-start | bytes 786440 | tf_op jit(solution)/shard_map/ppermute | solution.py:516
  48.7 1.6 %shard_map.146 = (f32[8,64,128]{2,1,0:T(8,128)S(1)}, f32[16,64,128]{2,1,0:T(8,128)S(1)}, f32[8,64,128]{2,1,0:T(8,128)S(1)}) custom-call(f32[2,8,128]{2,1,0:T(8,128)S(1)} %get-tuple-element.36.where, f32[4,64,128]{2,1,0:T(8,128)S(1)} %get-tuple-element.37.spots, bf16[4,64,128]{2,1,0:T(8,128)(2,1)S(1)} %bitcast.22, f32[20,64,128]{2,1,0:T(8,128)S(1)} %shard_map.142.now, ...), custom_call_target="tpu_custom_call" | custom-call | flops 5898240 | bytes 2097152 | tf_op jit(solution)/shard_map/pallas_call | solution.py:27
  50.3 2.2 %all-gather.3 = f32[16,64,128]{2,1,0:T(8,128)S(1)} all-gather(f32[8,64,128]{2,1,0:T(8,128)S(1)} %get-tuple-element.56), channel_id=5, replica_groups={{0,1},{2,3},{4,5},{6,7},{8,9},{10,11},{12,13},{14,15},{16,17},{18,19},{..., dimensions={0}, use_global_device_ids=true | all-gather | bytes 786432 | tf_op jit(solution)/shard_map/all_gather | solution.py:521
  52.5 1.6 %collective-permute-done.2.far = f32[8,64,128]{2,1,0:T(8,128)S(1)} collective-permute-done((f32[8,64,128]{2,1,0:T(8,128)S(1)}, f32[8,64,128]{2,1,0:T(8,128)S(1)}, u32[]{:S(2)}, u32[]{:S(2)}) %collective-permute-start.2) | collective-permute-done | bytes 262176 | tf_op jit(solution)/shard_map/ppermute | solution.py:516
  54.1 0.3 shard_map.147
  54.4 12.7 %all_to_all.10.got = f32[8,16,8,128]{3,2,1,0:T(8,128)S(1)} all-to-all(f32[8,16,8,128]{3,2,1,0:T(8,128)S(1)} %get-tuple-element.59), channel_id=1, replica_groups=mesh['shot'=8,'slab'=64] {'shot'}, dimensions={0} | all-to-all | bytes 1048576 | tf_op jit(solution)/shard_map/all_to_all | solution.py:526
  67.1 1.0 %shard_map.148 = (f32[512,128]{1,0:T(8,128)}, f32[512,128]{1,0:T(8,128)}, f32[512,128]{1,0:T(8,128)}) custom-call(s32[16,8,128]{2,1,0:T(8,128)S(1)} %get-tuple-element.34.put, f32[8,16,8,128]{3,2,1,0:T(8,128)S(1)} %all_to_all.10.got, f32[512,128]{1,0:T(8,128)S(1)} %get-tuple-element.60.src_rows, f32[512,128]{1,0:T(8,128)S(1)} %get-tuple-element.61.rec_rows), custom_call_target="tpu_custom_call" | custom-call | flops 5898240 | bytes 2097152 | tf_op jit(solution)/shard_map/pallas_call | solution.py:27
Async XLA Ops:
  2.6 15.8 %copy-start.1 = (f32[1,64,8,128]{3,2,1,0:T(8,128)S(1)}, f32[1,64,8,128]{3,2,1,0:T(8,128)}, u32[]{:S(2)}) copy-start(f32[1,64,8,128]{3,2,1,0:T(8,128)} %param.12) | copy-start | bytes 786436
  2.6 15.8 %copy-start.2 = (f32[1,64,8,128]{3,2,1,0:T(8,128)S(1)}, f32[1,64,8,128]{3,2,1,0:T(8,128)}, u32[]{:S(2)}) copy-start(f32[1,64,8,128]{3,2,1,0:T(8,128)} %param.15) | copy-start | bytes 786436
  2.6 19.0 %all-to-all-start = ((f32[8,2,64,128]{3,2,1,0:T(8,128)}), f32[8,2,64,128]{3,2,1,0:T(8,128)S(1)}, u32[]{:S(2)}, u32[]{:S(2)}) async-start(f32[8,2,64,128]{3,2,1,0:T(8,128)} %get-tuple-element.39), calls=%async_computation | async-start | bytes 1048576 | tf_op jit(solution)/shard_map/all_to_all | solution.py:484
  7.8 14.8 %collective-permute-start = (f32[8,64,128]{2,1,0:T(8,128)S(1)}, f32[8,64,128]{2,1,0:T(8,128)S(1)}, u32[]{:S(2)}, u32[]{:S(2)}) collective-permute-start(f32[8,64,128]{2,1,0:T(8,128)S(1)} %get-tuple-element.38), channel_id=1, source_target_pairs={{1,2},{2,1},{3,4},{4,3},{5,6},{6,5},{7,8},{8,7},{9,10},{10,9},{11,... | collective-permute-start | bytes 786440 | tf_op jit(solution)/shard_map/ppermute | solution.py:485
  19.3 2.3 %copy-start = (bf16[1,4,64,128]{3,2,1,0:T(8,128)(2,1)S(1)}, bf16[1,4,64,128]{3,2,1,0:T(8,128)(2,1)}, u32[]{:S(2)}) copy-start(bf16[1,4,64,128]{3,2,1,0:T(8,128)(2,1)} %param.23) | copy-start | bytes 196612
  22.6 17.7 %collective-permute-start.1 = (f32[20,64,128]{2,1,0:T(8,128)S(1)}, f32[20,64,128]{2,1,0:T(8,128)S(1)}, u32[]{:S(2)}, u32[]{:S(2)}) collective-permute-start(f32[20,64,128]{2,1,0:T(8,128)S(1)} %shard_map.142.now), channel_id=1, source_target_pairs={{1,2},{2,1},{3,4},{4,3},{5,6},{6,5},{7,8},{8,7},{9,10},{10,9},{11,... | collective-permute-start | bytes 1966088 | tf_op jit(solution)/shard_map/ppermute | solution.py:496
  41.4 12.7 %collective-permute-start.2 = (f32[8,64,128]{2,1,0:T(8,128)S(1)}, f32[8,64,128]{2,1,0:T(8,128)S(1)}, u32[]{:S(2)}, u32[]{:S(2)}) collective-permute-start(f32[8,64,128]{2,1,0:T(8,128)S(1)} %get-tuple-element.53.new_high), channel_id=1, source_target_pairs={{1,2},{2,1},{3,4},{4,3},{5,6},{6,5},{7,8},{8,7},{9,10},{10,9},{11,... | collective-permute-start | bytes 786440 | tf_op jit(solution)/shard_map/ppermute | solution.py:516
